TPU v7x, 512 devices: a whole 4x4x16 slice. The times are simulated.
512 devices in a mesh: row: 16 (over z), col: 32 (over y, x, core).
Axes of the slice: x: 4, y: 4, z: 16, core: 2. Of those that a mesh axis runs over, the one named last changes fastest.
Arguments:
- rhs_above: float32 [32768, 4096], P('col', 'row'), may hold values from -6 to 6
- rhs_a: float32 [1024, 4096], P('col', 'row'), may hold values from -6 to 6
- rhs_b: float32 [1024, 4096], P('col', 'row'), may hold values from -6 to 6
- rows_a_above: float32 [1024, 32768], P('row', 'col'), may hold values from -0.1875 to 0.1875
- rows_b_above: float32 [1024, 32768], P('row', 'col'), may hold values from -0.1875 to 0.1875
- rows_b_a: float32 [1024, 1024], P('row', 'col'), may hold values from -0.1875 to 0.1875
- inverse_a: float32 [1024, 1024], P(None, 'col'), as said below
- inverse_b: float32 [1024, 1024], P(None, 'col'), as said below
Outputs:
- x_b: float32 [1024, 4096], P('col', 'row')
- x_a: float32 [1024, 4096], P('col', 'row')
- updated_above: float32 [32768, 4096], P('col', 'row')
Inputs may be any that keep to these rules, and one draw needn't show every extreme that they name: inverse_a is lower triangular: zero above the diagonal, positive on it. inverse_b is lower triangular: zero above the diagonal, positive on it.
All inputs are finite; a program needn't handle non-finite values.
Results may differ from a plain program's by a relative error of at most 0.00012.
Values sent between devices are 32-bit elements; how exact they have to be, the bound alone decides.
No kernel may reach another device: no remote copies, remote signals or barrier semaphores. Data moves between devices by JAX's collectives and lax.ppermute only.
A program may use at most 64 MiB of HBM per device.

v0:
```python
import jax
import jax.numpy as jnp
from jax import lax
from jax.sharding import PartitionSpec as P

HIGHEST = lax.Precision.HIGHEST


def contract(left, right):
    return lax.dot_general(
        left, right, (((0,), (0,)), ((), ())), precision=HIGHEST, preferred_element_type=jnp.float32
    )


def contract_stack(left, right):
    return lax.dot_general(
        left,
        right,
        (((0, 1), (0, 1)), ((), ())),
        precision=HIGHEST,
        preferred_element_type=jnp.float32,
    )


def solve_panel(rhs_local, inverse_local):
    solved = contract(inverse_local, lax.all_gather(rhs_local, "col", axis=0, tiled=True))
    spread = lax.all_gather(solved, "col", axis=0, tiled=True)
    return (solved, spread)


def second_panel(rhs_a, rows_b_a, inverse_a, x_b_full):
    coupled = rhs_a - contract(lax.all_gather(rows_b_a, "row", axis=0, tiled=True), x_b_full)
    return solve_panel(coupled, inverse_a)


def update_above(factor_rows, solutions):
    return contract_stack(lax.all_gather(factor_rows, "row", axis=1, tiled=True), solutions)


def shards(rhs_above, rhs_a, rhs_b, rows_a_above, rows_b_above, rows_b_a, inverse_a, inverse_b):
    x_b_local, x_b_full = solve_panel(rhs_b, inverse_b)
    earlier = update_above(rows_b_above[None], x_b_full[None])
    x_a_local, x_a_full = second_panel(rhs_a, rows_b_a, inverse_a, x_b_full)
    removed = earlier + update_above(rows_a_above[None], x_a_full[None])
    return (x_b_local, x_a_local, rhs_above - removed)


def solution(mesh):
    in_specs = (
        P("col", "row"),
        P("col", "row"),
        P("col", "row"),
        P("row", "col"),
        P("row", "col"),
        P("row", "col"),
        P(None, "col"),
        P(None, "col"),
    )
    out_specs = (P("col", "row"), P("col", "row"), P("col", "row"))
    return jax.shard_map(shards, mesh=mesh, in_specs=in_specs, out_specs=out_specs, check_vma=False)
```

profile of v0, /device:TPU:1, one launch (start us, length us, event | category | flops | bytes accessed | tf_op | source)
XLA Modules:
  0.0 427.3 jit_solution(4352857697862620846)
XLA Ops:
  7.2 0.0 copy-start
  7.2 0.0 copy-start.3
  7.2 0.0 copy-start.2
  7.2 0.0 all-gather.10.cloned.1.call-start
  7.2 0.7 all-gather.10.cloned.1.call-update
  7.9 0.0 all-gather.12.cloned.1.call-start
  8.0 67.0 %all-gather.10.cloned.1.call-done = f32[1024,256]{1,0:T(8,128)} async-done(((f32[32,256]{1,0:T(8,128)}), f32[1024,256]{1,0:T(8,128)}) %all-gather.10.cloned.1.call-update) | async-done | bytes 1048592 | tf_op jit(solution)/shard_map/all_gather | solution.py:26
  75.0 0.0 copy-done
  75.0 2.4 fusion.3
  77.5 0.0 all-gather.12.cloned.1.call-update
  77.5 0.0 all-gather.14.cloned.1.call-start
  77.5 25.2 %all-gather.2 = f32[16,64,32]{1,2,0:T(8,128)S(1)} all-gather(f32[1,64,32]{1,2,0:T(8,128)} %bitcast.23), channel_id=1, replica_groups=mesh['row'=16,'col'=32] {'row'}, dimensions={0}, use_global_device_ids=true | all-gather | bytes 139264 | tf_op jit(solution)/shard_map/all_gather | solution.py:32
  102.8 0.2 copy.16
  102.9 0.1 reshape.23
  103.0 33.2 %all-gather.12.cloned.1.call-done = f32[1024,256]{1,0:T(8,128)} async-done(((f32[32,256]{1,0:T(8,128)}), f32[1024,256]{1,0:T(8,128)}) %all-gather.12.cloned.1.call-update) | async-done | bytes 1048592 | tf_op jit(solution)/shard_map/all_gather | solution.py:27
  136.3 0.0 copy-start.1
  136.3 2.6 fusion.2
  138.9 0.0 all-gather.14.cloned.1.call-update
  138.9 0.0 all-gather.18.cloned.1.call-start
  138.9 0.5 all-gather.18.cloned.1.call-update
  139.5 0.0 all-gather.20.cloned.1.call-start
  139.5 0.5 all-gather.20.cloned.1.call-update
  140.1 0.0 all-gather.16.cloned.1.call-start
  140.1 57.4 %all-gather.14.cloned.1.call-done = f32[1024,256]{1,0:T(8,128)} async-done(((f32[32,256]{1,0:T(8,128)}), f32[1024,256]{1,0:T(8,128)}) %all-gather.14.cloned.1.call-update) | async-done | bytes 1048592 | tf_op jit(solution)/shard_map/all_gather | solution.py:26
  197.6 0.0 copy-done.3
  197.6 2.5 convolution_bitcast_fusion
  200.1 0.0 all-gather.16.cloned.1.call-update
  200.1 0.0 copy-done.2
  200.1 0.3 copy.17
  200.4 68.0 %all-gather.18.cloned.1.call-done = f32[1024,1024]{1,0:T(8,128)} async-done(((f32[64,1024]{1,0:T(8,128)}), f32[1024,1024]{1,0:T(8,128)}) %all-gather.18.cloned.1.call-update) | async-done | bytes 4194320 | tf_op jit(solution)/shard_map/all_gather | solution.py:37
  268.4 0.0 copy-done.1
  268.5 5.6 %fusion.4 = f32[256,1024]{1,0:T(8,128)S(1)} fusion(f32[1024,256]{1,0:T(8,128)S(1)} %copy-done.1, f32[1024,1024]{1,0:T(8,128)} %all-gather.18.cloned.1.call-done), kind=kOutput, calls=%fused_computation.7 | convolution fusion | flops 3221225472 | bytes 6291456 | tf_op jit(solution)/shard_map/dot_general | solution.py:16
  274.0 71.7 %all-gather.20.cloned.1.call-done = f32[1024,1024]{1,0:T(8,128)} async-done(((f32[64,1024]{1,0:T(8,128)}), f32[1024,1024]{1,0:T(8,128)}) %all-gather.20.cloned.1.call-update) | async-done | bytes 4194320 | tf_op jit(solution)/shard_map/all_gather | solution.py:37
  345.7 67.5 %all-gather.16.cloned.1.call-done = f32[1024,256]{1,0:T(8,128)} async-done(((f32[32,256]{1,0:T(8,128)}), f32[1024,256]{1,0:T(8,128)}) %all-gather.16.cloned.1.call-update) | async-done | bytes 1048592 | tf_op jit(solution)/shard_map/all_gather | solution.py:27
  413.2 5.9 %fusion.1 = f32[1024,256]{0,1:T(8,128)S(1)} fusion(f32[1024,256]{0,1:T(8,128)S(1)} %copy.17, f32[256,1024]{1,0:T(8,128)S(1)} %fusion.4, f32[1024,256]{1,0:T(8,128)} %all-gather.16.cloned.1.call-done, f32[1024,1024]{1,0:T(8,128)} %all-gather.20.cloned.1.call-done), kind=kOutput, calls=%fused_computation.2 | convolution fusion | flops 3221749760 | bytes 8388608 | tf_op jit(solution)/shard_map/dot_general | solution.py:16
  419.1 1.3 copy.18
Async XLA Ops:
  7.2 67.9 %copy-start = (f32[1024,32]{0,1:T(8,128)S(1)}, f32[1024,32]{0,1:T(8,128)}, u32[]{:S(2)}) copy-start(f32[1024,32]{0,1:T(8,128)} %param.15) | copy-start | bytes 393220
  7.2 190.4 %copy-start.3 = (f32[1024,32]{0,1:T(8,128)S(1)}, f32[1024,32]{0,1:T(8,128)}, u32[]{:S(2)}) copy-start(f32[1024,32]{0,1:T(8,128)} %param.14) | copy-start | bytes 393220
  7.2 192.9 %copy-start.2 = (f32[1024,256]{1,0:T(8,128)S(1)}, f32[1024,256]{1,0:T(8,128)}, u32[]{:S(2)}) copy-start(f32[1024,256]{1,0:T(8,128)} %param.8) | copy-start | bytes 3145732
  7.2 67.8 %all-gather.10.cloned.1.call-start = ((), (), s32[]{:S(2)}) async-start(), calls=%async_computation | async-start | bytes 1081344 | tf_op jit(solution)/shard_map/all_gather | solution.py:26
  7.9 128.4 %all-gather.12.cloned.1.call-start = ((), (), s32[]{:S(2)}) async-start(), calls=%async_computation.1 | async-start | bytes 1081344 | tf_op jit(solution)/shard_map/all_gather | solution.py:27
  77.5 120.1 %all-gather.14.cloned.1.call-start = ((), (), s32[]{:S(2)}) async-start(), calls=%async_computation.2 | async-start | bytes 1081344 | tf_op jit(solution)/shard_map/all_gather | solution.py:26
  136.3 132.2 %copy-start.1 = (f32[1024,256]{1,0:T(8,128)S(1)}, f32[1024,256]{1,0:T(8,128)}, u32[]{:S(2)}) copy-start(f32[1024,256]{1,0:T(8,128)} %all-gather.12.cloned.1.call-done) | copy-start | bytes 3145732
  138.9 129.6 %all-gather.18.cloned.1.call-start = ((), (), s32[]{:S(2)}) async-start(), calls=%async_computation.4 | async-start | bytes 4456448 | tf_op jit(solution)/shard_map/all_gather | solution.py:37
  139.5 206.2 %all-gather.20.cloned.1.call-start = ((), (), s32[]{:S(2)}) async-start(), calls=%async_computation.5 | async-start | bytes 4456448 | tf_op jit(solution)/shard_map/all_gather | solution.py:37
  140.1 273.1 %all-gather.16.cloned.1.call-start = ((), (), s32[]{:S(2)}) async-start(), calls=%async_computation.3 | async-start | bytes 1081344 | tf_op jit(solution)/shard_map/all_gather | solution.py:27
Sparse Core Ops, SparseCore 0:
  11.2 63.8 all-gather.9
  78.7 57.5 all-gather.11
  140.0 57.5 all-gather.13
  199.5 68.9 all-gather.17
  270.4 75.2 all-gather.19
  349.3 63.8 all-gather.15
where the time goes:
time: 427 us
  waiting for transfers between devices  367 us (86%)
  blocking collectives  25.2 us (6%)
  matrix products  19 us (4%)
  between operations  14.2 us (3%)
    all_gather x2, waiting for transfers between devices, update_above(): lax.all_gather(factor_rows, 'row', axis=1, tiled=True)  140 us
    all_gather x2, waiting for transfers between devices, solve_panel(): lax.all_gather(rhs_local, 'col', axis=0, tiled=True)  124 us
    all_gather x2, waiting for transfers between devices, solve_panel(): spread = lax.all_gather(solved, 'col', axis=0, tiled=True)  101 us
    all_gather x1, blocking collectives, second_panel(): lax.all_gather(rows_b_a, 'row', axis=0, tiled=True)  25.2 us
    dot_general x2, matrix products, contract_stack(): lax.dot_general(left, right, (((0, 1), (0, 1)), ((), ())), precision=HIGH...  11.5 us
  transfers between devices with their start and end apart: 6, of which 6 were waited for; matrix products, arithmetic and copies ran while one was open for 2% of the time, Pallas kernels for 0%

commit v1 on v0

v1 whole, which is shorter than its diff:
```python
import functools

import jax
import jax.numpy as jnp
from jax import lax
from jax.experimental import pallas as pl
from jax.experimental.pallas import tpu as pltpu
from jax.sharding import PartitionSpec as P

F32 = jnp.float32
BF16 = jnp.bfloat16
VMEM_LIMIT = 40 * 1024 * 1024


def split(a):
    high = a.astype(BF16)
    return high, (a - high.astype(F32)).astype(BF16)


def dot(a, b):
    return lax.dot_general(a, b, (((1,), (0,)), ((), ())), preferred_element_type=F32)


def product(a, b):
    a_high, a_low = split(a)
    b_high, b_low = split(b)
    return dot(a_high, b_high) + (dot(a_high, b_low) + dot(a_low, b_high))


def solve_kernel(planes, plane_ref, factor_ref, rhs_b_ref, rhs_a_ref, x_b_ref, x_a_ref, coupled_ref):
    step = pl.program_id(0)
    tile = 256
    panel, width = x_b_ref.shape
    steps = panel // tile
    shard = panel // factor_ref.shape[0]
    lines = panel // planes
    per_tile = tile // shard

    def factor():
        return factor_ref[...].reshape(panel, tile)

    def triangular(j, rhs, out_ref):
        height = tile * (j + 1)
        part = product(factor()[:height], rhs)
        if j:
            out_ref[: height - tile] += part[: height - tile]
        out_ref[height - tile : height] = part[height - tile :]

    for j in range(steps):

        @pl.when(step == j)
        def _(j=j):
            rhs = rhs_b_ref[j * per_tile : (j + 1) * per_tile].reshape(tile, width)
            triangular(j, rhs, x_b_ref)

        @pl.when(step == steps + j)
        def _(j=j):
            blocks = []
            for i in range(tile // lines):
                block = lax.rem(plane_ref[0] + j * (tile // lines) + i, panel // lines)
                blocks.append(x_b_ref[pl.ds(pl.multiple_of(block * lines, lines), lines), :])
            part = product(factor(), jnp.concatenate(blocks, axis=0))
            before = coupled_ref[...] if j else rhs_a_ref[...].reshape(panel, width)
            coupled_ref[...] = before - part

        @pl.when(step == 2 * steps + j)
        def _(j=j):
            triangular(j, coupled_ref[j * tile : (j + 1) * tile], x_a_ref)


def solve(plane, gathered, panel, width, planes):
    shards, rows, tile = gathered.shape
    shard = panel // shards
    block = (shards, shard, tile)
    steps = 3 * panel // tile
    return pl.pallas_call(
        functools.partial(solve_kernel, planes),
        grid=(steps,),
        out_shape=[jax.ShapeDtypeStruct((panel, width), F32)] * 2,
        in_specs=[
            pl.BlockSpec(memory_space=pltpu.SMEM),
            pl.BlockSpec(block, lambda s: (0, s, 0)),
            pl.BlockSpec(block, lambda s: (0, steps, 0)),
            pl.BlockSpec(block, lambda s: (0, steps + 1, 0)),
        ],
        out_specs=[pl.BlockSpec((panel, width), lambda s: (0, 0))] * 2,
        scratch_shapes=[pltpu.VMEM((panel, width), F32)],
        compiler_params=pltpu.CompilerParams(vmem_limit_bytes=VMEM_LIMIT),
        name="solve",
    )(plane, gathered, gathered, gathered)


def update_kernel(offsets, plane_ref, x_b_ref, x_a_ref, rhs_ref, *refs):
    chunks, out_ref, high, low = refs[:-3], refs[-3], refs[-2], refs[-1]
    lines = chunks[0].shape[0] // 2
    planes = x_b_ref.shape[0] // lines
    depth = 2 * lines

    @pl.when(pl.program_id(0) == 0)
    def _():
        for n, offset in enumerate(offsets):
            block = lax.rem(plane_ref[0] + offset, planes)
            rows = pl.ds(pl.multiple_of(block * lines, lines), lines)
            x = jnp.concatenate([x_b_ref[rows, :], x_a_ref[rows, :]], axis=0).T
            x_high, x_low = split(x)
            high[:, n * depth : (n + 1) * depth] = x_high
            low[:, n * depth : (n + 1) * depth] = x_low

    total = None
    n = 0
    while n < len(chunks):
        pair = chunks[n : n + 2]
        rows = jnp.concatenate([c[...] for c in pair], axis=0) if len(pair) > 1 else pair[0][...]
        l_high, l_low = split(rows)
        lanes = slice(n * depth, (n + len(pair)) * depth)
        part = dot(high[:, lanes], l_high) + (dot(low[:, lanes], l_high) + dot(high[:, lanes], l_low))
        total = part if total is None else total + part
        n += len(pair)
    out_ref[...] = rhs_ref[...] - total.T


def update(plane, x_b, x_a, rhs, chunks, offsets, name):
    height, width = rhs.shape
    panel = x_b.shape[0]
    tile = 256
    depth = sum(c.shape[0] for c in chunks)
    whole = pl.BlockSpec((panel, width), lambda n: (0, 0))
    rows = pl.BlockSpec((tile, width), lambda n: (n, 0))

    return pl.pallas_call(
        functools.partial(update_kernel, offsets),
        grid=(height // tile,),
        out_shape=jax.ShapeDtypeStruct((height, width), F32),
        in_specs=[pl.BlockSpec(memory_space=pltpu.SMEM), whole, whole, rows]
        + [pl.BlockSpec((c.shape[0], tile), lambda n: (0, n)) for c in chunks],
        out_specs=rows,
        scratch_shapes=[pltpu.VMEM((width, depth), BF16)] * 2,
        compiler_params=pltpu.CompilerParams(vmem_limit_bytes=VMEM_LIMIT),
        name=name,
    )(plane, x_b, x_a, rhs, *chunks)


def shift(planes, by):
    return [(i, (i + by) % planes) for i in range(planes)]


def collect(block, planes):
    distance = 1
    while distance < planes:
        block = jnp.concatenate([block, lax.ppermute(block, "row", shift(planes, -distance))], axis=0)
        distance *= 2
    return block


def tiles(a, width):
    return [a[:, i : i + width] for i in range(0, a.shape[1], width)]


def make(planes):
    def shards(rhs_above, rhs_a, rhs_b, rows_a_above, rows_b_above, rows_b_a, inverse_a, inverse_b):
        width = rhs_b.shape[1]
        panel = inverse_b.shape[0]
        plane = lax.axis_index("row").astype(jnp.int32).reshape(1)
        column = lax.axis_index("col")

        across = collect(rows_b_a.T[None], planes)
        across = across.transpose(1, 0, 2).reshape(rhs_b.shape[0], panel)
        packed = jnp.concatenate(
            tiles(inverse_b.T, width) + tiles(across, width) + tiles(inverse_a.T, width) + [rhs_b, rhs_a], axis=0
        )
        gathered = lax.all_gather(packed, "col", axis=0)

        own = jnp.concatenate([rows_b_above, rows_a_above], axis=0)
        up = down = own
        chunks, offsets = [own], [0]
        half = planes // 2
        for step in range(1, half):
            up = lax.ppermute(up, "row", shift(planes, 1))
            down = lax.ppermute(down, "row", shift(planes, -1))
            chunks += [up, down]
            offsets += [planes - step, step]
        middle = own.shape[0] // 2
        last = [
            lax.ppermute(up[:middle], "row", shift(planes, 1)),
            lax.ppermute(down[middle:], "row", shift(planes, -1)),
        ]

        x_b, x_a = solve(plane, gathered, panel, width, planes)
        partial = update(plane, x_b, x_a, rhs_above, chunks, offsets, "update_near")
        far = jnp.concatenate(last, axis=0)
        updated = update(plane, x_b, x_a, partial, [far], [half], "update_far")
        first = column * rhs_b.shape[0]
        return (
            lax.dynamic_slice_in_dim(x_b, first, rhs_b.shape[0], 0),
            lax.dynamic_slice_in_dim(x_a, first, rhs_b.shape[0], 0),
            updated,
        )

    return shards


def solution(mesh):
    in_specs = (
        P("col", "row"),
        P("col", "row"),
        P("col", "row"),
        P("row", "col"),
        P("row", "col"),
        P("row", "col"),
        P(None, "col"),
        P(None, "col"),
    )
    out_specs = (P("col", "row"), P("col", "row"), P("col", "row"))
    return jax.shard_map(
        make(mesh.shape["row"]), mesh=mesh, in_specs=in_specs, out_specs=out_specs, check_vma=False
    )
```

time: 427 us -> 224 us (0.52)
  the two profiles are of different devices: /device:TPU:1 before, /device:TPU:10 now
where the time goes in v1:
time: 224 us; the launch traced here: 222 us
  starting transfers between devices  85.7 us (38%)
  waiting for transfers between devices  77.9 us (35%)
  Pallas kernels  21.5 us (10%)
  local copies, waits for them, and re-layouts  19.3 us (9%)
  between operations  14.6 us (7%)
  other arithmetic  3.17 us (1%)
    ppermute x7, waiting for transfers between devices, shards(): down = lax.ppermute(down, 'row', shift(planes, -1))  45 us
    ppermute x7, starting transfers between devices, shards(): down = lax.ppermute(down, 'row', shift(planes, -1))  37.3 us
    ppermute x4, starting transfers between devices, collect(): lax.ppermute(block, 'row', shift(planes, -distance))  25.8 us
    ppermute x4, waiting for transfers between devices, collect(): lax.ppermute(block, 'row', shift(planes, -distance))  21.9 us
    unnamed x62, local copies, waits for them, and re-layouts  16.6 us
    ppermute x7, starting transfers between devices, shards(): up = lax.ppermute(up, 'row', shift(planes, 1))  15.1 us
    pallas_call x1, Pallas kernels, solve(): pl.pallas_call(functools.partial(solve_kernel, planes), grid=(steps,), ou...  13.1 us
    pallas_call x2, Pallas kernels, update(): pl.pallas_call(functools.partial(update_kernel, offsets), grid=(height //...  8.41 us
  transfers between devices with their start and end apart: 21, of which 13 were waited for; matrix products, arithmetic and copies ran while one was open for 3% of the time, Pallas kernels for 0%

profile of v1, /device:TPU:10, one launch (start us, length us, event | category | flops | bytes accessed | tf_op | source)
XLA Modules:
  0.0 222.1 jit_solution(16163509851586960875)
XLA Ops:
  7.2 11.4 %collective-permute-start = (f32[1,32,64]{2,1,0:T(8,128)}, f32[1,32,64]{2,1,0:T(8,128)S(1)}, u32[]{:S(2)}, u32[]{:S(2)}) collective-permute-start(f32[1,32,64]{2,1,0:T(8,128)} %bitcast.13), channel_id=1, source_target_pairs={{0,480},{32,0},{64,32},{96,64},{128,96},{160,128},{192,160},{224,1... | collective-permute-start | bytes 24584 | tf_op jit(solution)/shard_map/ppermute | solution.py:150
  18.6 0.8 constant_dynamic-update-slice_fusion.18
  19.4 0.8 constant_dynamic-update-slice_fusion.17
  20.1 0.8 constant_dynamic-update-slice_fusion.16
  20.9 0.8 constant_dynamic-update-slice_fusion.15
  21.7 0.7 constant_dynamic-update-slice_fusion.4
  22.4 0.7 pad_maximum_fusion.3
  23.1 3.3 %collective-permute-start.1 = (f32[2,32,64]{2,1,0:T(8,128)S(1)}, f32[2,32,64]{2,1,0:T(8,128)S(1)}, u32[]{:S(2)}, u32[]{:S(2)}) collective-permute-start(f32[2,32,64]{2,1,0:T(8,128)S(1)} %pad_maximum_fusion.3), channel_id=1, source_target_pairs={{0,448},{32,480},{64,0},{96,32},{128,64},{160,96},{192,128},{224,1... | collective-permute-start | bytes 49160 | tf_op jit(solution)/shard_map/ppermute | solution.py:150
  26.5 3.4 %collective-permute-done.1 = f32[2,32,64]{2,1,0:T(8,128)S(1)} collective-permute-done((f32[2,32,64]{2,1,0:T(8,128)S(1)}, f32[2,32,64]{2,1,0:T(8,128)S(1)}, u32[]{:S(2)}, u32[]{:S(2)}) %collective-permute-start.1) | collective-permute-done | bytes 16416 | tf_op jit(solution)/shard_map/ppermute | solution.py:150
  29.9 0.7 pad_maximum_fusion.2
  30.6 5.4 %collective-permute-start.2 = (f32[4,32,64]{2,1,0:T(8,128)S(1)}, f32[4,32,64]{2,1,0:T(8,128)S(1)}, u32[]{:S(2)}, u32[]{:S(2)}) collective-permute-start(f32[4,32,64]{2,1,0:T(8,128)S(1)} %pad_maximum_fusion.2), channel_id=1, source_target_pairs={{0,384},{32,416},{64,448},{96,480},{128,0},{160,32},{192,64},{224,... | collective-permute-start | bytes 98312 | tf_op jit(solution)/shard_map/ppermute | solution.py:150
  36.1 5.8 %collective-permute-done.2 = f32[4,32,64]{2,1,0:T(8,128)S(1)} collective-permute-done((f32[4,32,64]{2,1,0:T(8,128)S(1)}, f32[4,32,64]{2,1,0:T(8,128)S(1)}, u32[]{:S(2)}, u32[]{:S(2)}) %collective-permute-start.2) | collective-permute-done | bytes 32800 | tf_op jit(solution)/shard_map/ppermute | solution.py:150
  41.9 0.7 pad_maximum_fusion.1
  42.6 5.6 %collective-permute-start.3 = (f32[8,32,64]{2,1,0:T(8,128)S(1)}, f32[8,32,64]{2,1,0:T(8,128)S(1)}, u32[]{:S(2)}, u32[]{:S(2)}) collective-permute-start(f32[8,32,64]{2,1,0:T(8,128)S(1)} %pad_maximum_fusion.1), channel_id=1, source_target_pairs={{0,256},{32,288},{64,320},{96,352},{128,384},{160,416},{192,448},{... | collective-permute-start | bytes 196616 | tf_op jit(solution)/shard_map/ppermute | solution.py:150
  48.2 12.6 %collective-permute-done.3 = f32[8,32,64]{2,1,0:T(8,128)S(1)} collective-permute-done((f32[8,32,64]{2,1,0:T(8,128)S(1)}, f32[8,32,64]{2,1,0:T(8,128)S(1)}, u32[]{:S(2)}, u32[]{:S(2)}) %collective-permute-start.3) | collective-permute-done | bytes 65568 | tf_op jit(solution)/shard_map/ppermute | solution.py:150
  61.2 0.8 constant_dynamic-update-slice_fusion.10
  62.0 0.8 constant_dynamic-update-slice_fusion.9
  62.7 0.8 constant_dynamic-update-slice_fusion.8
  63.5 0.8 constant_dynamic-update-slice_fusion.7
  64.3 0.8 constant_dynamic-update-slice_fusion.6
  65.0 0.8 constant_dynamic-update-slice_fusion.5
  65.8 0.8 copy-done.21
  66.6 1.0 constant_dynamic-update-slice_fusion.20
  67.6 1.0 constant_dynamic-update-slice_fusion.19.refs_0_
  68.5 7.0 %collective-permute-start.5 = (f32[128,1024]{1,0:T(8,128)S(1)}, f32[128,1024]{1,0:T(8,128)S(1)}, u32[]{:S(2)}, u32[]{:S(2)}) collective-permute-start(f32[128,1024]{1,0:T(8,128)S(1)} %constant_dynamic-update-slice_fusion.19.refs_0_), channel_id=1, source_target_pairs={{0,480},{32,0},{64,32},{96,64},{128,96},{160,128},{192,160},{224,1... | collective-permute-start | bytes 1572872 | tf_op jit(solution)/shard_map/ppermute | solution.py:179
  75.5 1.9 collective-permute-start.4
  77.4 7.1 %collective-permute-done.5.refs_2_ = f32[128,1024]{1,0:T(8,128)S(1)} collective-permute-done((f32[128,1024]{1,0:T(8,128)S(1)}, f32[128,1024]{1,0:T(8,128)S(1)}, u32[]{:S(2)}, u32[]{:S(2)}) %collective-permute-start.5) | collective-permute-done | bytes 524320 | tf_op jit(solution)/shard_map/ppermute | solution.py:179
  84.5 3.2 %collective-permute-start.7 = (f32[128,1024]{1,0:T(8,128)S(1)}, f32[128,1024]{1,0:T(8,128)S(1)}, u32[]{:S(2)}, u32[]{:S(2)}) collective-permute-start(f32[128,1024]{1,0:T(8,128)S(1)} %collective-permute-done.5.refs_2_), channel_id=1, source_target_pairs={{0,480},{32,0},{64,32},{96,64},{128,96},{160,128},{192,160},{224,1... | collective-permute-start | bytes 1572872 | tf_op jit(solution)/shard_map/ppermute | solution.py:179
  87.8 2.6 %collective-permute-start.6 = (f32[128,1024]{1,0:T(8,128)S(1)}, f32[128,1024]{1,0:T(8,128)S(1)}, u32[]{:S(2)}, u32[]{:S(2)}) collective-permute-start(f32[128,1024]{1,0:T(8,128)S(1)} %collective-permute-done.4.refs_1_), channel_id=1, source_target_pairs={{0,32},{32,64},{64,96},{96,128},{128,160},{160,192},{192,224},{224... | collective-permute-start | bytes 1572872 | tf_op jit(solution)/shard_map/ppermute | solution.py:178
  90.4 8.9 %collective-permute-done.7.refs_4_ = f32[128,1024]{1,0:T(8,128)S(1)} collective-permute-done((f32[128,1024]{1,0:T(8,128)S(1)}, f32[128,1024]{1,0:T(8,128)S(1)}, u32[]{:S(2)}, u32[]{:S(2)}) %collective-permute-start.7) | collective-permute-done | bytes 524320 | tf_op jit(solution)/shard_map/ppermute | solution.py:179
  99.3 3.4 %collective-permute-start.9 = (f32[128,1024]{1,0:T(8,128)S(1)}, f32[128,1024]{1,0:T(8,128)S(1)}, u32[]{:S(2)}, u32[]{:S(2)}) collective-permute-start(f32[128,1024]{1,0:T(8,128)S(1)} %collective-permute-done.7.refs_4_), channel_id=1, source_target_pairs={{0,480},{32,0},{64,32},{96,64},{128,96},{160,128},{192,160},{224,1... | collective-permute-start | bytes 1572872 | tf_op jit(solution)/shard_map/ppermute | solution.py:179
  102.7 0.8 copy-done.1
  103.5 2.4 %collective-permute-start.8 = (f32[128,1024]{1,0:T(8,128)S(1)}, f32[128,1024]{1,0:T(8,128)S(1)}, u32[]{:S(2)}, u32[]{:S(2)}) collective-permute-start(f32[128,1024]{1,0:T(8,128)S(1)} %collective-permute-done.6.refs_3_), channel_id=1, source_target_pairs={{0,32},{32,64},{64,96},{96,128},{128,160},{160,192},{192,224},{224... | collective-permute-start | bytes 1572872 | tf_op jit(solution)/shard_map/ppermute | solution.py:178
  105.9 0.8 copy-done.3
  106.7 6.3 %collective-permute-done.9.refs_6_ = f32[128,1024]{1,0:T(8,128)S(1)} collective-permute-done((f32[128,1024]{1,0:T(8,128)S(1)}, f32[128,1024]{1,0:T(8,128)S(1)}, u32[]{:S(2)}, u32[]{:S(2)}) %collective-permute-start.9) | collective-permute-done | bytes 524320 | tf_op jit(solution)/shard_map/ppermute | solution.py:179
  113.1 3.6 %collective-permute-start.11 = (f32[128,1024]{1,0:T(8,128)S(1)}, f32[128,1024]{1,0:T(8,128)S(1)}, u32[]{:S(2)}, u32[]{:S(2)}) collective-permute-start(f32[128,1024]{1,0:T(8,128)S(1)} %collective-permute-done.9.refs_6_), channel_id=1, source_target_pairs={{0,480},{32,0},{64,32},{96,64},{128,96},{160,128},{192,160},{224,1... | collective-permute-start | bytes 1572872 | tf_op jit(solution)/shard_map/ppermute | solution.py:179
  116.6 0.8 copy-done.5
  117.4 2.3 %collective-permute-start.10 = (f32[128,1024]{1,0:T(8,128)S(1)}, f32[128,1024]{1,0:T(8,128)S(1)}, u32[]{:S(2)}, u32[]{:S(2)}) collective-permute-start(f32[128,1024]{1,0:T(8,128)S(1)} %collective-permute-done.8.refs_5_), channel_id=1, source_target_pairs={{0,32},{32,64},{64,96},{96,128},{128,160},{160,192},{192,224},{224... | collective-permute-start | bytes 1572872 | tf_op jit(solution)/shard_map/ppermute | solution.py:178
  119.7 0.8 copy-done.7
  120.5 5.4 %collective-permute-done.11.refs_8_ = f32[128,1024]{1,0:T(8,128)S(1)} collective-permute-done((f32[128,1024]{1,0:T(8,128)S(1)}, f32[128,1024]{1,0:T(8,128)S(1)}, u32[]{:S(2)}, u32[]{:S(2)}) %collective-permute-start.11) | collective-permute-done | bytes 524320 | tf_op jit(solution)/shard_map/ppermute | solution.py:179
  125.9 3.7 %collective-permute-start.13 = (f32[128,1024]{1,0:T(8,128)S(1)}, f32[128,1024]{1,0:T(8,128)S(1)}, u32[]{:S(2)}, u32[]{:S(2)}) collective-permute-start(f32[128,1024]{1,0:T(8,128)S(1)} %collective-permute-done.11.refs_8_), channel_id=1, source_target_pairs={{0,480},{32,0},{64,32},{96,64},{128,96},{160,128},{192,160},{224,1... | collective-permute-start | bytes 1572872 | tf_op jit(solution)/shard_map/ppermute | solution.py:179
  129.7 0.8 copy-done.9
  130.5 2.1 collective-permute-start.12
  132.6 0.8 copy-done.11
  133.4 4.6 %collective-permute-done.13.refs_10_ = f32[128,1024]{1,0:T(8,128)S(1)} collective-permute-done((f32[128,1024]{1,0:T(8,128)S(1)}, f32[128,1024]{1,0:T(8,128)S(1)}, u32[]{:S(2)}, u32[]{:S(2)}) %collective-permute-start.13) | collective-permute-done | bytes 524320 | tf_op jit(solution)/shard_map/ppermute | solution.py:179
  138.0 10.8 %collective-permute-start.15 = (f32[128,1024]{1,0:T(8,128)S(1)}, f32[128,1024]{1,0:T(8,128)S(1)}, u32[]{:S(2)}, u32[]{:S(2)}) collective-permute-start(f32[128,1024]{1,0:T(8,128)S(1)} %collective-permute-done.13.refs_10_), channel_id=1, source_target_pairs={{0,480},{32,0},{64,32},{96,64},{128,96},{160,128},{192,160},{224,1... | collective-permute-start | bytes 1572872 | tf_op jit(solution)/shard_map/ppermute | solution.py:179
  148.8 0.8 copy-done.13
  149.5 1.9 collective-permute-start.14
  151.5 0.8 copy-done.15
  152.3 8.4 %collective-permute-done.15.refs_12_ = f32[128,1024]{1,0:T(8,128)S(1)} collective-permute-done((f32[128,1024]{1,0:T(8,128)S(1)}, f32[128,1024]{1,0:T(8,128)S(1)}, u32[]{:S(2)}, u32[]{:S(2)}) %collective-permute-start.15) | collective-permute-done | bytes 524320 | tf_op jit(solution)/shard_map/ppermute | solution.py:179
  160.7 5.6 %collective-permute-start.17 = (f32[128,1024]{1,0:T(8,128)S(1)}, f32[128,1024]{1,0:T(8,128)S(1)}, u32[]{:S(2)}, u32[]{:S(2)}) collective-permute-start(f32[128,1024]{1,0:T(8,128)S(1)} %collective-permute-done.15.refs_12_), channel_id=1, source_target_pairs={{0,480},{32,0},{64,32},{96,64},{128,96},{160,128},{192,160},{224,1... | collective-permute-start | bytes 1572872 | tf_op jit(solution)/shard_map/ppermute | solution.py:179
  166.3 0.8 copy-done.17
  167.1 1.3 collective-permute-done.14.refs_11_
  168.4 1.9 collective-permute-start.16
  170.3 4.3 %collective-permute-done.17.refs_14_ = f32[128,1024]{1,0:T(8,128)S(1)} collective-permute-done((f32[128,1024]{1,0:T(8,128)S(1)}, f32[128,1024]{1,0:T(8,128)S(1)}, u32[]{:S(2)}, u32[]{:S(2)}) %collective-permute-start.17) | collective-permute-done | bytes 524320 | tf_op jit(solution)/shard_map/ppermute | solution.py:179
  174.7 5.6 %collective-permute-start.19 = (f32[64,1024]{1,0:T(8,128)S(1)}, f32[64,1024]{1,0:T(8,128)S(1)}, u32[]{:S(2)}, u32[]{:S(2)}) collective-permute-start(f32[64,1024]{1,0:T(8,128)S(1)} %slice.69), channel_id=1, source_target_pairs={{0,480},{32,0},{64,32},{96,64},{128,96},{160,128},{192,160},{224,1... | collective-permute-start | bytes 786440 | tf_op jit(solution)/shard_map/ppermute | solution.py:185
  180.3 2.0 collective-permute-done.16.refs_13_
  182.3 1.9 collective-permute-start.18
  184.3 7.6 %collective-permute-done.18 = f32[64,1024]{1,0:T(8,128)} collective-permute-done((f32[64,1024]{1,0:T(8,128)S(1)}, f32[64,1024]{1,0:T(8,128)}, u32[]{:S(2)}, u32[]{:S(2)}) %collective-permute-start.18) | collective-permute-done | bytes 262176 | tf_op jit(solution)/shard_map/ppermute | solution.py:184
  191.9 1.0 pad_maximum_fusion.refs_0_
  193.0 13.1 %solve.1 = (f32[1024,256]{1,0:T(8,128)S(1)}, f32[1024,256]{1,0:T(8,128)S(1)}) custom-call(s32[1]{0:T(128)} %bitcast.plane_ref, f32[32,448,256]{2,1,0:T(8,128)} %bitcast.9, f32[32,448,256]{2,1,0:T(8,128)} %bitcast.10, f32[32,448,256]{2,1,0:T(8,128)} %bitcast.11), custom_call_target="tpu_custom_call" | custom-call | tf_op jit(solution)/shard_map/solve/pallas_call | solution.py:76
  206.1 0.6 constant_dynamic-slice_fusion
  206.8 5.8 %update_near.1.rhs_ref = f32[1024,256]{1,0:T(8,128)S(1)} custom-call(s32[1]{0:T(128)} %bitcast.plane_ref, f32[1024,256]{1,0:T(8,128)S(1)} %get-tuple-element.5.x_b_ref, f32[1024,256]{1,0:T(8,128)S(1)} %get-tuple-element.6.x_a_ref, f32[1024,256]{1,0:T(8,128)S(1)} %copy-done, f32[128,1024]{1,0:T(8,128)S(1)} %constant_dynamic-update-slice_fusion.19.refs_0_, ...), custom_call_target="tpu_custom_call" | custom-call | tf_op jit(solution)/shard_map/update_near/pallas_call | solution.py:130
  212.7 2.6 %update_far.1 = f32[1024,256]{1,0:T(8,128)} custom-call(s32[1]{0:T(128)} %bitcast.plane_ref, f32[1024,256]{1,0:T(8,128)S(1)} %get-tuple-element.5.x_b_ref, f32[1024,256]{1,0:T(8,128)S(1)} %get-tuple-element.6.x_a_ref, f32[1024,256]{1,0:T(8,128)S(1)} %update_near.1.rhs_ref, f32[128,1024]{1,0:T(8,128)S(1)} %pad_maximum_fusion.refs_0_), custom_call_target="tpu_custom_call" | custom-call | tf_op jit(solution)/shard_map/update_far/pallas_call | solution.py:130
  (56 shorter events, 0.5 us)
Async XLA Ops:
  7.2 185.8 %all-gather.3.cloned.1.call-start = ((), (), s32[]{:S(2)}) async-start(), calls=%async_computation | async-start | bytes 15138816 | tf_op jit(solution)/shard_map/all_gather | solution.py:171
  7.2 15.2 %collective-permute-start = (f32[1,32,64]{2,1,0:T(8,128)}, f32[1,32,64]{2,1,0:T(8,128)S(1)}, u32[]{:S(2)}, u32[]{:S(2)}) collective-permute-start(f32[1,32,64]{2,1,0:T(8,128)} %bitcast.13), channel_id=1, source_target_pairs={{0,480},{32,0},{64,32},{96,64},{128,96},{160,128},{192,160},{224,1... | collective-permute-start | bytes 24584 | tf_op jit(solution)/shard_map/ppermute | solution.py:150
  23.1 6.8 %collective-permute-start.1 = (f32[2,32,64]{2,1,0:T(8,128)S(1)}, f32[2,32,64]{2,1,0:T(8,128)S(1)}, u32[]{:S(2)}, u32[]{:S(2)}) collective-permute-start(f32[2,32,64]{2,1,0:T(8,128)S(1)} %pad_maximum_fusion.3), channel_id=1, source_target_pairs={{0,448},{32,480},{64,0},{96,32},{128,64},{160,96},{192,128},{224,1... | collective-permute-start | bytes 49160 | tf_op jit(solution)/shard_map/ppermute | solution.py:150
  30.6 11.3 %collective-permute-start.2 = (f32[4,32,64]{2,1,0:T(8,128)S(1)}, f32[4,32,64]{2,1,0:T(8,128)S(1)}, u32[]{:S(2)}, u32[]{:S(2)}) collective-permute-start(f32[4,32,64]{2,1,0:T(8,128)S(1)} %pad_maximum_fusion.2), channel_id=1, source_target_pairs={{0,384},{32,416},{64,448},{96,480},{128,0},{160,32},{192,64},{224,... | collective-permute-start | bytes 98312 | tf_op jit(solution)/shard_map/ppermute | solution.py:150
  42.6 18.2 %collective-permute-start.3 = (f32[8,32,64]{2,1,0:T(8,128)S(1)}, f32[8,32,64]{2,1,0:T(8,128)S(1)}, u32[]{:S(2)}, u32[]{:S(2)}) collective-permute-start(f32[8,32,64]{2,1,0:T(8,128)S(1)} %pad_maximum_fusion.1), channel_id=1, source_target_pairs={{0,256},{32,288},{64,320},{96,352},{128,384},{160,416},{192,448},{... | collective-permute-start | bytes 196616 | tf_op jit(solution)/shard_map/ppermute | solution.py:150
  65.8 0.8 copy-start.21
  68.5 16.0 %collective-permute-start.5 = (f32[128,1024]{1,0:T(8,128)S(1)}, f32[128,1024]{1,0:T(8,128)S(1)}, u32[]{:S(2)}, u32[]{:S(2)}) collective-permute-start(f32[128,1024]{1,0:T(8,128)S(1)} %constant_dynamic-update-slice_fusion.19.refs_0_), channel_id=1, source_target_pairs={{0,480},{32,0},{64,32},{96,64},{128,96},{160,128},{192,160},{224,1... | collective-permute-start | bytes 1572872 | tf_op jit(solution)/shard_map/ppermute | solution.py:179
  75.5 12.3 %collective-permute-start.4 = (f32[128,1024]{1,0:T(8,128)S(1)}, f32[128,1024]{1,0:T(8,128)S(1)}, u32[]{:S(2)}, u32[]{:S(2)}) collective-permute-start(f32[128,1024]{1,0:T(8,128)S(1)} %constant_dynamic-update-slice_fusion.19.refs_0_), channel_id=1, source_target_pairs={{0,32},{32,64},{64,96},{96,128},{128,160},{160,192},{192,224},{224... | collective-permute-start | bytes 1572872 | tf_op jit(solution)/shard_map/ppermute | solution.py:178
  84.5 14.7 %collective-permute-start.7 = (f32[128,1024]{1,0:T(8,128)S(1)}, f32[128,1024]{1,0:T(8,128)S(1)}, u32[]{:S(2)}, u32[]{:S(2)}) collective-permute-start(f32[128,1024]{1,0:T(8,128)S(1)} %collective-permute-done.5.refs_2_), channel_id=1, source_target_pairs={{0,480},{32,0},{64,32},{96,64},{128,96},{160,128},{192,160},{224,1... | collective-permute-start | bytes 1572872 | tf_op jit(solution)/shard_map/ppermute | solution.py:179
  87.8 15.7 %collective-permute-start.6 = (f32[128,1024]{1,0:T(8,128)S(1)}, f32[128,1024]{1,0:T(8,128)S(1)}, u32[]{:S(2)}, u32[]{:S(2)}) collective-permute-start(f32[128,1024]{1,0:T(8,128)S(1)} %collective-permute-done.4.refs_1_), channel_id=1, source_target_pairs={{0,32},{32,64},{64,96},{96,128},{128,160},{160,192},{192,224},{224... | collective-permute-start | bytes 1572872 | tf_op jit(solution)/shard_map/ppermute | solution.py:178
  99.3 13.8 %collective-permute-start.9 = (f32[128,1024]{1,0:T(8,128)S(1)}, f32[128,1024]{1,0:T(8,128)S(1)}, u32[]{:S(2)}, u32[]{:S(2)}) collective-permute-start(f32[128,1024]{1,0:T(8,128)S(1)} %collective-permute-done.7.refs_4_), channel_id=1, source_target_pairs={{0,480},{32,0},{64,32},{96,64},{128,96},{160,128},{192,160},{224,1... | collective-permute-start | bytes 1572872 | tf_op jit(solution)/shard_map/ppermute | solution.py:179
  102.7 0.8 copy-start.1
  103.5 13.9 %collective-permute-start.8 = (f32[128,1024]{1,0:T(8,128)S(1)}, f32[128,1024]{1,0:T(8,128)S(1)}, u32[]{:S(2)}, u32[]{:S(2)}) collective-permute-start(f32[128,1024]{1,0:T(8,128)S(1)} %collective-permute-done.6.refs_3_), channel_id=1, source_target_pairs={{0,32},{32,64},{64,96},{96,128},{128,160},{160,192},{192,224},{224... | collective-permute-start | bytes 1572872 | tf_op jit(solution)/shard_map/ppermute | solution.py:178
  105.9 0.8 copy-start.3
  113.1 12.9 %collective-permute-start.11 = (f32[128,1024]{1,0:T(8,128)S(1)}, f32[128,1024]{1,0:T(8,128)S(1)}, u32[]{:S(2)}, u32[]{:S(2)}) collective-permute-start(f32[128,1024]{1,0:T(8,128)S(1)} %collective-permute-done.9.refs_6_), channel_id=1, source_target_pairs={{0,480},{32,0},{64,32},{96,64},{128,96},{160,128},{192,160},{224,1... | collective-permute-start | bytes 1572872 | tf_op jit(solution)/shard_map/ppermute | solution.py:179
  116.6 0.8 copy-start.5
  117.4 13.0 %collective-permute-start.10 = (f32[128,1024]{1,0:T(8,128)S(1)}, f32[128,1024]{1,0:T(8,128)S(1)}, u32[]{:S(2)}, u32[]{:S(2)}) collective-permute-start(f32[128,1024]{1,0:T(8,128)S(1)} %collective-permute-done.8.refs_5_), channel_id=1, source_target_pairs={{0,32},{32,64},{64,96},{96,128},{128,160},{160,192},{192,224},{224... | collective-permute-start | bytes 1572872 | tf_op jit(solution)/shard_map/ppermute | solution.py:178
  119.7 0.8 copy-start.7
  125.9 12.1 %collective-permute-start.13 = (f32[128,1024]{1,0:T(8,128)S(1)}, f32[128,1024]{1,0:T(8,128)S(1)}, u32[]{:S(2)}, u32[]{:S(2)}) collective-permute-start(f32[128,1024]{1,0:T(8,128)S(1)} %collective-permute-done.11.refs_8_), channel_id=1, source_target_pairs={{0,480},{32,0},{64,32},{96,64},{128,96},{160,128},{192,160},{224,1... | collective-permute-start | bytes 1572872 | tf_op jit(solution)/shard_map/ppermute | solution.py:179
  129.7 0.8 copy-start.9
  130.5 19.1 %collective-permute-start.12 = (f32[128,1024]{1,0:T(8,128)S(1)}, f32[128,1024]{1,0:T(8,128)S(1)}, u32[]{:S(2)}, u32[]{:S(2)}) collective-permute-start(f32[128,1024]{1,0:T(8,128)S(1)} %collective-permute-done.10.refs_7_), channel_id=1, source_target_pairs={{0,32},{32,64},{64,96},{96,128},{128,160},{160,192},{192,224},{224... | collective-permute-start | bytes 1572872 | tf_op jit(solution)/shard_map/ppermute | solution.py:178
  132.6 0.8 copy-start.11
  138.0 22.7 %collective-permute-start.15 = (f32[128,1024]{1,0:T(8,128)S(1)}, f32[128,1024]{1,0:T(8,128)S(1)}, u32[]{:S(2)}, u32[]{:S(2)}) collective-permute-start(f32[128,1024]{1,0:T(8,128)S(1)} %collective-permute-done.13.refs_10_), channel_id=1, source_target_pairs={{0,480},{32,0},{64,32},{96,64},{128,96},{160,128},{192,160},{224,1... | collective-permute-start | bytes 1572872 | tf_op jit(solution)/shard_map/ppermute | solution.py:179
  148.8 0.8 copy-start.13
  149.5 18.9 %collective-permute-start.14 = (f32[128,1024]{1,0:T(8,128)S(1)}, f32[128,1024]{1,0:T(8,128)S(1)}, u32[]{:S(2)}, u32[]{:S(2)}) collective-permute-start(f32[128,1024]{1,0:T(8,128)S(1)} %collective-permute-done.12.refs_9_), channel_id=1, source_target_pairs={{0,32},{32,64},{64,96},{96,128},{128,160},{160,192},{192,224},{224... | collective-permute-start | bytes 1572872 | tf_op jit(solution)/shard_map/ppermute | solution.py:178
  151.5 0.8 copy-start.15
  160.7 14.0 %collective-permute-start.17 = (f32[128,1024]{1,0:T(8,128)S(1)}, f32[128,1024]{1,0:T(8,128)S(1)}, u32[]{:S(2)}, u32[]{:S(2)}) collective-permute-start(f32[128,1024]{1,0:T(8,128)S(1)} %collective-permute-done.15.refs_12_), channel_id=1, source_target_pairs={{0,480},{32,0},{64,32},{96,64},{128,96},{160,128},{192,160},{224,1... | collective-permute-start | bytes 1572872 | tf_op jit(solution)/shard_map/ppermute | solution.py:179
  166.3 0.8 copy-start.17
  168.4 13.9 %copy-start.19 = (f32[128,1024]{1,0:T(8,128)}, f32[128,1024]{1,0:T(8,128)S(1)}, u32[]{:S(2)}) copy-start(f32[128,1024]{1,0:T(8,128)S(1)} %collective-permute-done.14.refs_11_) | copy-start | bytes 1572868
  168.4 13.9 %collective-permute-start.16 = (f32[128,1024]{1,0:T(8,128)S(1)}, f32[128,1024]{1,0:T(8,128)S(1)}, u32[]{:S(2)}, u32[]{:S(2)}) collective-permute-start(f32[128,1024]{1,0:T(8,128)S(1)} %collective-permute-done.14.refs_11_), channel_id=1, source_target_pairs={{0,32},{32,64},{64,96},{96,128},{128,160},{160,192},{192,224},{224... | collective-permute-start | bytes 1572872 | tf_op jit(solution)/shard_map/ppermute | solution.py:178
  174.7 9.5 %collective-permute-start.19 = (f32[64,1024]{1,0:T(8,128)S(1)}, f32[64,1024]{1,0:T(8,128)S(1)}, u32[]{:S(2)}, u32[]{:S(2)}) collective-permute-start(f32[64,1024]{1,0:T(8,128)S(1)} %slice.69), channel_id=1, source_target_pairs={{0,480},{32,0},{64,32},{96,64},{128,96},{160,128},{192,160},{224,1... | collective-permute-start | bytes 786440 | tf_op jit(solution)/shard_map/ppermute | solution.py:185
  182.3 9.6 %collective-permute-start.18 = (f32[64,1024]{1,0:T(8,128)S(1)}, f32[64,1024]{1,0:T(8,128)}, u32[]{:S(2)}, u32[]{:S(2)}) collective-permute-start(f32[64,1024]{1,0:T(8,128)S(1)} %slice.68), channel_id=1, source_target_pairs={{0,32},{32,64},{64,96},{96,128},{128,160},{160,192},{192,224},{224... | collective-permute-start | bytes 786440 | tf_op jit(solution)/shard_map/ppermute | solution.py:184
  192.9 13.8 %copy-start = (f32[1024,256]{1,0:T(8,128)S(1)}, f32[1024,256]{1,0:T(8,128)}, u32[]{:S(2)}) copy-start(f32[1024,256]{1,0:T(8,128)} %rhs_ref.1) | copy-start | bytes 3145732
  192.9 13.8 %copy-start.2 = (f32[128,1024]{1,0:T(8,128)S(1)}, f32[128,1024]{1,0:T(8,128)}, u32[]{:S(2)}) copy-start(f32[128,1024]{1,0:T(8,128)} %copy-done.1) | copy-start | bytes 1572868
  192.9 13.8 %copy-start.4 = (f32[128,1024]{1,0:T(8,128)S(1)}, f32[128,1024]{1,0:T(8,128)}, u32[]{:S(2)}) copy-start(f32[128,1024]{1,0:T(8,128)} %copy-done.3) | copy-start | bytes 1572868
  193.0 13.8 %copy-start.6 = (f32[128,1024]{1,0:T(8,128)S(1)}, f32[128,1024]{1,0:T(8,128)}, u32[]{:S(2)}) copy-start(f32[128,1024]{1,0:T(8,128)} %copy-done.5) | copy-start | bytes 1572868
  193.0 13.8 %copy-start.8 = (f32[128,1024]{1,0:T(8,128)S(1)}, f32[128,1024]{1,0:T(8,128)}, u32[]{:S(2)}) copy-start(f32[128,1024]{1,0:T(8,128)} %copy-done.7) | copy-start | bytes 1572868
  193.0 13.8 %copy-start.10 = (f32[128,1024]{1,0:T(8,128)S(1)}, f32[128,1024]{1,0:T(8,128)}, u32[]{:S(2)}) copy-start(f32[128,1024]{1,0:T(8,128)} %copy-done.9) | copy-start | bytes 1572868
  193.0 13.8 %copy-start.12 = (f32[128,1024]{1,0:T(8,128)S(1)}, f32[128,1024]{1,0:T(8,128)}, u32[]{:S(2)}) copy-start(f32[128,1024]{1,0:T(8,128)} %copy-done.11) | copy-start | bytes 1572868
  193.0 13.8 %copy-start.14 = (f32[128,1024]{1,0:T(8,128)S(1)}, f32[128,1024]{1,0:T(8,128)}, u32[]{:S(2)}) copy-start(f32[128,1024]{1,0:T(8,128)} %copy-done.13) | copy-start | bytes 1572868
  193.0 13.8 %copy-start.16 = (f32[128,1024]{1,0:T(8,128)S(1)}, f32[128,1024]{1,0:T(8,128)}, u32[]{:S(2)}) copy-start(f32[128,1024]{1,0:T(8,128)} %copy-done.15) | copy-start | bytes 1572868
  193.0 13.8 %copy-start.18 = (f32[128,1024]{1,0:T(8,128)S(1)}, f32[128,1024]{1,0:T(8,128)}, u32[]{:S(2)}) copy-start(f32[128,1024]{1,0:T(8,128)} %copy-done.17) | copy-start | bytes 1572868
  193.0 13.8 %copy-start.20 = (f32[128,1024]{1,0:T(8,128)S(1)}, f32[128,1024]{1,0:T(8,128)}, u32[]{:S(2)}) copy-start(f32[128,1024]{1,0:T(8,128)} %copy-done.19) | copy-start | bytes 1572868
Sparse Core Ops, SparseCore 0:
  66.7 79.2 all-gather.2

commit v2 on v0

v2 whole, which is shorter than its diff:
```python
import functools

import jax
import jax.numpy as jnp
from jax import lax
from jax.experimental import pallas as pl
from jax.experimental.pallas import tpu as pltpu
from jax.sharding import PartitionSpec as P

F32 = jnp.float32
BF16 = jnp.bfloat16
VMEM_LIMIT = 20 * 1024 * 1024
UPDATE_LIMIT = 56 * 1024 * 1024


def split(a):
    high = a.astype(BF16)
    return high, (a - high.astype(F32)).astype(BF16)


def dot(a, b):
    return lax.dot_general(a, b, (((1,), (0,)), ((), ())), preferred_element_type=F32)


def product(a, b):
    a_high, a_low = split(a)
    b_high, b_low = split(b)
    return dot(a_high, b_high) + (dot(a_high, b_low) + dot(a_low, b_high))


def call(kernel, shapes, args, after=()):
    vmem = pl.BlockSpec(memory_space=pltpu.VMEM)

    def body(*refs):
        kernel(*refs[: len(args)], *refs[len(args) + len(after) :])

    return pl.pallas_call(
        body,
        out_shape=[jax.ShapeDtypeStruct(*s) for s in shapes],
        in_specs=[vmem] * len(args) + [pl.BlockSpec(memory_space=pl.ANY)] * len(after),
        out_specs=[vmem] * len(shapes),
        compiler_params=pltpu.CompilerParams(vmem_limit_bytes=VMEM_LIMIT),
        name=kernel.__name__,
    )(*args, *after)


def copy_out(copies_ref, block):
    for i in range(copies_ref.shape[0]):
        copies_ref[i] = block


def begin(across_ref, rows_b_ref, rows_a_ref, across_copies_ref, own_ref):
    half = across_ref.shape[0] // 2
    copy_out(across_copies_ref, jnp.concatenate([across_ref[:half, :], across_ref[half:, :]], axis=1))
    lines = rows_b_ref.shape[0]
    own_ref[:lines, :] = rows_b_ref[...]
    own_ref[lines:, :] = rows_a_ref[...]


def send(block_ref, copies_ref):
    copy_out(copies_ref, block_ref[...])


def solve(inverse_ref, rhs_ref, x_ref, copies_ref):
    panel, width = inverse_ref.shape[1], x_ref.shape[1]
    x = product(inverse_ref[...], rhs_ref[...].reshape(panel, width))
    x_ref[...] = x
    copy_out(copies_ref, x)


def couple(rhs_ref, across_ref, x_ref, copies_ref):
    planes, _, lanes = across_ref.shape
    lines = lanes // 2
    parts = [across_ref[z] for z in range(planes)]
    parts = [jnp.concatenate([p[:, :lines], p[:, lines:]], axis=0) for p in parts]
    width = rhs_ref.shape[1]
    x = x_ref[...].reshape(planes * lines, width)
    copy_out(copies_ref, rhs_ref[...] - product(jnp.concatenate(parts, axis=1), x))


def update_kernel(planes, sources, plane_ref, x_b_ref, x_a_ref, rhs_ref, *refs):
    row_refs, (out_ref, x_ref, high, low) = refs[:-4], refs[-4:]
    shards, shard, width = x_b_ref.shape
    lines = shards * shard // planes
    tile = 256
    depth = x_ref.shape[0]

    @pl.when(pl.program_id(0) == 0)
    def _():
        x = [r.reshape(shards * shard, width) for r in (x_b_ref, x_a_ref)]
        for n, (panel, offset) in enumerate(sources):
            place = lax.rem(plane_ref[0] + offset, planes)
            x_ref[n * lines : (n + 1) * lines] = x[panel][pl.ds(pl.multiple_of(place * lines, lines), lines), :]
        for k in range(0, depth, tile):
            x_high, x_low = split(x_ref[k : min(k + tile, depth)].T)
            high[:, k : k + tile] = x_high
            low[:, k : k + tile] = x_low

    total = None
    for k in range(0, depth, tile):
        pieces = row_refs[k // lines : (k + tile) // lines]
        l_high, l_low = split(jnp.concatenate([r[...] for r in pieces], axis=0))
        lanes = slice(k, k + l_high.shape[0])
        part = dot(high[:, lanes], l_high) + (dot(low[:, lanes], l_high) + dot(high[:, lanes], l_low))
        total = part if total is None else total + part
    out_ref[...] = rhs_ref[...] - total.T


def update(plane, x_b, x_a, rhs, blocks, sources, planes, name):
    height, width = rhs.shape
    tile = 256
    shards, shard, _ = x_b.shape
    lines = shards * shard // planes
    whole = pl.BlockSpec(x_b.shape, lambda n: (0, 0, 0))
    out = pl.BlockSpec((tile, width), lambda n: (n, 0))
    rows, specs = [], []
    for r, half in blocks:
        rows.append(r)
        specs.append(pl.BlockSpec((lines, tile), lambda n, half=half: (half, n)))
    depth = lines * len(sources)
    return pl.pallas_call(
        functools.partial(update_kernel, planes, tuple(sources)),
        grid=(height // tile,),
        out_shape=jax.ShapeDtypeStruct((height, width), F32),
        in_specs=[pl.BlockSpec(memory_space=pltpu.SMEM), whole, whole, out] + specs,
        out_specs=out,
        scratch_shapes=[pltpu.VMEM((depth, width), F32)] + [pltpu.VMEM((width, depth), BF16)] * 2,
        compiler_params=pltpu.CompilerParams(vmem_limit_bytes=UPDATE_LIMIT),
        name=name,
    )(plane, x_b, x_a, rhs, *rows)


def exchange(copies, axis):
    return lax.all_to_all(copies, axis, 0, 0, tiled=True)


def ring(own, planes):
    def move(block, by):
        return lax.ppermute(block, "row", [(i, (i + by) % planes) for i in range(planes)])

    up = down = own
    blocks, offsets = [own], [0]
    half = planes // 2
    for step in range(1, half):
        up, down = move(up, 1), move(down, -1)
        blocks += [up, down]
        offsets += [planes - step, step]
    middle = own.shape[0] // 2
    blocks += [move(up[:middle], 1), move(down[middle:], -1)]
    offsets += [half]
    return blocks, tuple(offsets)


def make(planes, columns):
    def shards(rhs_above, rhs_a, rhs_b, rows_a_above, rows_b_above, rows_b_a, inverse_a, inverse_b):
        shard, width = rhs_b.shape
        lines, height = rows_b_above.shape
        plane = lax.axis_index("row").astype(jnp.int32).reshape(1)
        local = ((shard, width), F32)
        copies = ((columns, shard, width), F32)

        across_copies, own = call(
            begin,
            [((planes, shard // 2, 2 * lines), F32), ((2 * lines, height), F32)],
            [rows_b_a.T, rows_b_above, rows_a_above],
        )
        blocks, offsets = ring(own, planes)
        across = exchange(across_copies, "row")
        (rhs_copies,) = call(send, [copies], [rhs_b])
        x_b, x_copies = call(solve, [local, copies], [inverse_b.T, exchange(rhs_copies, "col")], after=blocks[1:3])
        x_b_all = exchange(x_copies, "col")
        (coupled,) = call(couple, [copies], [rhs_a, across, x_b_all], after=blocks[5:7])
        x_a, x_copies = call(solve, [local, copies], [inverse_a.T, exchange(coupled, "col")], after=blocks[9:11])
        x_a_all = exchange(x_copies, "col")

        near, offsets = offsets[:-1], offsets[-1]
        whole, halves = blocks[:-2], blocks[-2:]
        partial = update(
            plane, x_b_all, x_b_all, rhs_above, [(r, 0) for r in whole], [(0, z) for z in near], planes, "update_b"
        )
        updated = update(
            plane,
            x_b_all,
            x_a_all,
            partial,
            [(r, 1) for r in whole] + [(r, 0) for r in halves],
            [(1, z) for z in near] + [(0, offsets), (1, offsets)],
            planes,
            "update_a",
        )
        return x_b, x_a, updated

    return shards


def solution(mesh):
    in_specs = (
        P("col", "row"),
        P("col", "row"),
        P("col", "row"),
        P("row", "col"),
        P("row", "col"),
        P("row", "col"),
        P(None, "col"),
        P(None, "col"),
    )
    out_specs = (P("col", "row"), P("col", "row"), P("col", "row"))
    return jax.shard_map(
        make(mesh.shape["row"], mesh.shape["col"]),
        mesh=mesh,
        in_specs=in_specs,
        out_specs=out_specs,
        check_vma=False,
    )
```

time: 427 us -> 171 us (0.40)
  waiting for transfers between devices: 367 us -> 37.3 us
  starting transfers between devices: 0.24 us -> 106 us
  blocking collectives: 25.2 us -> 0 us
  Pallas kernels: 0 us -> 19.8 us
  matrix products: 19 us -> 0 us
  between operations: 14.2 us -> 1.08 us
    all_gather x6 -> x0, waiting for transfers between devices: 365 us -> none  [the longest x2 140 us: update_above(): lax.all_gather(factor_rows, 'row', axis=1, tiled=True)]
    ppermute x0 -> x16, starting transfers between devices: none -> 58.6 us  [move(): lax.ppermute(block, 'row', [(i, (i + by) % planes) for i in range(planes)])]
    all_to_all x0 -> x5, starting transfers between devices: none -> 47.9 us  [exchange(): return lax.all_to_all(copies, axis, 0, 0, tiled=True)]
    ppermute x0 -> x16, waiting for transfers between devices: none -> 28.3 us  [move(): lax.ppermute(block, 'row', [(i, (i + by) % planes) for i in range(planes)])]
    all_gather x1 -> x0, blocking collectives: 25.2 us -> none  [second_panel(): lax.all_gather(rows_b_a, 'row', axis=0, tiled=True)]
    pallas_call x0 -> x7, Pallas kernels: none -> 19.8 us  [the longest x2 14 us: update(): pl.pallas_call(functools.partial(update_kernel, planes, tuple(sources)),...]
    dot_general x5 -> x0, matrix products: 19 us -> none  [the longest x2 11.5 us: contract_stack(): lax.dot_general(left, right, (((0, 1), (0, 1)), ((), ())), precision=HIGH...]
    all_to_all x0 -> x5, waiting for transfers between devices: none -> 8.95 us  [exchange(): return lax.all_to_all(copies, axis, 0, 0, tiled=True)]
  transfers between devices with their start and end apart: 6 -> 21, of which waited for: 6 -> 7; matrix products, arithmetic and copies ran while one was open for 2% -> 0% of each run, Pallas kernels for 0% -> 7%
where the time goes in v2:
time: 171 us; the launch traced here: 169 us
  starting transfers between devices  106 us (62%)
  waiting for transfers between devices  37.3 us (22%)
  Pallas kernels  19.8 us (12%)
  local copies, waits for them, and re-layouts  4.26 us (2%)
    ppermute x16, starting transfers between devices, move(): lax.ppermute(block, 'row', [(i, (i + by) % planes) for i in range(planes)])  58.6 us
    all_to_all x5, starting transfers between devices, exchange(): return lax.all_to_all(copies, axis, 0, 0, tiled=True)  47.9 us
    ppermute x16, waiting for transfers between devices, move(): lax.ppermute(block, 'row', [(i, (i + by) % planes) for i in range(planes)])  28.3 us
    pallas_call x2, Pallas kernels, update(): pl.pallas_call(functools.partial(update_kernel, planes, tuple(sources)),...  14 us
    all_to_all x5, waiting for transfers between devices, exchange(): return lax.all_to_all(copies, axis, 0, 0, tiled=True)  8.95 us
    pallas_call x5, Pallas kernels, call(): pl.pallas_call(body, out_shape=[jax.ShapeDtypeStruct(*s) for s in shapes]...  5.89 us
    unnamed x46, local copies, waits for them, and re-layouts  3.44 us
  transfers between devices with their start and end apart: 21, of which 7 were waited for; matrix products, arithmetic and copies ran while one was open for 0% of the time, Pallas kernels for 7%

profile of v2, /device:TPU:1, one launch (start us, length us, event | category | flops | bytes accessed | tf_op | source)
XLA Modules:
  0.0 168.9 jit_solution(8186373457993380576)
XLA Ops:
  0.6 0.0 copy-start.14
  0.6 0.7 copy-done.14
  1.4 1.1 send.1
  2.5 10.6 %all-to-all-start = ((f32[32,32,256]{2,1,0:T(8,128)}), f32[32,32,256]{2,1,0:T(8,128)S(1)}, u32[]{:S(2)}, u32[]{:S(2)}) async-start(f32[32,32,256]{2,1,0:T(8,128)} %send.1), calls=%async_computation | async-start | bytes 2097152 | tf_op jit(solution)/shard_map/all_to_all | solution.py:134
  13.1 0.7 begin.1
  13.8 9.2 %collective-permute-start.1 = (f32[128,1024]{1,0:T(8,128)S(1)}, f32[128,1024]{1,0:T(8,128)S(1)}, u32[]{:S(2)}, u32[]{:S(2)}) collective-permute-start(f32[128,1024]{1,0:T(8,128)S(1)} %get-tuple-element.9.refs_0_), channel_id=1, source_target_pairs={{0,480},{32,0},{64,32},{96,64},{128,96},{160,128},{192,160},{224,1... | collective-permute-start | bytes 1572872 | tf_op jit(solution)/shard_map/ppermute | solution.py:139
  23.1 1.9 %collective-permute-start = (f32[128,1024]{1,0:T(8,128)S(1)}, f32[128,1024]{1,0:T(8,128)S(1)}, u32[]{:S(2)}, u32[]{:S(2)}) collective-permute-start(f32[128,1024]{1,0:T(8,128)S(1)} %get-tuple-element.9.refs_0_), channel_id=1, source_target_pairs={{0,32},{32,64},{64,96},{96,128},{128,160},{160,192},{192,224},{224... | collective-permute-start | bytes 1572872 | tf_op jit(solution)/shard_map/ppermute | solution.py:139
  25.0 5.4 %all-to-all-done.refs_1_ = f32[32,32,256]{2,1,0:T(8,128)S(1)} async-done(((f32[32,32,256]{2,1,0:T(8,128)}), f32[32,32,256]{2,1,0:T(8,128)S(1)}, u32[]{:S(2)}, u32[]{:S(2)}) %all-to-all-start) | async-done | bytes 1048608 | tf_op jit(solution)/shard_map/all_to_all | solution.py:134
  30.4 13.1 %all-to-all-start.1 = ((f32[16,16,128]{2,1,0:T(8,128)}), f32[16,16,128]{2,1,0:T(8,128)S(1)}, u32[]{:S(2)}, u32[]{:S(2)}) async-start(f32[16,16,128]{2,1,0:T(8,128)} %get-tuple-element.11), calls=%async_computation.1 | async-start | bytes 262144 | tf_op jit(solution)/shard_map/all_to_all | solution.py:134
  43.4 0.0 collective-permute-done.1.refs_3_.refs_2_
  43.5 4.5 %collective-permute-start.4 = (f32[128,1024]{1,0:T(8,128)S(1)}, f32[128,1024]{1,0:T(8,128)S(1)}, u32[]{:S(2)}, u32[]{:S(2)}) collective-permute-start(f32[128,1024]{1,0:T(8,128)S(1)} %collective-permute-done.1.refs_3_.refs_2_), channel_id=1, source_target_pairs={{0,480},{32,0},{64,32},{96,64},{128,96},{160,128},{192,160},{224,1... | collective-permute-start | bytes 1572872 | tf_op jit(solution)/shard_map/ppermute | solution.py:139
  48.0 0.0 collective-permute-done.refs_2_.refs_1_
  48.0 1.9 %collective-permute-start.2 = (f32[128,1024]{1,0:T(8,128)S(1)}, f32[128,1024]{1,0:T(8,128)}, u32[]{:S(2)}, u32[]{:S(2)}) collective-permute-start(f32[128,1024]{1,0:T(8,128)S(1)} %collective-permute-done.refs_2_.refs_1_), channel_id=1, source_target_pairs={{0,32},{32,64},{64,96},{96,128},{128,160},{160,192},{192,224},{224... | collective-permute-start | bytes 1572872 | tf_op jit(solution)/shard_map/ppermute | solution.py:139
  49.9 1.1 solve.2
  51.0 0.0 copy-done.1
  51.0 1.0 copy-done.8
  52.0 3.6 %all-to-all-done.1.refs_1_ = f32[16,16,128]{2,1,0:T(8,128)S(1)} async-done(((f32[16,16,128]{2,1,0:T(8,128)}), f32[16,16,128]{2,1,0:T(8,128)S(1)}, u32[]{:S(2)}, u32[]{:S(2)}) %all-to-all-start.1) | async-done | bytes 131104 | tf_op jit(solution)/shard_map/all_to_all | solution.py:134
  55.6 6.9 %all-to-all-start.2 = ((f32[32,32,256]{2,1,0:T(8,128)}), f32[32,32,256]{2,1,0:T(8,128)S(1)}, u32[]{:S(2)}, u32[]{:S(2)}) async-start(f32[32,32,256]{2,1,0:T(8,128)} %copy-done.8), calls=%async_computation.2 | async-start | bytes 2097152 | tf_op jit(solution)/shard_map/all_to_all | solution.py:134
  62.5 0.5 collective-permute-done.4.refs_4_
  63.0 3.9 %collective-permute-start.5 = (f32[128,1024]{1,0:T(8,128)S(1)}, f32[128,1024]{1,0:T(8,128)S(1)}, u32[]{:S(2)}, u32[]{:S(2)}) collective-permute-start(f32[128,1024]{1,0:T(8,128)S(1)} %collective-permute-done.4.refs_4_), channel_id=1, source_target_pairs={{0,480},{32,0},{64,32},{96,64},{128,96},{160,128},{192,160},{224,1... | collective-permute-start | bytes 1572872 | tf_op jit(solution)/shard_map/ppermute | solution.py:139
  67.0 0.0 collective-permute-done.2.refs_3_
  67.0 1.9 %collective-permute-start.3 = (f32[128,1024]{1,0:T(8,128)}, f32[128,1024]{1,0:T(8,128)S(1)}, u32[]{:S(2)}, u32[]{:S(2)}) collective-permute-start(f32[128,1024]{1,0:T(8,128)} %collective-permute-done.2.refs_3_), channel_id=1, source_target_pairs={{0,32},{32,64},{64,96},{96,128},{128,160},{160,192},{192,224},{224... | collective-permute-start | bytes 1572872 | tf_op jit(solution)/shard_map/ppermute | solution.py:139
  68.9 9.1 %collective-permute-done.5.refs_4_.refs_6_ = f32[128,1024]{1,0:T(8,128)S(1)} collective-permute-done((f32[128,1024]{1,0:T(8,128)S(1)}, f32[128,1024]{1,0:T(8,128)S(1)}, u32[]{:S(2)}, u32[]{:S(2)}) %collective-permute-start.5) | collective-permute-done | bytes 524320 | tf_op jit(solution)/shard_map/ppermute | solution.py:139
  78.0 5.3 %collective-permute-start.8 = (f32[128,1024]{1,0:T(8,128)S(1)}, f32[128,1024]{1,0:T(8,128)}, u32[]{:S(2)}, u32[]{:S(2)}) collective-permute-start(f32[128,1024]{1,0:T(8,128)S(1)} %collective-permute-done.5.refs_4_.refs_6_), channel_id=1, source_target_pairs={{0,480},{32,0},{64,32},{96,64},{128,96},{160,128},{192,160},{224,1... | collective-permute-start | bytes 1572872 | tf_op jit(solution)/shard_map/ppermute | solution.py:139
  83.3 0.0 collective-permute-done.3.refs_3_.refs_5_
  83.3 1.9 %collective-permute-start.6 = (f32[128,1024]{1,0:T(8,128)S(1)}, f32[128,1024]{1,0:T(8,128)}, u32[]{:S(2)}, u32[]{:S(2)}) collective-permute-start(f32[128,1024]{1,0:T(8,128)S(1)} %collective-permute-done.3.refs_3_.refs_5_), channel_id=1, source_target_pairs={{0,32},{32,64},{64,96},{96,128},{128,160},{160,192},{192,224},{224... | collective-permute-start | bytes 1572872 | tf_op jit(solution)/shard_map/ppermute | solution.py:139
  85.3 0.0 all-to-all-done.2.refs_2_.x_b_ref.x_a_ref
  85.3 1.5 couple.1
  86.8 0.0 copy-done.4
  86.8 0.0 copy-start.12
  86.9 8.6 %all-to-all-start.3 = ((f32[32,32,256]{2,1,0:T(8,128)}), f32[32,32,256]{2,1,0:T(8,128)S(1)}, u32[]{:S(2)}, u32[]{:S(2)}) async-start(f32[32,32,256]{2,1,0:T(8,128)} %couple.1), calls=%async_computation.3 | async-start | bytes 2097152 | tf_op jit(solution)/shard_map/all_to_all | solution.py:134
  95.4 0.0 collective-permute-done.8.refs_8_
  95.4 4.9 %collective-permute-start.9 = (f32[128,1024]{1,0:T(8,128)}, f32[128,1024]{1,0:T(8,128)S(1)}, u32[]{:S(2)}, u32[]{:S(2)}) collective-permute-start(f32[128,1024]{1,0:T(8,128)} %collective-permute-done.8.refs_8_), channel_id=1, source_target_pairs={{0,480},{32,0},{64,32},{96,64},{128,96},{160,128},{192,160},{224,1... | collective-permute-start | bytes 1572872 | tf_op jit(solution)/shard_map/ppermute | solution.py:139
  100.3 0.0 collective-permute-done.6.refs_7_
  100.3 1.9 %collective-permute-start.7 = (f32[128,1024]{1,0:T(8,128)}, f32[128,1024]{1,0:T(8,128)S(1)}, u32[]{:S(2)}, u32[]{:S(2)}) collective-permute-start(f32[128,1024]{1,0:T(8,128)} %collective-permute-done.6.refs_7_), channel_id=1, source_target_pairs={{0,32},{32,64},{64,96},{96,128},{128,160},{160,192},{192,224},{224... | collective-permute-start | bytes 1572872 | tf_op jit(solution)/shard_map/ppermute | solution.py:139
  102.2 9.1 %collective-permute-done.9.refs_3_.refs_10_ = f32[128,1024]{1,0:T(8,128)S(1)} collective-permute-done((f32[128,1024]{1,0:T(8,128)}, f32[128,1024]{1,0:T(8,128)S(1)}, u32[]{:S(2)}, u32[]{:S(2)}) %collective-permute-start.9) | collective-permute-done | bytes 524320 | tf_op jit(solution)/shard_map/ppermute | solution.py:139
  111.3 5.2 %collective-permute-start.11 = (f32[128,1024]{1,0:T(8,128)S(1)}, f32[128,1024]{1,0:T(8,128)S(1)}, u32[]{:S(2)}, u32[]{:S(2)}) collective-permute-start(f32[128,1024]{1,0:T(8,128)S(1)} %collective-permute-done.9.refs_3_.refs_10_), channel_id=1, source_target_pairs={{0,480},{32,0},{64,32},{96,64},{128,96},{160,128},{192,160},{224,1... | collective-permute-start | bytes 1572872 | tf_op jit(solution)/shard_map/ppermute | solution.py:139
  116.5 0.0 collective-permute-done.7.refs_2_.refs_9_
  116.5 1.9 %collective-permute-start.10 = (f32[128,1024]{1,0:T(8,128)S(1)}, f32[128,1024]{1,0:T(8,128)}, u32[]{:S(2)}, u32[]{:S(2)}) collective-permute-start(f32[128,1024]{1,0:T(8,128)S(1)} %collective-permute-done.7.refs_2_.refs_9_), channel_id=1, source_target_pairs={{0,32},{32,64},{64,96},{96,128},{128,160},{160,192},{192,224},{224... | collective-permute-start | bytes 1572872 | tf_op jit(solution)/shard_map/ppermute | solution.py:139
  118.5 0.0 all-to-all-done.3.refs_1_
  118.5 1.5 solve.3
  119.9 0.0 copy-done.5
  119.9 8.7 %all-to-all-start.4 = ((f32[32,32,256]{2,1,0:T(8,128)}), f32[32,32,256]{2,1,0:T(8,128)S(1)}, u32[]{:S(2)}, u32[]{:S(2)}) async-start(f32[32,32,256]{2,1,0:T(8,128)} %get-tuple-element.14), calls=%async_computation.4 | async-start | bytes 2097152 | tf_op jit(solution)/shard_map/all_to_all | solution.py:134
  128.7 0.0 collective-permute-done.11.refs_12_
  128.7 0.0 copy-start.20
  128.7 4.9 %collective-permute-start.13 = (f32[128,1024]{1,0:T(8,128)S(1)}, f32[128,1024]{1,0:T(8,128)S(1)}, u32[]{:S(2)}, u32[]{:S(2)}) collective-permute-start(f32[128,1024]{1,0:T(8,128)S(1)} %collective-permute-done.11.refs_12_), channel_id=1, source_target_pairs={{0,480},{32,0},{64,32},{96,64},{128,96},{160,128},{192,160},{224,1... | collective-permute-start | bytes 1572872 | tf_op jit(solution)/shard_map/ppermute | solution.py:139
  133.6 0.0 collective-permute-done.10.refs_11_
  133.6 1.9 %collective-permute-start.12 = (f32[128,1024]{1,0:T(8,128)}, f32[128,1024]{1,0:T(8,128)S(1)}, u32[]{:S(2)}, u32[]{:S(2)}) collective-permute-start(f32[128,1024]{1,0:T(8,128)} %collective-permute-done.10.refs_11_), channel_id=1, source_target_pairs={{0,32},{32,64},{64,96},{96,128},{128,160},{160,192},{192,224},{224... | collective-permute-start | bytes 1572872 | tf_op jit(solution)/shard_map/ppermute | solution.py:139
  135.5 9.0 %collective-permute-done.13.refs_14_ = f32[128,1024]{1,0:T(8,128)S(1)} collective-permute-done((f32[128,1024]{1,0:T(8,128)S(1)}, f32[128,1024]{1,0:T(8,128)S(1)}, u32[]{:S(2)}, u32[]{:S(2)}) %collective-permute-start.13) | collective-permute-done | bytes 524320 | tf_op jit(solution)/shard_map/ppermute | solution.py:139
  144.5 5.3 %collective-permute-start.15 = (f32[64,1024]{1,0:T(8,128)S(1)}, f32[64,1024]{1,0:T(8,128)S(1)}, u32[]{:S(2)}, u32[]{:S(2)}) collective-permute-start(f32[64,1024]{1,0:T(8,128)S(1)} %slice.9), channel_id=1, source_target_pairs={{0,480},{32,0},{64,32},{96,64},{128,96},{160,128},{192,160},{224,1... | collective-permute-start | bytes 786440 | tf_op jit(solution)/shard_map/ppermute | solution.py:139
  149.8 0.0 collective-permute-done.12.refs_13_
  149.8 0.0 copy-start.18
  149.8 0.8 slice.8
  150.6 0.0 copy-done.17
  150.6 1.9 %collective-permute-start.14 = (f32[64,1024]{1,0:T(8,128)}, f32[64,1024]{1,0:T(8,128)S(1)}, u32[]{:S(2)}, u32[]{:S(2)}) collective-permute-start(f32[64,1024]{1,0:T(8,128)} %slice.8), channel_id=1, source_target_pairs={{0,32},{32,64},{64,96},{96,128},{128,160},{160,192},{192,224},{224... | collective-permute-start | bytes 786440 | tf_op jit(solution)/shard_map/ppermute | solution.py:139
  152.5 0.0 copy-done.20
  152.5 0.0 copy-done.18
  152.6 6.9 %update_b.1.rhs_ref = f32[1024,256]{1,0:T(8,128)} custom-call(s32[1]{0:T(128)} %bitcast.3.plane_ref, f32[32,32,256]{2,1,0:T(8,128)} %copy-done, f32[32,32,256]{2,1,0:T(8,128)} %copy-done, f32[1024,256]{1,0:T(8,128)} %rhs_ref.1, f32[128,1024]{1,0:T(8,128)} %copy-done.7, f32[128,1024]{1,0:T(8,128)} %copy-done.2, f32[128,1024]{1,0:T(8,128)} %copy-done.1, ...), custom_call_target="tpu_custom_call" | custom-call | tf_op jit(solution)/shard_map/update_b/pallas_call | solution.py:121
  159.5 0.0 collective-permute-done.15.refs_16_
  159.5 0.7 collective-permute-done.14.refs_15_
  160.2 0.0 all-to-all-done.4.x_a_ref
  160.2 0.7 copy-done.22
  160.9 1.0 copy-done.16
  161.9 7.0 %update_a.1 = f32[1024,256]{1,0:T(8,128)} custom-call(s32[1]{0:T(128)} %bitcast.3.plane_ref, f32[32,32,256]{2,1,0:T(8,128)} %copy-done, f32[32,32,256]{2,1,0:T(8,128)} %copy-done.16, f32[1024,256]{1,0:T(8,128)} %update_b.1.rhs_ref, f32[128,1024]{1,0:T(8,128)} %copy-done.7, f32[128,1024]{1,0:T(8,128)} %copy-done.2, f32[128,1024]{1,0:T(8,128)} %copy-done.1, ...), custom_call_target="tpu_custom_call" | custom-call | tf_op jit(solution)/shard_map/update_a/pallas_call | solution.py:121
  (33 shorter events, 0.1 us)
Async XLA Ops:
  0.6 0.8 copy-start.14
  2.5 10.6 %copy-start.9 = (f32[64,1024]{1,0:T(8,128)S(1)}, f32[64,1024]{1,0:T(8,128)}, u32[]{:S(2)}) copy-start(f32[64,1024]{1,0:T(8,128)} %refs_1_.1) | copy-start | bytes 786436
  2.5 10.6 %copy-start.10 = (f32[64,1024]{1,0:T(8,128)S(1)}, f32[64,1024]{1,0:T(8,128)}, u32[]{:S(2)}) copy-start(f32[64,1024]{1,0:T(8,128)} %refs_2_.1) | copy-start | bytes 786436
  2.5 10.6 %copy-start.15 = (f32[64,32]{0,1:T(8,128)S(1)}, f32[64,32]{0,1:T(8,128)}, u32[]{:S(2)}) copy-start(f32[64,32]{0,1:T(8,128)} %param.13) | copy-start | bytes 24580
  2.5 27.9 %all-to-all-start = ((f32[32,32,256]{2,1,0:T(8,128)}), f32[32,32,256]{2,1,0:T(8,128)S(1)}, u32[]{:S(2)}, u32[]{:S(2)}) async-start(f32[32,32,256]{2,1,0:T(8,128)} %send.1), calls=%async_computation | async-start | bytes 2097152 | tf_op jit(solution)/shard_map/all_to_all | solution.py:134
  13.8 37.2 %copy-start.7 = (f32[128,1024]{1,0:T(8,128)}, f32[128,1024]{1,0:T(8,128)S(1)}, u32[]{:S(2)}) copy-start(f32[128,1024]{1,0:T(8,128)S(1)} %get-tuple-element.9.refs_0_) | copy-start | bytes 1572868
  13.8 29.6 %collective-permute-start.1 = (f32[128,1024]{1,0:T(8,128)S(1)}, f32[128,1024]{1,0:T(8,128)S(1)}, u32[]{:S(2)}, u32[]{:S(2)}) collective-permute-start(f32[128,1024]{1,0:T(8,128)S(1)} %get-tuple-element.9.refs_0_), channel_id=1, source_target_pairs={{0,480},{32,0},{64,32},{96,64},{128,96},{160,128},{192,160},{224,1... | collective-permute-start | bytes 1572872 | tf_op jit(solution)/shard_map/ppermute | solution.py:139
  23.1 24.9 %collective-permute-start = (f32[128,1024]{1,0:T(8,128)S(1)}, f32[128,1024]{1,0:T(8,128)S(1)}, u32[]{:S(2)}, u32[]{:S(2)}) collective-permute-start(f32[128,1024]{1,0:T(8,128)S(1)} %get-tuple-element.9.refs_0_), channel_id=1, source_target_pairs={{0,32},{32,64},{64,96},{96,128},{128,160},{160,192},{192,224},{224... | collective-permute-start | bytes 1572872 | tf_op jit(solution)/shard_map/ppermute | solution.py:139
  30.4 19.5 %copy-start.11 = (f32[1024,32]{0,1:T(8,128)S(1)}, f32[1024,32]{0,1:T(8,128)}, u32[]{:S(2)}) copy-start(f32[1024,32]{0,1:T(8,128)} %param.15) | copy-start | bytes 393220
  30.4 25.2 %all-to-all-start.1 = ((f32[16,16,128]{2,1,0:T(8,128)}), f32[16,16,128]{2,1,0:T(8,128)S(1)}, u32[]{:S(2)}, u32[]{:S(2)}) async-start(f32[16,16,128]{2,1,0:T(8,128)} %get-tuple-element.11), calls=%async_computation.1 | async-start | bytes 262144 | tf_op jit(solution)/shard_map/all_to_all | solution.py:134
  43.5 7.6 %copy-start.1 = (f32[128,1024]{1,0:T(8,128)}, f32[128,1024]{1,0:T(8,128)S(1)}, u32[]{:S(2)}) copy-start(f32[128,1024]{1,0:T(8,128)S(1)} %collective-permute-done.1.refs_3_.refs_2_) | copy-start | bytes 1572868
  43.5 19.6 %collective-permute-start.4 = (f32[128,1024]{1,0:T(8,128)S(1)}, f32[128,1024]{1,0:T(8,128)S(1)}, u32[]{:S(2)}, u32[]{:S(2)}) collective-permute-start(f32[128,1024]{1,0:T(8,128)S(1)} %collective-permute-done.1.refs_3_.refs_2_), channel_id=1, source_target_pairs={{0,480},{32,0},{64,32},{96,64},{128,96},{160,128},{192,160},{224,1... | collective-permute-start | bytes 1572872 | tf_op jit(solution)/shard_map/ppermute | solution.py:139
  48.0 3.1 %copy-start.2 = (f32[128,1024]{1,0:T(8,128)}, f32[128,1024]{1,0:T(8,128)S(1)}, u32[]{:S(2)}) copy-start(f32[128,1024]{1,0:T(8,128)S(1)} %collective-permute-done.refs_2_.refs_1_) | copy-start | bytes 1572868
  48.0 19.0 %collective-permute-start.2 = (f32[128,1024]{1,0:T(8,128)S(1)}, f32[128,1024]{1,0:T(8,128)}, u32[]{:S(2)}, u32[]{:S(2)}) collective-permute-start(f32[128,1024]{1,0:T(8,128)S(1)} %collective-permute-done.refs_2_.refs_1_), channel_id=1, source_target_pairs={{0,32},{32,64},{64,96},{96,128},{128,160},{160,192},{192,224},{224... | collective-permute-start | bytes 1572872 | tf_op jit(solution)/shard_map/ppermute | solution.py:139
  51.0 1.0 copy-start.8
  55.6 29.7 %copy-start.13 = (f32[32,256]{1,0:T(8,128)S(1)}, f32[32,256]{1,0:T(8,128)}, u32[]{:S(2)}) copy-start(f32[32,256]{1,0:T(8,128)} %refs_0_.3) | copy-start | bytes 98308
  55.6 29.7 %all-to-all-start.2 = ((f32[32,32,256]{2,1,0:T(8,128)}), f32[32,32,256]{2,1,0:T(8,128)S(1)}, u32[]{:S(2)}, u32[]{:S(2)}) async-start(f32[32,32,256]{2,1,0:T(8,128)} %copy-done.8), calls=%async_computation.2 | async-start | bytes 2097152 | tf_op jit(solution)/shard_map/all_to_all | solution.py:134
  63.0 23.8 %copy-start.19 = (f32[128,1024]{1,0:T(8,128)}, f32[128,1024]{1,0:T(8,128)S(1)}, u32[]{:S(2)}) copy-start(f32[128,1024]{1,0:T(8,128)S(1)} %collective-permute-done.4.refs_4_) | copy-start | bytes 1572868
  63.0 15.0 %collective-permute-start.5 = (f32[128,1024]{1,0:T(8,128)S(1)}, f32[128,1024]{1,0:T(8,128)S(1)}, u32[]{:S(2)}, u32[]{:S(2)}) collective-permute-start(f32[128,1024]{1,0:T(8,128)S(1)} %collective-permute-done.4.refs_4_), channel_id=1, source_target_pairs={{0,480},{32,0},{64,32},{96,64},{128,96},{160,128},{192,160},{224,1... | collective-permute-start | bytes 1572872 | tf_op jit(solution)/shard_map/ppermute | solution.py:139
  67.0 16.3 %collective-permute-start.3 = (f32[128,1024]{1,0:T(8,128)}, f32[128,1024]{1,0:T(8,128)S(1)}, u32[]{:S(2)}, u32[]{:S(2)}) collective-permute-start(f32[128,1024]{1,0:T(8,128)} %collective-permute-done.2.refs_3_), channel_id=1, source_target_pairs={{0,32},{32,64},{64,96},{96,128},{128,160},{160,192},{192,224},{224... | collective-permute-start | bytes 1572872 | tf_op jit(solution)/shard_map/ppermute | solution.py:139
  78.0 8.8 %copy-start.3 = (f32[128,1024]{1,0:T(8,128)}, f32[128,1024]{1,0:T(8,128)S(1)}, u32[]{:S(2)}) copy-start(f32[128,1024]{1,0:T(8,128)S(1)} %collective-permute-done.5.refs_4_.refs_6_) | copy-start | bytes 1572868
  78.0 17.4 %collective-permute-start.8 = (f32[128,1024]{1,0:T(8,128)S(1)}, f32[128,1024]{1,0:T(8,128)}, u32[]{:S(2)}, u32[]{:S(2)}) collective-permute-start(f32[128,1024]{1,0:T(8,128)S(1)} %collective-permute-done.5.refs_4_.refs_6_), channel_id=1, source_target_pairs={{0,480},{32,0},{64,32},{96,64},{128,96},{160,128},{192,160},{224,1... | collective-permute-start | bytes 1572872 | tf_op jit(solution)/shard_map/ppermute | solution.py:139
  83.3 3.5 %copy-start.4 = (f32[128,1024]{1,0:T(8,128)}, f32[128,1024]{1,0:T(8,128)S(1)}, u32[]{:S(2)}) copy-start(f32[128,1024]{1,0:T(8,128)S(1)} %collective-permute-done.3.refs_3_.refs_5_) | copy-start | bytes 1572868
  83.3 16.9 %collective-permute-start.6 = (f32[128,1024]{1,0:T(8,128)S(1)}, f32[128,1024]{1,0:T(8,128)}, u32[]{:S(2)}, u32[]{:S(2)}) collective-permute-start(f32[128,1024]{1,0:T(8,128)S(1)} %collective-permute-done.3.refs_3_.refs_5_), channel_id=1, source_target_pairs={{0,32},{32,64},{64,96},{96,128},{128,160},{160,192},{192,224},{224... | collective-permute-start | bytes 1572872 | tf_op jit(solution)/shard_map/ppermute | solution.py:139
  85.3 1.5 copy-start
  86.8 31.6 %copy-start.12 = (f32[1024,32]{0,1:T(8,128)S(1)}, f32[1024,32]{0,1:T(8,128)}, u32[]{:S(2)}) copy-start(f32[1024,32]{0,1:T(8,128)} %param.14) | copy-start | bytes 393220
  86.9 31.6 %all-to-all-start.3 = ((f32[32,32,256]{2,1,0:T(8,128)}), f32[32,32,256]{2,1,0:T(8,128)S(1)}, u32[]{:S(2)}, u32[]{:S(2)}) async-start(f32[32,32,256]{2,1,0:T(8,128)} %couple.1), calls=%async_computation.3 | async-start | bytes 2097152 | tf_op jit(solution)/shard_map/all_to_all | solution.py:134
  95.4 15.9 %collective-permute-start.9 = (f32[128,1024]{1,0:T(8,128)}, f32[128,1024]{1,0:T(8,128)S(1)}, u32[]{:S(2)}, u32[]{:S(2)}) collective-permute-start(f32[128,1024]{1,0:T(8,128)} %collective-permute-done.8.refs_8_), channel_id=1, source_target_pairs={{0,480},{32,0},{64,32},{96,64},{128,96},{160,128},{192,160},{224,1... | collective-permute-start | bytes 1572872 | tf_op jit(solution)/shard_map/ppermute | solution.py:139
  100.3 16.2 %collective-permute-start.7 = (f32[128,1024]{1,0:T(8,128)}, f32[128,1024]{1,0:T(8,128)S(1)}, u32[]{:S(2)}, u32[]{:S(2)}) collective-permute-start(f32[128,1024]{1,0:T(8,128)} %collective-permute-done.6.refs_7_), channel_id=1, source_target_pairs={{0,32},{32,64},{64,96},{96,128},{128,160},{160,192},{192,224},{224... | collective-permute-start | bytes 1572872 | tf_op jit(solution)/shard_map/ppermute | solution.py:139
  111.3 8.6 %copy-start.5 = (f32[128,1024]{1,0:T(8,128)}, f32[128,1024]{1,0:T(8,128)S(1)}, u32[]{:S(2)}) copy-start(f32[128,1024]{1,0:T(8,128)S(1)} %collective-permute-done.9.refs_3_.refs_10_) | copy-start | bytes 1572868
  111.3 17.4 %collective-permute-start.11 = (f32[128,1024]{1,0:T(8,128)S(1)}, f32[128,1024]{1,0:T(8,128)S(1)}, u32[]{:S(2)}, u32[]{:S(2)}) collective-permute-start(f32[128,1024]{1,0:T(8,128)S(1)} %collective-permute-done.9.refs_3_.refs_10_), channel_id=1, source_target_pairs={{0,480},{32,0},{64,32},{96,64},{128,96},{160,128},{192,160},{224,1... | collective-permute-start | bytes 1572872 | tf_op jit(solution)/shard_map/ppermute | solution.py:139
  116.5 3.4 %copy-start.6 = (f32[128,1024]{1,0:T(8,128)}, f32[128,1024]{1,0:T(8,128)S(1)}, u32[]{:S(2)}) copy-start(f32[128,1024]{1,0:T(8,128)S(1)} %collective-permute-done.7.refs_2_.refs_9_) | copy-start | bytes 1572868
  116.5 17.0 %collective-permute-start.10 = (f32[128,1024]{1,0:T(8,128)S(1)}, f32[128,1024]{1,0:T(8,128)}, u32[]{:S(2)}, u32[]{:S(2)}) collective-permute-start(f32[128,1024]{1,0:T(8,128)S(1)} %collective-permute-done.7.refs_2_.refs_9_), channel_id=1, source_target_pairs={{0,32},{32,64},{64,96},{96,128},{128,160},{160,192},{192,224},{224... | collective-permute-start | bytes 1572872 | tf_op jit(solution)/shard_map/ppermute | solution.py:139
  119.9 40.3 %all-to-all-start.4 = ((f32[32,32,256]{2,1,0:T(8,128)}), f32[32,32,256]{2,1,0:T(8,128)S(1)}, u32[]{:S(2)}, u32[]{:S(2)}) async-start(f32[32,32,256]{2,1,0:T(8,128)} %get-tuple-element.14), calls=%async_computation.4 | async-start | bytes 2097152 | tf_op jit(solution)/shard_map/all_to_all | solution.py:134
  128.7 23.9 %copy-start.20 = (f32[128,1024]{1,0:T(8,128)}, f32[128,1024]{1,0:T(8,128)S(1)}, u32[]{:S(2)}) copy-start(f32[128,1024]{1,0:T(8,128)S(1)} %collective-permute-done.11.refs_12_) | copy-start | bytes 1572868
  128.7 15.8 %collective-permute-start.13 = (f32[128,1024]{1,0:T(8,128)S(1)}, f32[128,1024]{1,0:T(8,128)S(1)}, u32[]{:S(2)}, u32[]{:S(2)}) collective-permute-start(f32[128,1024]{1,0:T(8,128)S(1)} %collective-permute-done.11.refs_12_), channel_id=1, source_target_pairs={{0,480},{32,0},{64,32},{96,64},{128,96},{160,128},{192,160},{224,1... | collective-permute-start | bytes 1572872 | tf_op jit(solution)/shard_map/ppermute | solution.py:139
  133.6 16.2 %collective-permute-start.12 = (f32[128,1024]{1,0:T(8,128)}, f32[128,1024]{1,0:T(8,128)S(1)}, u32[]{:S(2)}, u32[]{:S(2)}) collective-permute-start(f32[128,1024]{1,0:T(8,128)} %collective-permute-done.10.refs_11_), channel_id=1, source_target_pairs={{0,32},{32,64},{64,96},{96,128},{128,160},{160,192},{192,224},{224... | collective-permute-start | bytes 1572872 | tf_op jit(solution)/shard_map/ppermute | solution.py:139
  144.4 6.2 %copy-start.17 = (f32[128,1024]{1,0:T(8,128)}, f32[128,1024]{1,0:T(8,128)S(1)}, u32[]{:S(2)}) copy-start(f32[128,1024]{1,0:T(8,128)S(1)} %collective-permute-done.13.refs_14_) | copy-start | bytes 1572868
  144.5 15.0 %collective-permute-start.15 = (f32[64,1024]{1,0:T(8,128)S(1)}, f32[64,1024]{1,0:T(8,128)S(1)}, u32[]{:S(2)}, u32[]{:S(2)}) collective-permute-start(f32[64,1024]{1,0:T(8,128)S(1)} %slice.9), channel_id=1, source_target_pairs={{0,480},{32,0},{64,32},{96,64},{128,96},{160,128},{192,160},{224,1... | collective-permute-start | bytes 786440 | tf_op jit(solution)/shard_map/ppermute | solution.py:139
  149.8 2.7 %copy-start.18 = (f32[128,1024]{1,0:T(8,128)}, f32[128,1024]{1,0:T(8,128)S(1)}, u32[]{:S(2)}) copy-start(f32[128,1024]{1,0:T(8,128)S(1)} %collective-permute-done.12.refs_13_) | copy-start | bytes 1572868
  150.6 9.6 %collective-permute-start.14 = (f32[64,1024]{1,0:T(8,128)}, f32[64,1024]{1,0:T(8,128)S(1)}, u32[]{:S(2)}, u32[]{:S(2)}) collective-permute-start(f32[64,1024]{1,0:T(8,128)} %slice.8), channel_id=1, source_target_pairs={{0,32},{32,64},{64,96},{96,128},{128,160},{160,192},{192,224},{224... | collective-permute-start | bytes 786440 | tf_op jit(solution)/shard_map/ppermute | solution.py:139
  159.5 0.7 copy-start.21
  160.2 0.7 copy-start.22
  160.9 1.0 copy-start.16

commit v3 on v2

v3 whole, which is shorter than its diff:
```python
import functools

import jax
import jax.numpy as jnp
from jax import lax
from jax.experimental import pallas as pl
from jax.experimental.pallas import tpu as pltpu
from jax.sharding import PartitionSpec as P

F32 = jnp.float32
BF16 = jnp.bfloat16
VMEM_LIMIT = 20 * 1024 * 1024
UPDATE_LIMIT = 56 * 1024 * 1024


def split(a):
    high = a.astype(BF16)
    return high, (a - high.astype(F32)).astype(BF16)


def dot(a, b):
    return lax.dot_general(a, b, (((1,), (0,)), ((), ())), preferred_element_type=F32)


def product(a, b):
    a_high, a_low = split(a)
    b_high, b_low = split(b)
    return dot(a_high, b_high) + (dot(a_high, b_low) + dot(a_low, b_high))


def call(kernel, shapes, args, after=(), scratch=()):
    vmem = pl.BlockSpec(memory_space=pltpu.VMEM)
    smem = pl.BlockSpec(memory_space=pltpu.SMEM)

    def body(*refs):
        kernel(*refs[: len(args)], *refs[len(args) + len(after) :])

    return pl.pallas_call(
        body,
        out_shape=[jax.ShapeDtypeStruct(s, F32) for s in shapes],
        in_specs=[smem if a.dtype == jnp.int32 else vmem for a in args] + [pl.BlockSpec(memory_space=pl.ANY)] * len(after),
        out_specs=[vmem] * len(shapes),
        scratch_shapes=[pltpu.VMEM(s, F32) for s in scratch],
        compiler_params=pltpu.CompilerParams(vmem_limit_bytes=VMEM_LIMIT),
        name=kernel.__name__,
    )(*args, *after)


def copy_out(copies_ref, block):
    for i in range(copies_ref.shape[0]):
        copies_ref[i] = block


def begin(across_ref, copies_ref):
    half = across_ref.shape[0] // 2
    copy_out(copies_ref, jnp.concatenate([across_ref[:half, :], across_ref[half:, :]], axis=1))


def join(rows_b_ref, rows_a_ref, own_ref):
    lines = rows_b_ref.shape[0]
    own_ref[:lines, :] = rows_b_ref[...]
    own_ref[lines:, :] = rows_a_ref[...]


def send(block_ref, copies_ref):
    copy_out(copies_ref, block_ref[...])


def merge(core, same, other, whole_ref):
    whole_ref[:, pl.ds(core, 1)] = same[...][:, None]
    whole_ref[:, pl.ds(1 - core, 1)] = other[...][:, None]
    chips, cores, shard, width = whole_ref.shape
    return whole_ref[...].reshape(chips * cores * shard, width)


def solve(core_ref, inverse_ref, same_ref, other_ref, x_ref, copies_ref, whole_ref):
    x = product(inverse_ref[...], merge(core_ref[0], same_ref, other_ref, whole_ref))
    x_ref[...] = x
    copy_out(copies_ref, x)


def couple(core_ref, rhs_ref, across_ref, same_ref, other_ref, copies_ref, whole_ref):
    planes, _, lanes = across_ref.shape
    lines = lanes // 2
    parts = [across_ref[z] for z in range(planes)]
    parts = [jnp.concatenate([p[:, :lines], p[:, lines:]], axis=0) for p in parts]
    x = merge(core_ref[0], same_ref, other_ref, whole_ref)
    copy_out(copies_ref, rhs_ref[...] - product(jnp.concatenate(parts, axis=1), x))


def gather_x(refs, place, core, out_ref, at):
    for same, other in refs:
        shard = same.shape[-2]
        out_ref[pl.ds(pl.multiple_of(at + core * shard, shard), shard), :] = same[place]
        out_ref[pl.ds(pl.multiple_of(at + (1 - core) * shard, shard), shard), :] = other[place]
        at += 2 * shard


def near_kernel(planes, offsets, plane_ref, core_ref, b_same, b_other, a_same, a_other, rhs_ref, *refs):
    count = len(offsets)
    row_refs, (out_ref, x_ref, rows_ref, total_ref, semaphores) = refs[:count], refs[count:]
    block = rows_ref.shape[1]
    copies = [pltpu.make_async_copy(r, rows_ref.at[n], semaphores.at[n]) for n, r in enumerate(row_refs)]
    for copy in copies:
        copy.start()
    for n, offset in enumerate(offsets):
        place = lax.rem(plane_ref[0] + offset, planes)
        gather_x(((b_same, b_other), (a_same, a_other)), place, core_ref[0], x_ref, n * block)
    for n in range(0, count, 2):
        last = min(n + 2, count)
        for copy in copies[n:last]:
            copy.wait()
        rows = rows_ref[n:last].reshape((last - n) * block, rows_ref.shape[2])
        part = product(x_ref[n * block : last * block].T, rows)
        total_ref[...] = part if n == 0 else total_ref[...] + part
    out_ref[...] = rhs_ref[...] - total_ref[...].T


def update_near(plane, core, x, rhs, blocks, offsets, planes):
    height, width = rhs.shape
    vmem, smem = pl.BlockSpec(memory_space=pltpu.VMEM), pl.BlockSpec(memory_space=pltpu.SMEM)
    count, block = len(blocks), blocks[0].shape[0]
    return pl.pallas_call(
        functools.partial(near_kernel, planes, offsets),
        out_shape=jax.ShapeDtypeStruct((height, width), F32),
        in_specs=[smem] * 2 + [vmem] * (len(x) + 1) + [pl.BlockSpec(memory_space=pl.ANY)] * count,
        out_specs=vmem,
        scratch_shapes=[
            pltpu.VMEM((count * block, width), F32),
            pltpu.VMEM((count, block, height), F32),
            pltpu.VMEM((width, height), F32),
            pltpu.SemaphoreType.DMA((count,)),
        ],
        compiler_params=pltpu.CompilerParams(vmem_limit_bytes=UPDATE_LIMIT),
        name="update_near",
    )(plane, core, *x, rhs, *blocks)


def far_kernel(planes, plane_ref, core_ref, b_same, b_other, a_same, a_other, rhs_ref, rows_b_ref, rows_a_ref, out_ref, x_ref):
    place = lax.rem(plane_ref[0] + planes // 2, planes)
    gather_x(((b_same, b_other), (a_same, a_other)), place, core_ref[0], x_ref, 0)
    rows = jnp.concatenate([rows_b_ref[...], rows_a_ref[...]], axis=0)
    out_ref[...] = rhs_ref[...] - product(x_ref[...].T, rows).T


def update_far(plane, core, x, rhs, blocks, planes):
    height, width = rhs.shape
    tile = 512
    smem = pl.BlockSpec(memory_space=pltpu.SMEM)
    out = pl.BlockSpec((tile, width), lambda n: (n, 0))
    return pl.pallas_call(
        functools.partial(far_kernel, planes),
        grid=(height // tile,),
        out_shape=jax.ShapeDtypeStruct((height, width), F32),
        in_specs=[smem] * 2
        + [pl.BlockSpec(a.shape, lambda n: (0, 0, 0)) for a in x]
        + [out]
        + [pl.BlockSpec((b.shape[0], tile), lambda n: (0, n)) for b in blocks],
        out_specs=out,
        scratch_shapes=[pltpu.VMEM((sum(b.shape[0] for b in blocks), width), F32)],
        compiler_params=pltpu.CompilerParams(vmem_limit_bytes=VMEM_LIMIT),
        name="update_far",
    )(plane, core, *x, rhs, *blocks)


def exchange(copies, axis):
    return lax.all_to_all(copies, axis, 0, 0, tiled=True)


def spread(copies):
    same = exchange(copies, "chip")
    return same, lax.ppermute(same, "core", [(0, 1), (1, 0)])


def ring(own, planes):
    def move(block, by):
        return lax.ppermute(block, "row", [(i, (i + by) % planes) for i in range(planes)])

    up = down = own
    blocks, offsets = [own], [0]
    half = planes // 2
    for step in range(1, half):
        up, down = move(up, 1), move(down, -1)
        blocks += [up, down]
        offsets += [planes - step, step]
    middle = own.shape[0] // 2
    blocks += [move(up[:middle], 1), move(down[middle:], -1)]
    offsets += [half]
    return blocks, tuple(offsets)


def make(planes, chips):
    def shards(rhs_above, rhs_a, rhs_b, rows_a_above, rows_b_above, rows_b_a, inverse_a, inverse_b):
        shard, width = rhs_b.shape
        lines, height = rows_b_above.shape
        plane, core = (lax.axis_index(a).astype(jnp.int32).reshape(1) for a in ("row", "core"))
        local, copies, whole = (shard, width), (chips, shard, width), (chips, 2, shard, width)

        (across_copies,) = call(begin, [(planes, shard // 2, 2 * lines)], [rows_b_a.T])
        across = exchange(across_copies, "row")
        (own,) = call(join, [(2 * lines, height)], [rows_b_above, rows_a_above])
        blocks, offsets = ring(own, planes)
        (rhs_copies,) = call(send, [copies], [rhs_b])
        x_b, x_copies = call(
            solve, [local, copies], [core, inverse_b.T, *spread(rhs_copies)], after=blocks[1:3] + [across], scratch=[whole]
        )
        x_b_all = spread(x_copies)
        (coupled,) = call(
            couple, [copies], [core, rhs_a, across, *x_b_all], after=blocks[5:7], scratch=[whole]
        )
        x_a, x_copies = call(
            solve, [local, copies], [core, inverse_a.T, *spread(coupled)], after=blocks[9:11], scratch=[whole]
        )
        x = x_b_all + spread(x_copies)
        partial = update_near(plane, core, x, rhs_above, blocks[:-2], offsets[:-1], planes)
        return x_b, x_a, update_far(plane, core, x, partial, blocks[-2:], planes)

    return shards


def solution(mesh):
    planes, columns = mesh.shape["row"], mesh.shape["col"]
    mesh = jax.sharding.Mesh(mesh.devices.reshape(planes, columns // 2, 2), ("row", "chip", "core"))
    column = ("chip", "core")
    in_specs = (
        P(column, "row"),
        P(column, "row"),
        P(column, "row"),
        P("row", column),
        P("row", column),
        P("row", column),
        P(None, column),
        P(None, column),
    )
    out_specs = (P(column, "row"), P(column, "row"), P(column, "row"))
    return jax.shard_map(
        make(planes, columns // 2), mesh=mesh, in_specs=in_specs, out_specs=out_specs, check_vma=False
    )
```

time: 171 us -> 157 us (0.918)
  waiting for transfers between devices: 37.3 us -> 22.6 us
  starting transfers between devices: 106 us -> 110 us
  Pallas kernels: 19.8 us -> 16.2 us
    ppermute x0 -> x4, starting transfers between devices: none -> 19.7 us  [spread(): return (same, lax.ppermute(same, 'core', [(0, 1), (1, 0)]))]
    all_to_all x5, starting transfers between devices: 47.9 us -> 31.7 us  [exchange(): return lax.all_to_all(copies, axis, 0, 0, tiled=True)]
    ppermute x16, waiting for transfers between devices: 28.3 us -> 15.7 us  [move(): lax.ppermute(block, 'row', [(i, (i + by) % planes) for i in range(planes)])]
    pallas_call x7 -> x8, Pallas kernels: 19.8 us -> 16.2 us  [the longest x1 8.69 us: update_near(): pl.pallas_call(functools.partial(near_kernel, planes, offsets), out_shape...]
    all_to_all x5, waiting for transfers between devices: 8.95 us -> 6.87 us  [exchange(): return lax.all_to_all(copies, axis, 0, 0, tiled=True)]
    unnamed x46 -> x54, local copies, waits for them, and re-layouts: 3.44 us -> 3.89 us
  transfers between devices with their start and end apart: 21 -> 25, of which waited for: 7 -> 7; matrix products, arithmetic and copies ran while one was open for 0% -> 0% of each run, Pallas kernels for 7% -> 9%
where the time goes in v3:
time: 157 us; the launch traced here: 154 us
  starting transfers between devices  110 us (70%)
  waiting for transfers between devices  22.6 us (14%)
  Pallas kernels  16.2 us (10%)
  local copies, waits for them, and re-layouts  4.66 us (3%)
    ppermute x16, starting transfers between devices, move(): lax.ppermute(block, 'row', [(i, (i + by) % planes) for i in range(planes)])  58.4 us
    all_to_all x5, starting transfers between devices, exchange(): return lax.all_to_all(copies, axis, 0, 0, tiled=True)  31.7 us
    ppermute x4, starting transfers between devices, spread(): return (same, lax.ppermute(same, 'core', [(0, 1), (1, 0)]))  19.7 us
    ppermute x16, waiting for transfers between devices, move(): lax.ppermute(block, 'row', [(i, (i + by) % planes) for i in range(planes)])  15.7 us
    pallas_call x1, Pallas kernels, update_near(): pl.pallas_call(functools.partial(near_kernel, planes, offsets), out_shape...  8.69 us
    all_to_all x5, waiting for transfers between devices, exchange(): return lax.all_to_all(copies, axis, 0, 0, tiled=True)  6.87 us
    pallas_call x6, Pallas kernels, call(): pl.pallas_call(body, out_shape=[jax.ShapeDtypeStruct(s, F32) for s in sha...  5.48 us
    unnamed x54, local copies, waits for them, and re-layouts  3.89 us
  transfers between devices with their start and end apart: 25, of which 7 were waited for; matrix products, arithmetic and copies ran while one was open for 0% of the time, Pallas kernels for 9%

profile of v3, /device:TPU:1, one launch (start us, length us, event | category | flops | bytes accessed | tf_op | source)
XLA Modules:
  0.0 154.5 jit_solution(15536166510138233657)
XLA Ops:
  0.6 0.7 copy-done.21
  1.4 0.8 send.1
  2.2 7.7 %all-to-all-start = ((f32[16,32,256]{2,1,0:T(8,128)}), f32[16,32,256]{2,1,0:T(8,128)S(1)}, u32[]{:S(2)}, u32[]{:S(2)}) async-start(f32[16,32,256]{2,1,0:T(8,128)} %send.1), calls=%async_computation | async-start | bytes 1048576 | tf_op jit(solution)/shard_map/all_to_all | solution.py:167
  10.0 0.0 copy-start.22
  10.0 3.5 %collective-permute-start.1 = (f32[128,1024]{1,0:T(8,128)S(1)}, f32[128,1024]{1,0:T(8,128)S(1)}, u32[]{:S(2)}, u32[]{:S(2)}) collective-permute-start(f32[128,1024]{1,0:T(8,128)S(1)} %join.1.refs_0_), channel_id=1, source_target_pairs={{0,32},{32,64},{64,96},{96,128},{128,160},{160,192},{192,224},{224... | collective-permute-start | bytes 1572872 | tf_op jit(solution)/shard_map/ppermute | solution.py:177
  13.6 9.5 %collective-permute-start.2 = (f32[128,1024]{1,0:T(8,128)S(1)}, f32[128,1024]{1,0:T(8,128)S(1)}, u32[]{:S(2)}, u32[]{:S(2)}) collective-permute-start(f32[128,1024]{1,0:T(8,128)S(1)} %join.1.refs_0_), channel_id=1, source_target_pairs={{0,480},{32,0},{64,32},{96,64},{128,96},{160,128},{192,160},{224,1... | collective-permute-start | bytes 1572872 | tf_op jit(solution)/shard_map/ppermute | solution.py:177
  23.1 0.0 all-to-all-done.refs_2_
  23.1 3.1 %collective-permute-start = (f32[16,32,256]{2,1,0:T(8,128)S(1)}, f32[16,32,256]{2,1,0:T(8,128)S(1)}, u32[]{:S(2)}, u32[]{:S(2)}) collective-permute-start(f32[16,32,256]{2,1,0:T(8,128)S(1)} %all-to-all-done.refs_2_), channel_id=1, source_target_pairs={{0,1},{1,0},{2,3},{3,2},{4,5},{5,4},{6,7},{7,6},{8,9},{9,8},{10,11... | collective-permute-start | bytes 1572872 | tf_op jit(solution)/shard_map/ppermute | solution.py:172
  26.3 0.7 begin.1
  27.0 13.1 %all-to-all-start.1 = ((f32[16,16,128]{2,1,0:T(8,128)}), f32[16,16,128]{2,1,0:T(8,128)S(1)}, u32[]{:S(2)}, u32[]{:S(2)}) async-start(f32[16,16,128]{2,1,0:T(8,128)} %begin.1), calls=%async_computation.1 | async-start | bytes 262144 | tf_op jit(solution)/shard_map/all_to_all | solution.py:167
  40.2 0.0 collective-permute-done.1.refs_4_.refs_1_
  40.2 3.3 %collective-permute-start.4 = (f32[128,1024]{1,0:T(8,128)S(1)}, f32[128,1024]{1,0:T(8,128)S(1)}, u32[]{:S(2)}, u32[]{:S(2)}) collective-permute-start(f32[128,1024]{1,0:T(8,128)S(1)} %collective-permute-done.1.refs_4_.refs_1_), channel_id=1, source_target_pairs={{0,32},{32,64},{64,96},{96,128},{128,160},{160,192},{192,224},{224... | collective-permute-start | bytes 1572872 | tf_op jit(solution)/shard_map/ppermute | solution.py:177
  43.5 0.0 collective-permute-done.2.refs_5_.refs_2_
  43.5 3.2 %collective-permute-start.6 = (f32[128,1024]{1,0:T(8,128)S(1)}, f32[128,1024]{1,0:T(8,128)}, u32[]{:S(2)}, u32[]{:S(2)}) collective-permute-start(f32[128,1024]{1,0:T(8,128)S(1)} %collective-permute-done.2.refs_5_.refs_2_), channel_id=1, source_target_pairs={{0,480},{32,0},{64,32},{96,64},{128,96},{160,128},{192,160},{224,1... | collective-permute-start | bytes 1572872 | tf_op jit(solution)/shard_map/ppermute | solution.py:177
  46.7 5.9 %all-to-all-done.1.refs_6_.refs_2_ = f32[16,16,128]{2,1,0:T(8,128)S(1)} async-done(((f32[16,16,128]{2,1,0:T(8,128)}), f32[16,16,128]{2,1,0:T(8,128)S(1)}, u32[]{:S(2)}, u32[]{:S(2)}) %all-to-all-start.1) | async-done | bytes 131104 | tf_op jit(solution)/shard_map/all_to_all | solution.py:167
  52.6 0.0 collective-permute-done.refs_3_
  52.6 1.3 solve.2
  53.9 0.0 copy-start.20
  53.9 3.6 %all-to-all-start.2 = ((f32[16,32,256]{2,1,0:T(8,128)}), f32[16,32,256]{2,1,0:T(8,128)S(1)}, u32[]{:S(2)}, u32[]{:S(2)}) async-start(f32[16,32,256]{2,1,0:T(8,128)} %get-tuple-element.8), calls=%async_computation.2 | async-start | bytes 1048576 | tf_op jit(solution)/shard_map/all_to_all | solution.py:167
  57.5 3.3 %collective-permute-done.4.refs_3_ = f32[128,1024]{1,0:T(8,128)S(1)} collective-permute-done((f32[128,1024]{1,0:T(8,128)S(1)}, f32[128,1024]{1,0:T(8,128)S(1)}, u32[]{:S(2)}, u32[]{:S(2)}) %collective-permute-start.4) | collective-permute-done | bytes 524320 | tf_op jit(solution)/shard_map/ppermute | solution.py:177
  60.8 2.0 %collective-permute-start.5 = (f32[128,1024]{1,0:T(8,128)S(1)}, f32[128,1024]{1,0:T(8,128)S(1)}, u32[]{:S(2)}, u32[]{:S(2)}) collective-permute-start(f32[128,1024]{1,0:T(8,128)S(1)} %collective-permute-done.4.refs_3_), channel_id=1, source_target_pairs={{0,32},{32,64},{64,96},{96,128},{128,160},{160,192},{192,224},{224... | collective-permute-start | bytes 1572872 | tf_op jit(solution)/shard_map/ppermute | solution.py:177
  62.9 0.0 collective-permute-done.6.refs_4_
  62.9 4.5 %collective-permute-start.7 = (f32[128,1024]{1,0:T(8,128)}, f32[128,1024]{1,0:T(8,128)S(1)}, u32[]{:S(2)}, u32[]{:S(2)}) collective-permute-start(f32[128,1024]{1,0:T(8,128)} %collective-permute-done.6.refs_4_), channel_id=1, source_target_pairs={{0,480},{32,0},{64,32},{96,64},{128,96},{160,128},{192,160},{224,1... | collective-permute-start | bytes 1572872 | tf_op jit(solution)/shard_map/ppermute | solution.py:177
  67.4 0.0 all-to-all-done.2.refs_3_.b_same
  67.4 4.7 %collective-permute-start.3 = (f32[16,32,256]{2,1,0:T(8,128)S(1)}, f32[16,32,256]{2,1,0:T(8,128)S(1)}, u32[]{:S(2)}, u32[]{:S(2)}) collective-permute-start(f32[16,32,256]{2,1,0:T(8,128)S(1)} %all-to-all-done.2.refs_3_.b_same), channel_id=1, source_target_pairs={{0,1},{1,0},{2,3},{3,2},{4,5},{5,4},{6,7},{7,6},{8,9},{9,8},{10,11... | collective-permute-start | bytes 1572872 | tf_op jit(solution)/shard_map/ppermute | solution.py:172
  72.0 4.6 %collective-permute-done.5.refs_5_ = f32[128,1024]{1,0:T(8,128)S(1)} collective-permute-done((f32[128,1024]{1,0:T(8,128)S(1)}, f32[128,1024]{1,0:T(8,128)S(1)}, u32[]{:S(2)}, u32[]{:S(2)}) %collective-permute-start.5) | collective-permute-done | bytes 524320 | tf_op jit(solution)/shard_map/ppermute | solution.py:177
  76.7 1.9 %collective-permute-start.9 = (f32[128,1024]{1,0:T(8,128)S(1)}, f32[128,1024]{1,0:T(8,128)}, u32[]{:S(2)}, u32[]{:S(2)}) collective-permute-start(f32[128,1024]{1,0:T(8,128)S(1)} %collective-permute-done.5.refs_5_), channel_id=1, source_target_pairs={{0,32},{32,64},{64,96},{96,128},{128,160},{160,192},{192,224},{224... | collective-permute-start | bytes 1572872 | tf_op jit(solution)/shard_map/ppermute | solution.py:177
  78.6 0.0 collective-permute-done.7.refs_6_
  78.6 4.6 %collective-permute-start.11 = (f32[128,1024]{1,0:T(8,128)S(1)}, f32[128,1024]{1,0:T(8,128)}, u32[]{:S(2)}, u32[]{:S(2)}) collective-permute-start(f32[128,1024]{1,0:T(8,128)S(1)} %collective-permute-done.7.refs_6_), channel_id=1, source_target_pairs={{0,480},{32,0},{64,32},{96,64},{128,96},{160,128},{192,160},{224,1... | collective-permute-start | bytes 1572872 | tf_op jit(solution)/shard_map/ppermute | solution.py:177
  83.2 0.0 collective-permute-done.3.refs_4_.b_other
  83.2 1.3 couple.1
  84.5 0.0 copy-start.19
  84.6 3.7 %all-to-all-start.3 = ((f32[16,32,256]{2,1,0:T(8,128)}), f32[16,32,256]{2,1,0:T(8,128)S(1)}, u32[]{:S(2)}, u32[]{:S(2)}) async-start(f32[16,32,256]{2,1,0:T(8,128)} %couple.1), calls=%async_computation.3 | async-start | bytes 1048576 | tf_op jit(solution)/shard_map/all_to_all | solution.py:167
  88.3 3.4 %collective-permute-done.9.refs_7_ = f32[128,1024]{1,0:T(8,128)} collective-permute-done((f32[128,1024]{1,0:T(8,128)S(1)}, f32[128,1024]{1,0:T(8,128)}, u32[]{:S(2)}, u32[]{:S(2)}) %collective-permute-start.9) | collective-permute-done | bytes 524320 | tf_op jit(solution)/shard_map/ppermute | solution.py:177
  91.7 1.9 %collective-permute-start.10 = (f32[128,1024]{1,0:T(8,128)}, f32[128,1024]{1,0:T(8,128)S(1)}, u32[]{:S(2)}, u32[]{:S(2)}) collective-permute-start(f32[128,1024]{1,0:T(8,128)} %collective-permute-done.9.refs_7_), channel_id=1, source_target_pairs={{0,32},{32,64},{64,96},{96,128},{128,160},{160,192},{192,224},{224... | collective-permute-start | bytes 1572872 | tf_op jit(solution)/shard_map/ppermute | solution.py:177
  93.6 0.0 collective-permute-done.11.refs_8_
  93.6 4.6 %collective-permute-start.12 = (f32[128,1024]{1,0:T(8,128)}, f32[128,1024]{1,0:T(8,128)S(1)}, u32[]{:S(2)}, u32[]{:S(2)}) collective-permute-start(f32[128,1024]{1,0:T(8,128)} %collective-permute-done.11.refs_8_), channel_id=1, source_target_pairs={{0,480},{32,0},{64,32},{96,64},{128,96},{160,128},{192,160},{224,1... | collective-permute-start | bytes 1572872 | tf_op jit(solution)/shard_map/ppermute | solution.py:177
  98.2 0.0 all-to-all-done.3.refs_2_
  98.2 5.0 %collective-permute-start.8 = (f32[16,32,256]{2,1,0:T(8,128)S(1)}, f32[16,32,256]{2,1,0:T(8,128)S(1)}, u32[]{:S(2)}, u32[]{:S(2)}) collective-permute-start(f32[16,32,256]{2,1,0:T(8,128)S(1)} %all-to-all-done.3.refs_2_), channel_id=1, source_target_pairs={{0,1},{1,0},{2,3},{3,2},{4,5},{5,4},{6,7},{7,6},{8,9},{9,8},{10,11... | collective-permute-start | bytes 1572872 | tf_op jit(solution)/shard_map/ppermute | solution.py:172
  103.2 2.7 %collective-permute-done.10.refs_4_.refs_9_ = f32[128,1024]{1,0:T(8,128)S(1)} collective-permute-done((f32[128,1024]{1,0:T(8,128)}, f32[128,1024]{1,0:T(8,128)S(1)}, u32[]{:S(2)}, u32[]{:S(2)}) %collective-permute-start.10) | collective-permute-done | bytes 524320 | tf_op jit(solution)/shard_map/ppermute | solution.py:177
  105.9 1.9 %collective-permute-start.14 = (f32[128,1024]{1,0:T(8,128)S(1)}, f32[128,1024]{1,0:T(8,128)S(1)}, u32[]{:S(2)}, u32[]{:S(2)}) collective-permute-start(f32[128,1024]{1,0:T(8,128)S(1)} %collective-permute-done.10.refs_4_.refs_9_), channel_id=1, source_target_pairs={{0,32},{32,64},{64,96},{96,128},{128,160},{160,192},{192,224},{224... | collective-permute-start | bytes 1572872 | tf_op jit(solution)/shard_map/ppermute | solution.py:177
  107.8 4.6 %collective-permute-start.15 = (f32[128,1024]{1,0:T(8,128)S(1)}, f32[128,1024]{1,0:T(8,128)}, u32[]{:S(2)}, u32[]{:S(2)}) collective-permute-start(f32[128,1024]{1,0:T(8,128)S(1)} %collective-permute-done.12.refs_5_.refs_10_), channel_id=1, source_target_pairs={{0,480},{32,0},{64,32},{96,64},{128,96},{160,128},{192,160},{224,1... | collective-permute-start | bytes 1572872 | tf_op jit(solution)/shard_map/ppermute | solution.py:177
  112.4 0.0 collective-permute-done.8.refs_3_
  112.4 1.3 solve.3
  113.7 3.6 %all-to-all-start.4 = ((f32[16,32,256]{2,1,0:T(8,128)}), f32[16,32,256]{2,1,0:T(8,128)S(1)}, u32[]{:S(2)}, u32[]{:S(2)}) async-start(f32[16,32,256]{2,1,0:T(8,128)} %get-tuple-element.10), calls=%async_computation.4 | async-start | bytes 1048576 | tf_op jit(solution)/shard_map/all_to_all | solution.py:167
  117.3 1.6 %collective-permute-done.14.refs_11_ = f32[128,1024]{1,0:T(8,128)S(1)} collective-permute-done((f32[128,1024]{1,0:T(8,128)S(1)}, f32[128,1024]{1,0:T(8,128)S(1)}, u32[]{:S(2)}, u32[]{:S(2)}) %collective-permute-start.14) | collective-permute-done | bytes 524320 | tf_op jit(solution)/shard_map/ppermute | solution.py:177
  118.9 1.9 %collective-permute-start.16 = (f32[128,1024]{1,0:T(8,128)S(1)}, f32[128,1024]{1,0:T(8,128)S(1)}, u32[]{:S(2)}, u32[]{:S(2)}) collective-permute-start(f32[128,1024]{1,0:T(8,128)S(1)} %collective-permute-done.14.refs_11_), channel_id=1, source_target_pairs={{0,32},{32,64},{64,96},{96,128},{128,160},{160,192},{192,224},{224... | collective-permute-start | bytes 1572872 | tf_op jit(solution)/shard_map/ppermute | solution.py:177
  120.9 0.0 collective-permute-done.15.refs_12_
  120.9 4.6 %collective-permute-start.17 = (f32[128,1024]{1,0:T(8,128)}, f32[128,1024]{1,0:T(8,128)S(1)}, u32[]{:S(2)}, u32[]{:S(2)}) collective-permute-start(f32[128,1024]{1,0:T(8,128)} %collective-permute-done.15.refs_12_), channel_id=1, source_target_pairs={{0,480},{32,0},{64,32},{96,64},{128,96},{160,128},{192,160},{224,1... | collective-permute-start | bytes 1572872 | tf_op jit(solution)/shard_map/ppermute | solution.py:177
  125.4 1.0 all-to-all-done.4.a_same
  126.4 6.9 %collective-permute-start.13 = (f32[16,32,256]{2,1,0:T(8,128)S(1)}, f32[16,32,256]{2,1,0:T(8,128)S(1)}, u32[]{:S(2)}, u32[]{:S(2)}) collective-permute-start(f32[16,32,256]{2,1,0:T(8,128)S(1)} %all-to-all-done.4.a_same), channel_id=1, source_target_pairs={{0,1},{1,0},{2,3},{3,2},{4,5},{5,4},{6,7},{7,6},{8,9},{9,8},{10,11... | collective-permute-start | bytes 1572872 | tf_op jit(solution)/shard_map/ppermute | solution.py:172
  133.3 0.0 collective-permute-done.16.refs_13_
  133.4 1.9 %collective-permute-start.18 = (f32[64,1024]{1,0:T(8,128)S(1)}, f32[64,1024]{1,0:T(8,128)S(1)}, u32[]{:S(2)}, u32[]{:S(2)}) collective-permute-start(f32[64,1024]{1,0:T(8,128)S(1)} %slice.8), channel_id=1, source_target_pairs={{0,32},{32,64},{64,96},{96,128},{128,160},{160,192},{192,224},{224... | collective-permute-start | bytes 786440 | tf_op jit(solution)/shard_map/ppermute | solution.py:177
  135.3 0.8 slice.9
  136.1 4.6 %collective-permute-start.19 = (f32[64,1024]{1,0:T(8,128)}, f32[64,1024]{1,0:T(8,128)S(1)}, u32[]{:S(2)}, u32[]{:S(2)}) collective-permute-start(f32[64,1024]{1,0:T(8,128)} %slice.9), channel_id=1, source_target_pairs={{0,480},{32,0},{64,32},{96,64},{128,96},{160,128},{192,160},{224,1... | collective-permute-start | bytes 786440 | tf_op jit(solution)/shard_map/ppermute | solution.py:177
  140.6 0.0 collective-permute-done.13.a_other
  140.7 0.8 copy-done.11
  141.5 8.7 %update_near.1.rhs_ref = f32[1024,256]{1,0:T(8,128)} custom-call(s32[1]{0:T(128)} %bitcast.4.plane_ref, s32[1]{0:T(128)} %bitcast.refs_0_.core_ref, f32[16,32,256]{2,1,0:T(8,128)} %copy-done, f32[16,32,256]{2,1,0:T(8,128)} %copy-done.4, f32[16,32,256]{2,1,0:T(8,128)} %copy-done.2, f32[16,32,256]{2,1,0:T(8,128)} %copy-done.11, f32[1024,256]{1,0:T(8,128)} %rhs_ref.1, ...), custom_call_target="tpu_custom_call" | custom-call | tf_op jit(solution)/shard_map/update_near/pallas_call | solution.py:123
  150.2 0.0 collective-permute-done.18.rows_b_ref
  150.2 0.0 collective-permute-done.19.rows_a_ref
  150.2 0.0 copy-start.6
  150.2 1.2 copy-done.6
  151.4 1.0 copy-done.12
  152.5 2.0 %update_far.1 = f32[1024,256]{1,0:T(8,128)} custom-call(s32[1]{0:T(128)} %bitcast.4.plane_ref, s32[1]{0:T(128)} %bitcast.refs_0_.core_ref, f32[16,32,256]{2,1,0:T(8,128)S(1)} %copy-done.1, f32[16,32,256]{2,1,0:T(8,128)S(1)} %copy-done.5, f32[16,32,256]{2,1,0:T(8,128)S(1)} %copy-done.3, f32[16,32,256]{2,1,0:T(8,128)S(1)} %copy-done.12, ...), custom_call_target="tpu_custom_call" | custom-call | tf_op jit(solution)/shard_map/update_far/pallas_call | solution.py:151
  (50 shorter events, 0.2 us)
Async XLA Ops:
  0.6 0.8 copy-start.21
  2.2 7.7 %copy-start.16 = (f32[64,1024]{1,0:T(8,128)S(1)}, f32[64,1024]{1,0:T(8,128)}, u32[]{:S(2)}) copy-start(f32[64,1024]{1,0:T(8,128)} %refs_0_.3) | copy-start | bytes 786436
  2.2 7.7 %copy-start.17 = (f32[64,1024]{1,0:T(8,128)S(1)}, f32[64,1024]{1,0:T(8,128)}, u32[]{:S(2)}) copy-start(f32[64,1024]{1,0:T(8,128)} %refs_1_.2) | copy-start | bytes 786436
  2.2 20.9 %all-to-all-start = ((f32[16,32,256]{2,1,0:T(8,128)}), f32[16,32,256]{2,1,0:T(8,128)S(1)}, u32[]{:S(2)}, u32[]{:S(2)}) async-start(f32[16,32,256]{2,1,0:T(8,128)} %send.1), calls=%async_computation | async-start | bytes 1048576 | tf_op jit(solution)/shard_map/all_to_all | solution.py:167
  10.0 16.3 %copy-start.22 = (f32[64,32]{0,1:T(8,128)S(1)}, f32[64,32]{0,1:T(8,128)}, u32[]{:S(2)}) copy-start(f32[64,32]{0,1:T(8,128)} %param.13) | copy-start | bytes 24580
  10.0 43.9 %copy-start.13 = (f32[128,1024]{1,0:T(8,128)}, f32[128,1024]{1,0:T(8,128)S(1)}, u32[]{:S(2)}) copy-start(f32[128,1024]{1,0:T(8,128)S(1)} %join.1.refs_0_) | copy-start | bytes 1572868
  10.0 30.1 %collective-permute-start.1 = (f32[128,1024]{1,0:T(8,128)S(1)}, f32[128,1024]{1,0:T(8,128)S(1)}, u32[]{:S(2)}, u32[]{:S(2)}) collective-permute-start(f32[128,1024]{1,0:T(8,128)S(1)} %join.1.refs_0_), channel_id=1, source_target_pairs={{0,32},{32,64},{64,96},{96,128},{128,160},{160,192},{192,224},{224... | collective-permute-start | bytes 1572872 | tf_op jit(solution)/shard_map/ppermute | solution.py:177
  13.6 29.9 %collective-permute-start.2 = (f32[128,1024]{1,0:T(8,128)S(1)}, f32[128,1024]{1,0:T(8,128)S(1)}, u32[]{:S(2)}, u32[]{:S(2)}) collective-permute-start(f32[128,1024]{1,0:T(8,128)S(1)} %join.1.refs_0_), channel_id=1, source_target_pairs={{0,480},{32,0},{64,32},{96,64},{128,96},{160,128},{192,160},{224,1... | collective-permute-start | bytes 1572872 | tf_op jit(solution)/shard_map/ppermute | solution.py:177
  23.1 29.5 %collective-permute-start = (f32[16,32,256]{2,1,0:T(8,128)S(1)}, f32[16,32,256]{2,1,0:T(8,128)S(1)}, u32[]{:S(2)}, u32[]{:S(2)}) collective-permute-start(f32[16,32,256]{2,1,0:T(8,128)S(1)} %all-to-all-done.refs_2_), channel_id=1, source_target_pairs={{0,1},{1,0},{2,3},{3,2},{4,5},{5,4},{6,7},{7,6},{8,9},{9,8},{10,11... | collective-permute-start | bytes 1572872 | tf_op jit(solution)/shard_map/ppermute | solution.py:172
  27.0 25.6 %copy-start.18 = (f32[1024,32]{0,1:T(8,128)S(1)}, f32[1024,32]{0,1:T(8,128)}, u32[]{:S(2)}) copy-start(f32[1024,32]{0,1:T(8,128)} %param.15) | copy-start | bytes 393220
  27.0 25.6 %all-to-all-start.1 = ((f32[16,16,128]{2,1,0:T(8,128)}), f32[16,16,128]{2,1,0:T(8,128)S(1)}, u32[]{:S(2)}, u32[]{:S(2)}) async-start(f32[16,16,128]{2,1,0:T(8,128)} %begin.1), calls=%async_computation.1 | async-start | bytes 262144 | tf_op jit(solution)/shard_map/all_to_all | solution.py:167
  40.2 13.7 %copy-start.7 = (f32[128,1024]{1,0:T(8,128)}, f32[128,1024]{1,0:T(8,128)S(1)}, u32[]{:S(2)}) copy-start(f32[128,1024]{1,0:T(8,128)S(1)} %collective-permute-done.1.refs_4_.refs_1_) | copy-start | bytes 1572868
  40.2 20.7 %collective-permute-start.4 = (f32[128,1024]{1,0:T(8,128)S(1)}, f32[128,1024]{1,0:T(8,128)S(1)}, u32[]{:S(2)}, u32[]{:S(2)}) collective-permute-start(f32[128,1024]{1,0:T(8,128)S(1)} %collective-permute-done.1.refs_4_.refs_1_), channel_id=1, source_target_pairs={{0,32},{32,64},{64,96},{96,128},{128,160},{160,192},{192,224},{224... | collective-permute-start | bytes 1572872 | tf_op jit(solution)/shard_map/ppermute | solution.py:177
  43.5 10.4 %copy-start.8 = (f32[128,1024]{1,0:T(8,128)}, f32[128,1024]{1,0:T(8,128)S(1)}, u32[]{:S(2)}) copy-start(f32[128,1024]{1,0:T(8,128)S(1)} %collective-permute-done.2.refs_5_.refs_2_) | copy-start | bytes 1572868
  43.5 19.4 %collective-permute-start.6 = (f32[128,1024]{1,0:T(8,128)S(1)}, f32[128,1024]{1,0:T(8,128)}, u32[]{:S(2)}, u32[]{:S(2)}) collective-permute-start(f32[128,1024]{1,0:T(8,128)S(1)} %collective-permute-done.2.refs_5_.refs_2_), channel_id=1, source_target_pairs={{0,480},{32,0},{64,32},{96,64},{128,96},{160,128},{192,160},{224,1... | collective-permute-start | bytes 1572872 | tf_op jit(solution)/shard_map/ppermute | solution.py:177
  53.9 29.3 %copy-start.20 = (f32[32,256]{1,0:T(8,128)S(1)}, f32[32,256]{1,0:T(8,128)}, u32[]{:S(2)}) copy-start(f32[32,256]{1,0:T(8,128)} %refs_1_.3) | copy-start | bytes 98308
  53.9 13.4 %all-to-all-start.2 = ((f32[16,32,256]{2,1,0:T(8,128)}), f32[16,32,256]{2,1,0:T(8,128)S(1)}, u32[]{:S(2)}, u32[]{:S(2)}) async-start(f32[16,32,256]{2,1,0:T(8,128)} %get-tuple-element.8), calls=%async_computation.2 | async-start | bytes 1048576 | tf_op jit(solution)/shard_map/all_to_all | solution.py:167
  60.8 23.7 %copy-start.25 = (f32[128,1024]{1,0:T(8,128)}, f32[128,1024]{1,0:T(8,128)S(1)}, u32[]{:S(2)}) copy-start(f32[128,1024]{1,0:T(8,128)S(1)} %collective-permute-done.4.refs_3_) | copy-start | bytes 1572868
  60.8 15.8 %collective-permute-start.5 = (f32[128,1024]{1,0:T(8,128)S(1)}, f32[128,1024]{1,0:T(8,128)S(1)}, u32[]{:S(2)}, u32[]{:S(2)}) collective-permute-start(f32[128,1024]{1,0:T(8,128)S(1)} %collective-permute-done.4.refs_3_), channel_id=1, source_target_pairs={{0,32},{32,64},{64,96},{96,128},{128,160},{160,192},{192,224},{224... | collective-permute-start | bytes 1572872 | tf_op jit(solution)/shard_map/ppermute | solution.py:177
  62.9 15.7 %collective-permute-start.7 = (f32[128,1024]{1,0:T(8,128)}, f32[128,1024]{1,0:T(8,128)S(1)}, u32[]{:S(2)}, u32[]{:S(2)}) collective-permute-start(f32[128,1024]{1,0:T(8,128)} %collective-permute-done.6.refs_4_), channel_id=1, source_target_pairs={{0,480},{32,0},{64,32},{96,64},{128,96},{160,128},{192,160},{224,1... | collective-permute-start | bytes 1572872 | tf_op jit(solution)/shard_map/ppermute | solution.py:177
  67.4 17.2 %copy-start = (f32[16,32,256]{2,1,0:T(8,128)}, f32[16,32,256]{2,1,0:T(8,128)S(1)}, u32[]{:S(2)}) copy-start(f32[16,32,256]{2,1,0:T(8,128)S(1)} %all-to-all-done.2.refs_3_.b_same) | copy-start | bytes 1572868
  67.4 15.8 %collective-permute-start.3 = (f32[16,32,256]{2,1,0:T(8,128)S(1)}, f32[16,32,256]{2,1,0:T(8,128)S(1)}, u32[]{:S(2)}, u32[]{:S(2)}) collective-permute-start(f32[16,32,256]{2,1,0:T(8,128)S(1)} %all-to-all-done.2.refs_3_.b_same), channel_id=1, source_target_pairs={{0,1},{1,0},{2,3},{3,2},{4,5},{5,4},{6,7},{7,6},{8,9},{9,8},{10,11... | collective-permute-start | bytes 1572872 | tf_op jit(solution)/shard_map/ppermute | solution.py:172
  76.7 7.9 %copy-start.14 = (f32[128,1024]{1,0:T(8,128)}, f32[128,1024]{1,0:T(8,128)S(1)}, u32[]{:S(2)}) copy-start(f32[128,1024]{1,0:T(8,128)S(1)} %collective-permute-done.5.refs_5_) | copy-start | bytes 1572868
  76.7 15.0 %collective-permute-start.9 = (f32[128,1024]{1,0:T(8,128)S(1)}, f32[128,1024]{1,0:T(8,128)}, u32[]{:S(2)}, u32[]{:S(2)}) collective-permute-start(f32[128,1024]{1,0:T(8,128)S(1)} %collective-permute-done.5.refs_5_), channel_id=1, source_target_pairs={{0,32},{32,64},{64,96},{96,128},{128,160},{160,192},{192,224},{224... | collective-permute-start | bytes 1572872 | tf_op jit(solution)/shard_map/ppermute | solution.py:177
  78.6 5.9 %copy-start.15 = (f32[128,1024]{1,0:T(8,128)}, f32[128,1024]{1,0:T(8,128)S(1)}, u32[]{:S(2)}) copy-start(f32[128,1024]{1,0:T(8,128)S(1)} %collective-permute-done.7.refs_6_) | copy-start | bytes 1572868
  78.6 15.0 %collective-permute-start.11 = (f32[128,1024]{1,0:T(8,128)S(1)}, f32[128,1024]{1,0:T(8,128)}, u32[]{:S(2)}, u32[]{:S(2)}) collective-permute-start(f32[128,1024]{1,0:T(8,128)S(1)} %collective-permute-done.7.refs_6_), channel_id=1, source_target_pairs={{0,480},{32,0},{64,32},{96,64},{128,96},{160,128},{192,160},{224,1... | collective-permute-start | bytes 1572872 | tf_op jit(solution)/shard_map/ppermute | solution.py:177
  83.2 1.3 copy-start.4
  84.5 27.9 %copy-start.19 = (f32[1024,32]{0,1:T(8,128)S(1)}, f32[1024,32]{0,1:T(8,128)}, u32[]{:S(2)}) copy-start(f32[1024,32]{0,1:T(8,128)} %param.14) | copy-start | bytes 393220
  84.6 13.6 %all-to-all-start.3 = ((f32[16,32,256]{2,1,0:T(8,128)}), f32[16,32,256]{2,1,0:T(8,128)S(1)}, u32[]{:S(2)}, u32[]{:S(2)}) async-start(f32[16,32,256]{2,1,0:T(8,128)} %couple.1), calls=%async_computation.3 | async-start | bytes 1048576 | tf_op jit(solution)/shard_map/all_to_all | solution.py:167
  91.7 14.2 %collective-permute-start.10 = (f32[128,1024]{1,0:T(8,128)}, f32[128,1024]{1,0:T(8,128)S(1)}, u32[]{:S(2)}, u32[]{:S(2)}) collective-permute-start(f32[128,1024]{1,0:T(8,128)} %collective-permute-done.9.refs_7_), channel_id=1, source_target_pairs={{0,32},{32,64},{64,96},{96,128},{128,160},{160,192},{192,224},{224... | collective-permute-start | bytes 1572872 | tf_op jit(solution)/shard_map/ppermute | solution.py:177
  93.6 14.2 %collective-permute-start.12 = (f32[128,1024]{1,0:T(8,128)}, f32[128,1024]{1,0:T(8,128)S(1)}, u32[]{:S(2)}, u32[]{:S(2)}) collective-permute-start(f32[128,1024]{1,0:T(8,128)} %collective-permute-done.11.refs_8_), channel_id=1, source_target_pairs={{0,480},{32,0},{64,32},{96,64},{128,96},{160,128},{192,160},{224,1... | collective-permute-start | bytes 1572872 | tf_op jit(solution)/shard_map/ppermute | solution.py:177
  98.2 14.2 %collective-permute-start.8 = (f32[16,32,256]{2,1,0:T(8,128)S(1)}, f32[16,32,256]{2,1,0:T(8,128)S(1)}, u32[]{:S(2)}, u32[]{:S(2)}) collective-permute-start(f32[16,32,256]{2,1,0:T(8,128)S(1)} %all-to-all-done.3.refs_2_), channel_id=1, source_target_pairs={{0,1},{1,0},{2,3},{3,2},{4,5},{5,4},{6,7},{7,6},{8,9},{9,8},{10,11... | collective-permute-start | bytes 1572872 | tf_op jit(solution)/shard_map/ppermute | solution.py:172
  105.9 7.8 %copy-start.9 = (f32[128,1024]{1,0:T(8,128)}, f32[128,1024]{1,0:T(8,128)S(1)}, u32[]{:S(2)}) copy-start(f32[128,1024]{1,0:T(8,128)S(1)} %collective-permute-done.10.refs_4_.refs_9_) | copy-start | bytes 1572868
  105.9 13.1 %collective-permute-start.14 = (f32[128,1024]{1,0:T(8,128)S(1)}, f32[128,1024]{1,0:T(8,128)S(1)}, u32[]{:S(2)}, u32[]{:S(2)}) collective-permute-start(f32[128,1024]{1,0:T(8,128)S(1)} %collective-permute-done.10.refs_4_.refs_9_), channel_id=1, source_target_pairs={{0,32},{32,64},{64,96},{96,128},{128,160},{160,192},{192,224},{224... | collective-permute-start | bytes 1572872 | tf_op jit(solution)/shard_map/ppermute | solution.py:177
  107.8 5.9 %copy-start.10 = (f32[128,1024]{1,0:T(8,128)}, f32[128,1024]{1,0:T(8,128)S(1)}, u32[]{:S(2)}) copy-start(f32[128,1024]{1,0:T(8,128)S(1)} %collective-permute-done.12.refs_5_.refs_10_) | copy-start | bytes 1572868
  107.8 13.0 %collective-permute-start.15 = (f32[128,1024]{1,0:T(8,128)S(1)}, f32[128,1024]{1,0:T(8,128)}, u32[]{:S(2)}, u32[]{:S(2)}) collective-permute-start(f32[128,1024]{1,0:T(8,128)S(1)} %collective-permute-done.12.refs_5_.refs_10_), channel_id=1, source_target_pairs={{0,480},{32,0},{64,32},{96,64},{128,96},{160,128},{192,160},{224,1... | collective-permute-start | bytes 1572872 | tf_op jit(solution)/shard_map/ppermute | solution.py:177
  113.7 12.7 %all-to-all-start.4 = ((f32[16,32,256]{2,1,0:T(8,128)}), f32[16,32,256]{2,1,0:T(8,128)S(1)}, u32[]{:S(2)}, u32[]{:S(2)}) async-start(f32[16,32,256]{2,1,0:T(8,128)} %get-tuple-element.10), calls=%async_computation.4 | async-start | bytes 1048576 | tf_op jit(solution)/shard_map/all_to_all | solution.py:167
  118.9 21.7 %copy-start.26 = (f32[128,1024]{1,0:T(8,128)}, f32[128,1024]{1,0:T(8,128)S(1)}, u32[]{:S(2)}) copy-start(f32[128,1024]{1,0:T(8,128)S(1)} %collective-permute-done.14.refs_11_) | copy-start | bytes 1572868
  118.9 14.4 %collective-permute-start.16 = (f32[128,1024]{1,0:T(8,128)S(1)}, f32[128,1024]{1,0:T(8,128)S(1)}, u32[]{:S(2)}, u32[]{:S(2)}) collective-permute-start(f32[128,1024]{1,0:T(8,128)S(1)} %collective-permute-done.14.refs_11_), channel_id=1, source_target_pairs={{0,32},{32,64},{64,96},{96,128},{128,160},{160,192},{192,224},{224... | collective-permute-start | bytes 1572872 | tf_op jit(solution)/shard_map/ppermute | solution.py:177
  120.9 14.4 %collective-permute-start.17 = (f32[128,1024]{1,0:T(8,128)}, f32[128,1024]{1,0:T(8,128)S(1)}, u32[]{:S(2)}, u32[]{:S(2)}) collective-permute-start(f32[128,1024]{1,0:T(8,128)} %collective-permute-done.15.refs_12_), channel_id=1, source_target_pairs={{0,480},{32,0},{64,32},{96,64},{128,96},{160,128},{192,160},{224,1... | collective-permute-start | bytes 1572872 | tf_op jit(solution)/shard_map/ppermute | solution.py:177
  126.4 9.6 %copy-start.2 = (f32[16,32,256]{2,1,0:T(8,128)}, f32[16,32,256]{2,1,0:T(8,128)S(1)}, u32[]{:S(2)}) copy-start(f32[16,32,256]{2,1,0:T(8,128)S(1)} %all-to-all-done.4.a_same) | copy-start | bytes 1572868
  126.4 14.2 %collective-permute-start.13 = (f32[16,32,256]{2,1,0:T(8,128)S(1)}, f32[16,32,256]{2,1,0:T(8,128)S(1)}, u32[]{:S(2)}, u32[]{:S(2)}) collective-permute-start(f32[16,32,256]{2,1,0:T(8,128)S(1)} %all-to-all-done.4.a_same), channel_id=1, source_target_pairs={{0,1},{1,0},{2,3},{3,2},{4,5},{5,4},{6,7},{7,6},{8,9},{9,8},{10,11... | collective-permute-start | bytes 1572872 | tf_op jit(solution)/shard_map/ppermute | solution.py:172
  133.3 2.7 %copy-start.23 = (f32[128,1024]{1,0:T(8,128)}, f32[128,1024]{1,0:T(8,128)S(1)}, u32[]{:S(2)}) copy-start(f32[128,1024]{1,0:T(8,128)S(1)} %collective-permute-done.16.refs_13_) | copy-start | bytes 1572868
  133.4 16.8 %collective-permute-start.18 = (f32[64,1024]{1,0:T(8,128)S(1)}, f32[64,1024]{1,0:T(8,128)S(1)}, u32[]{:S(2)}, u32[]{:S(2)}) collective-permute-start(f32[64,1024]{1,0:T(8,128)S(1)} %slice.8), channel_id=1, source_target_pairs={{0,32},{32,64},{64,96},{96,128},{128,160},{160,192},{192,224},{224... | collective-permute-start | bytes 786440 | tf_op jit(solution)/shard_map/ppermute | solution.py:177
  135.3 5.4 %copy-start.24 = (f32[128,1024]{1,0:T(8,128)}, f32[128,1024]{1,0:T(8,128)S(1)}, u32[]{:S(2)}) copy-start(f32[128,1024]{1,0:T(8,128)S(1)} %collective-permute-done.17.refs_14_) | copy-start | bytes 1572868
  136.1 14.1 %collective-permute-start.19 = (f32[64,1024]{1,0:T(8,128)}, f32[64,1024]{1,0:T(8,128)S(1)}, u32[]{:S(2)}, u32[]{:S(2)}) collective-permute-start(f32[64,1024]{1,0:T(8,128)} %slice.9), channel_id=1, source_target_pairs={{0,480},{32,0},{64,32},{96,64},{128,96},{160,128},{192,160},{224,1... | collective-permute-start | bytes 786440 | tf_op jit(solution)/shard_map/ppermute | solution.py:177
  140.6 0.8 copy-start.11
  141.5 8.7 %copy-start.1 = (f32[16,32,256]{2,1,0:T(8,128)S(1)}, f32[16,32,256]{2,1,0:T(8,128)}, u32[]{:S(2)}) copy-start(f32[16,32,256]{2,1,0:T(8,128)} %copy-done) | copy-start | bytes 1572868
  141.5 8.7 %copy-start.3 = (f32[16,32,256]{2,1,0:T(8,128)S(1)}, f32[16,32,256]{2,1,0:T(8,128)}, u32[]{:S(2)}) copy-start(f32[16,32,256]{2,1,0:T(8,128)} %copy-done.2) | copy-start | bytes 1572868
  141.5 8.7 %copy-start.5 = (f32[16,32,256]{2,1,0:T(8,128)S(1)}, f32[16,32,256]{2,1,0:T(8,128)}, u32[]{:S(2)}) copy-start(f32[16,32,256]{2,1,0:T(8,128)} %copy-done.4) | copy-start | bytes 1572868
  150.2 1.2 copy-start.6
  151.4 1.0 copy-start.12

commit v4 on v3

--- a/solution.py
+++ b/solution.py
@@ -136,29 +136,42 @@
     )(plane, core, *x, rhs, *blocks)
 
 
-def far_kernel(planes, plane_ref, core_ref, b_same, b_other, a_same, a_other, rhs_ref, rows_b_ref, rows_a_ref, out_ref, x_ref):
+def far_kernel(planes, plane_ref, core_ref, *refs):
+    x_refs, rhs_in, row_refs = refs[:4], refs[4], refs[5:-6]
+    out_ref, parts_ref, x_ref, rhs_ref, rows_ref, semaphores = refs[-6:]
     place = lax.rem(plane_ref[0] + planes // 2, planes)
-    gather_x(((b_same, b_other), (a_same, a_other)), place, core_ref[0], x_ref, 0)
-    rows = jnp.concatenate([rows_b_ref[...], rows_a_ref[...]], axis=0)
-    out_ref[...] = rhs_ref[...] - product(x_ref[...].T, rows).T
+    lines = row_refs[0].shape[0]
+    pairs = [(r.at[pl.ds(place, 1)], parts_ref.at[pl.ds(n, 1)]) for n, r in enumerate(x_refs)]
+    pairs += [(r, rows_ref.at[pl.ds(n * lines, lines)]) for n, r in enumerate(row_refs)] + [(rhs_in, rhs_ref)]
+    copies = [pltpu.make_async_copy(*pair, semaphores.at[n]) for n, pair in enumerate(pairs)]
+    for copy in copies:
+        copy.start()
+    for copy in copies[:-1]:
+        copy.wait()
+    parts = [parts_ref.at[pl.ds(n, 1)] for n in range(4)]
+    gather_x((parts[:2], parts[2:]), 0, core_ref[0], x_ref, 0)
+    part = product(x_ref[...].T, rows_ref[...]).T
+    copies[-1].wait()
+    out_ref[...] = rhs_ref[...] - part
 
 
 def update_far(plane, core, x, rhs, blocks, planes):
+    vmem, smem, whole = (pl.BlockSpec(memory_space=m) for m in (pltpu.VMEM, pltpu.SMEM, pl.ANY))
     height, width = rhs.shape
-    tile = 512
-    smem = pl.BlockSpec(memory_space=pltpu.SMEM)
-    out = pl.BlockSpec((tile, width), lambda n: (n, 0))
+    depth = sum(b.shape[0] for b in blocks)
     return pl.pallas_call(
         functools.partial(far_kernel, planes),
-        grid=(height // tile,),
-        out_shape=jax.ShapeDtypeStruct((height, width), F32),
-        in_specs=[smem] * 2
-        + [pl.BlockSpec(a.shape, lambda n: (0, 0, 0)) for a in x]
-        + [out]
-        + [pl.BlockSpec((b.shape[0], tile), lambda n: (0, n)) for b in blocks],
-        out_specs=out,
-        scratch_shapes=[pltpu.VMEM((sum(b.shape[0] for b in blocks), width), F32)],
-        compiler_params=pltpu.CompilerParams(vmem_limit_bytes=VMEM_LIMIT),
+        out_shape=jax.ShapeDtypeStruct(rhs.shape, F32),
+        in_specs=[smem] * 2 + [whole] * (len(x) + 1 + len(blocks)),
+        out_specs=vmem,
+        scratch_shapes=[
+            pltpu.VMEM((len(x),) + x[0].shape[1:], F32),
+            pltpu.VMEM((depth, width), F32),
+            pltpu.VMEM(rhs.shape, F32),
+            pltpu.VMEM((depth, height), F32),
+            pltpu.SemaphoreType.DMA((len(x) + len(blocks) + 1,)),
+        ],
+        compiler_params=pltpu.CompilerParams(vmem_limit_bytes=UPDATE_LIMIT),
         name="update_far",
     )(plane, core, *x, rhs, *blocks)
 
@@ -202,14 +215,14 @@
         blocks, offsets = ring(own, planes)
         (rhs_copies,) = call(send, [copies], [rhs_b])
         x_b, x_copies = call(
-            solve, [local, copies], [core, inverse_b.T, *spread(rhs_copies)], after=blocks[1:3] + [across], scratch=[whole]
+            solve, [local, copies], [core, inverse_b.T, *spread(rhs_copies)], after=blocks[1:2] + [across], scratch=[whole]
         )
         x_b_all = spread(x_copies)
         (coupled,) = call(
-            couple, [copies], [core, rhs_a, across, *x_b_all], after=blocks[5:7], scratch=[whole]
+            couple, [copies], [core, rhs_a, across, *x_b_all], after=blocks[5:6], scratch=[whole]
         )
         x_a, x_copies = call(
-            solve, [local, copies], [core, inverse_a.T, *spread(coupled)], after=blocks[9:11], scratch=[whole]
+            solve, [local, copies], [core, inverse_a.T, *spread(coupled)], after=blocks[9:10], scratch=[whole]
         )
         x = x_b_all + spread(x_copies)
         partial = update_near(plane, core, x, rhs_above, blocks[:-2], offsets[:-1], planes)

time: 157 us -> 157 us (level)
  local copies, waits for them, and re-layouts: 4.66 us -> 3.03 us
    unnamed x54 -> x46, local copies, waits for them, and re-layouts: 3.89 us -> 2.99 us
where the time goes in v4:
time: 157 us; the launch traced here: 154 us
  starting transfers between devices  110 us (70%)
  waiting for transfers between devices  22.6 us (14%)
  Pallas kernels  17.1 us (11%)
  local copies, waits for them, and re-layouts  3.03 us (2%)
    ppermute x16, starting transfers between devices, move(): lax.ppermute(block, 'row', [(i, (i + by) % planes) for i in range(planes)])  58.4 us
    all_to_all x5, starting transfers between devices, exchange(): return lax.all_to_all(copies, axis, 0, 0, tiled=True)  31.7 us
    ppermute x4, starting transfers between devices, spread(): return (same, lax.ppermute(same, 'core', [(0, 1), (1, 0)]))  19.8 us
    ppermute x16, waiting for transfers between devices, move(): lax.ppermute(block, 'row', [(i, (i + by) % planes) for i in range(planes)])  15.9 us
    pallas_call x1, Pallas kernels, update_near(): pl.pallas_call(functools.partial(near_kernel, planes, offsets), out_shape...  8.59 us
    all_to_all x5, waiting for transfers between devices, exchange(): return lax.all_to_all(copies, axis, 0, 0, tiled=True)  6.68 us
    pallas_call x6, Pallas kernels, call(): pl.pallas_call(body, out_shape=[jax.ShapeDtypeStruct(s, F32) for s in sha...  5.48 us
  transfers between devices with their start and end apart: 25, of which 7 were waited for; matrix products, arithmetic and copies ran while one was open for 0% of the time, Pallas kernels for 9%

profile of v4, /device:TPU:1, one launch (start us, length us, event | category | flops | bytes accessed | tf_op | source)
XLA Modules:
  0.0 153.9 jit_solution(13490222800479531290)
XLA Ops:
  0.6 0.7 copy-done.11
  1.4 0.8 send.1
  2.2 7.7 %all-to-all-start = ((f32[16,32,256]{2,1,0:T(8,128)}), f32[16,32,256]{2,1,0:T(8,128)S(1)}, u32[]{:S(2)}, u32[]{:S(2)}) async-start(f32[16,32,256]{2,1,0:T(8,128)} %send.1), calls=%async_computation | async-start | bytes 1048576 | tf_op jit(solution)/shard_map/all_to_all | solution.py:180
  10.0 0.0 copy-start.12
  10.0 3.5 %collective-permute-start.1 = (f32[128,1024]{1,0:T(8,128)S(1)}, f32[128,1024]{1,0:T(8,128)S(1)}, u32[]{:S(2)}, u32[]{:S(2)}) collective-permute-start(f32[128,1024]{1,0:T(8,128)S(1)} %join.1.refs_0_), channel_id=1, source_target_pairs={{0,32},{32,64},{64,96},{96,128},{128,160},{160,192},{192,224},{224... | collective-permute-start | bytes 1572872 | tf_op jit(solution)/shard_map/ppermute | solution.py:190
  13.6 9.5 %collective-permute-start.9 = (f32[128,1024]{1,0:T(8,128)S(1)}, f32[128,1024]{1,0:T(8,128)S(1)}, u32[]{:S(2)}, u32[]{:S(2)}) collective-permute-start(f32[128,1024]{1,0:T(8,128)S(1)} %join.1.refs_0_), channel_id=1, source_target_pairs={{0,480},{32,0},{64,32},{96,64},{128,96},{160,128},{192,160},{224,1... | collective-permute-start | bytes 1572872 | tf_op jit(solution)/shard_map/ppermute | solution.py:190
  23.1 0.0 all-to-all-done.refs_2_
  23.1 3.1 %collective-permute-start = (f32[16,32,256]{2,1,0:T(8,128)S(1)}, f32[16,32,256]{2,1,0:T(8,128)S(1)}, u32[]{:S(2)}, u32[]{:S(2)}) collective-permute-start(f32[16,32,256]{2,1,0:T(8,128)S(1)} %all-to-all-done.refs_2_), channel_id=1, source_target_pairs={{0,1},{1,0},{2,3},{3,2},{4,5},{5,4},{6,7},{7,6},{8,9},{9,8},{10,11... | collective-permute-start | bytes 1572872 | tf_op jit(solution)/shard_map/ppermute | solution.py:185
  26.3 0.7 begin.1
  27.0 13.1 %all-to-all-start.1 = ((f32[16,16,128]{2,1,0:T(8,128)}), f32[16,16,128]{2,1,0:T(8,128)S(1)}, u32[]{:S(2)}, u32[]{:S(2)}) async-start(f32[16,16,128]{2,1,0:T(8,128)} %begin.1), calls=%async_computation.1 | async-start | bytes 262144 | tf_op jit(solution)/shard_map/all_to_all | solution.py:180
  40.2 0.0 collective-permute-done.1.refs_4_.refs_1_
  40.2 3.3 %collective-permute-start.3 = (f32[128,1024]{1,0:T(8,128)S(1)}, f32[128,1024]{1,0:T(8,128)}, u32[]{:S(2)}, u32[]{:S(2)}) collective-permute-start(f32[128,1024]{1,0:T(8,128)S(1)} %collective-permute-done.1.refs_4_.refs_1_), channel_id=1, source_target_pairs={{0,32},{32,64},{64,96},{96,128},{128,160},{160,192},{192,224},{224... | collective-permute-start | bytes 1572872 | tf_op jit(solution)/shard_map/ppermute | solution.py:190
  43.5 0.0 collective-permute-done.9.refs_2_
  43.5 3.2 %collective-permute-start.10 = (f32[128,1024]{1,0:T(8,128)S(1)}, f32[128,1024]{1,0:T(8,128)}, u32[]{:S(2)}, u32[]{:S(2)}) collective-permute-start(f32[128,1024]{1,0:T(8,128)S(1)} %collective-permute-done.9.refs_2_), channel_id=1, source_target_pairs={{0,480},{32,0},{64,32},{96,64},{128,96},{160,128},{192,160},{224,1... | collective-permute-start | bytes 1572872 | tf_op jit(solution)/shard_map/ppermute | solution.py:190
  46.7 5.9 %all-to-all-done.1.refs_5_.refs_2_ = f32[16,16,128]{2,1,0:T(8,128)S(1)} async-done(((f32[16,16,128]{2,1,0:T(8,128)}), f32[16,16,128]{2,1,0:T(8,128)S(1)}, u32[]{:S(2)}, u32[]{:S(2)}) %all-to-all-start.1) | async-done | bytes 131104 | tf_op jit(solution)/shard_map/all_to_all | solution.py:180
  52.6 0.0 collective-permute-done.refs_3_
  52.6 1.3 solve.2
  53.9 0.0 copy-start.10
  53.9 3.6 %all-to-all-start.2 = ((f32[16,32,256]{2,1,0:T(8,128)}), f32[16,32,256]{2,1,0:T(8,128)S(1)}, u32[]{:S(2)}, u32[]{:S(2)}) async-start(f32[16,32,256]{2,1,0:T(8,128)} %get-tuple-element.8), calls=%async_computation.2 | async-start | bytes 1048576 | tf_op jit(solution)/shard_map/all_to_all | solution.py:180
  57.5 3.4 %collective-permute-done.3.refs_3_ = f32[128,1024]{1,0:T(8,128)} collective-permute-done((f32[128,1024]{1,0:T(8,128)S(1)}, f32[128,1024]{1,0:T(8,128)}, u32[]{:S(2)}, u32[]{:S(2)}) %collective-permute-start.3) | collective-permute-done | bytes 524320 | tf_op jit(solution)/shard_map/ppermute | solution.py:190
  60.9 1.9 %collective-permute-start.4 = (f32[128,1024]{1,0:T(8,128)}, f32[128,1024]{1,0:T(8,128)S(1)}, u32[]{:S(2)}, u32[]{:S(2)}) collective-permute-start(f32[128,1024]{1,0:T(8,128)} %collective-permute-done.3.refs_3_), channel_id=1, source_target_pairs={{0,32},{32,64},{64,96},{96,128},{128,160},{160,192},{192,224},{224... | collective-permute-start | bytes 1572872 | tf_op jit(solution)/shard_map/ppermute | solution.py:190
  62.9 0.0 collective-permute-done.10.refs_4_
  62.9 4.6 %collective-permute-start.11 = (f32[128,1024]{1,0:T(8,128)}, f32[128,1024]{1,0:T(8,128)S(1)}, u32[]{:S(2)}, u32[]{:S(2)}) collective-permute-start(f32[128,1024]{1,0:T(8,128)} %collective-permute-done.10.refs_4_), channel_id=1, source_target_pairs={{0,480},{32,0},{64,32},{96,64},{128,96},{160,128},{192,160},{224,1... | collective-permute-start | bytes 1572872 | tf_op jit(solution)/shard_map/ppermute | solution.py:190
  67.5 0.0 all-to-all-done.2.refs_3_.b_same.refs_0_
  67.5 4.6 %collective-permute-start.2 = (f32[16,32,256]{2,1,0:T(8,128)S(1)}, f32[16,32,256]{2,1,0:T(8,128)S(1)}, u32[]{:S(2)}, u32[]{:S(2)}) collective-permute-start(f32[16,32,256]{2,1,0:T(8,128)S(1)} %all-to-all-done.2.refs_3_.b_same.refs_0_), channel_id=1, source_target_pairs={{0,1},{1,0},{2,3},{3,2},{4,5},{5,4},{6,7},{7,6},{8,9},{9,8},{10,11... | collective-permute-start | bytes 1572872 | tf_op jit(solution)/shard_map/ppermute | solution.py:185
  72.0 4.9 %collective-permute-done.4.refs_5_ = f32[128,1024]{1,0:T(8,128)S(1)} collective-permute-done((f32[128,1024]{1,0:T(8,128)}, f32[128,1024]{1,0:T(8,128)S(1)}, u32[]{:S(2)}, u32[]{:S(2)}) %collective-permute-start.4) | collective-permute-done | bytes 524320 | tf_op jit(solution)/shard_map/ppermute | solution.py:190
  77.0 1.9 %collective-permute-start.6 = (f32[128,1024]{1,0:T(8,128)S(1)}, f32[128,1024]{1,0:T(8,128)S(1)}, u32[]{:S(2)}, u32[]{:S(2)}) collective-permute-start(f32[128,1024]{1,0:T(8,128)S(1)} %collective-permute-done.4.refs_5_), channel_id=1, source_target_pairs={{0,32},{32,64},{64,96},{96,128},{128,160},{160,192},{192,224},{224... | collective-permute-start | bytes 1572872 | tf_op jit(solution)/shard_map/ppermute | solution.py:190
  78.9 0.0 collective-permute-done.11.refs_6_
  78.9 4.6 %collective-permute-start.12 = (f32[128,1024]{1,0:T(8,128)S(1)}, f32[128,1024]{1,0:T(8,128)}, u32[]{:S(2)}, u32[]{:S(2)}) collective-permute-start(f32[128,1024]{1,0:T(8,128)S(1)} %collective-permute-done.11.refs_6_), channel_id=1, source_target_pairs={{0,480},{32,0},{64,32},{96,64},{128,96},{160,128},{192,160},{224,1... | collective-permute-start | bytes 1572872 | tf_op jit(solution)/shard_map/ppermute | solution.py:190
  83.5 0.0 collective-permute-done.2.refs_4_.b_other.refs_1_
  83.5 1.3 couple.1
  84.8 0.0 copy-start.8
  84.9 3.7 %all-to-all-start.3 = ((f32[16,32,256]{2,1,0:T(8,128)}), f32[16,32,256]{2,1,0:T(8,128)S(1)}, u32[]{:S(2)}, u32[]{:S(2)}) async-start(f32[16,32,256]{2,1,0:T(8,128)} %couple.1), calls=%async_computation.3 | async-start | bytes 1048576 | tf_op jit(solution)/shard_map/all_to_all | solution.py:180
  88.6 3.3 %collective-permute-done.6.refs_7_ = f32[128,1024]{1,0:T(8,128)S(1)} collective-permute-done((f32[128,1024]{1,0:T(8,128)S(1)}, f32[128,1024]{1,0:T(8,128)S(1)}, u32[]{:S(2)}, u32[]{:S(2)}) %collective-permute-start.6) | collective-permute-done | bytes 524320 | tf_op jit(solution)/shard_map/ppermute | solution.py:190
  91.9 1.9 %collective-permute-start.7 = (f32[128,1024]{1,0:T(8,128)S(1)}, f32[128,1024]{1,0:T(8,128)S(1)}, u32[]{:S(2)}, u32[]{:S(2)}) collective-permute-start(f32[128,1024]{1,0:T(8,128)S(1)} %collective-permute-done.6.refs_7_), channel_id=1, source_target_pairs={{0,32},{32,64},{64,96},{96,128},{128,160},{160,192},{192,224},{224... | collective-permute-start | bytes 1572872 | tf_op jit(solution)/shard_map/ppermute | solution.py:190
  93.8 0.0 collective-permute-done.12.refs_8_
  93.8 4.6 %collective-permute-start.13 = (f32[128,1024]{1,0:T(8,128)}, f32[128,1024]{1,0:T(8,128)S(1)}, u32[]{:S(2)}, u32[]{:S(2)}) collective-permute-start(f32[128,1024]{1,0:T(8,128)} %collective-permute-done.12.refs_8_), channel_id=1, source_target_pairs={{0,480},{32,0},{64,32},{96,64},{128,96},{160,128},{192,160},{224,1... | collective-permute-start | bytes 1572872 | tf_op jit(solution)/shard_map/ppermute | solution.py:190
  98.4 0.0 all-to-all-done.3.refs_2_
  98.4 5.0 %collective-permute-start.5 = (f32[16,32,256]{2,1,0:T(8,128)S(1)}, f32[16,32,256]{2,1,0:T(8,128)S(1)}, u32[]{:S(2)}, u32[]{:S(2)}) collective-permute-start(f32[16,32,256]{2,1,0:T(8,128)S(1)} %all-to-all-done.3.refs_2_), channel_id=1, source_target_pairs={{0,1},{1,0},{2,3},{3,2},{4,5},{5,4},{6,7},{7,6},{8,9},{9,8},{10,11... | collective-permute-start | bytes 1572872 | tf_op jit(solution)/shard_map/ppermute | solution.py:185
  103.4 2.5 %collective-permute-done.7.refs_4_.refs_9_ = f32[128,1024]{1,0:T(8,128)S(1)} collective-permute-done((f32[128,1024]{1,0:T(8,128)S(1)}, f32[128,1024]{1,0:T(8,128)S(1)}, u32[]{:S(2)}, u32[]{:S(2)}) %collective-permute-start.7) | collective-permute-done | bytes 524320 | tf_op jit(solution)/shard_map/ppermute | solution.py:190
  105.9 1.9 %collective-permute-start.14 = (f32[128,1024]{1,0:T(8,128)S(1)}, f32[128,1024]{1,0:T(8,128)}, u32[]{:S(2)}, u32[]{:S(2)}) collective-permute-start(f32[128,1024]{1,0:T(8,128)S(1)} %collective-permute-done.7.refs_4_.refs_9_), channel_id=1, source_target_pairs={{0,32},{32,64},{64,96},{96,128},{128,160},{160,192},{192,224},{224... | collective-permute-start | bytes 1572872 | tf_op jit(solution)/shard_map/ppermute | solution.py:190
  107.8 0.0 collective-permute-done.13.refs_10_
  107.8 4.6 %collective-permute-start.15 = (f32[128,1024]{1,0:T(8,128)S(1)}, f32[128,1024]{1,0:T(8,128)}, u32[]{:S(2)}, u32[]{:S(2)}) collective-permute-start(f32[128,1024]{1,0:T(8,128)S(1)} %collective-permute-done.13.refs_10_), channel_id=1, source_target_pairs={{0,480},{32,0},{64,32},{96,64},{128,96},{160,128},{192,160},{224,1... | collective-permute-start | bytes 1572872 | tf_op jit(solution)/shard_map/ppermute | solution.py:190
  112.4 0.0 collective-permute-done.5.refs_3_
  112.4 1.3 solve.3
  113.7 3.6 %all-to-all-start.4 = ((f32[16,32,256]{2,1,0:T(8,128)}), f32[16,32,256]{2,1,0:T(8,128)S(1)}, u32[]{:S(2)}, u32[]{:S(2)}) async-start(f32[16,32,256]{2,1,0:T(8,128)} %get-tuple-element.10), calls=%async_computation.4 | async-start | bytes 1048576 | tf_op jit(solution)/shard_map/all_to_all | solution.py:180
  117.3 1.7 %collective-permute-done.14.refs_11_ = f32[128,1024]{1,0:T(8,128)} collective-permute-done((f32[128,1024]{1,0:T(8,128)S(1)}, f32[128,1024]{1,0:T(8,128)}, u32[]{:S(2)}, u32[]{:S(2)}) %collective-permute-start.14) | collective-permute-done | bytes 524320 | tf_op jit(solution)/shard_map/ppermute | solution.py:190
  119.0 1.9 %collective-permute-start.16 = (f32[128,1024]{1,0:T(8,128)}, f32[128,1024]{1,0:T(8,128)S(1)}, u32[]{:S(2)}, u32[]{:S(2)}) collective-permute-start(f32[128,1024]{1,0:T(8,128)} %collective-permute-done.14.refs_11_), channel_id=1, source_target_pairs={{0,32},{32,64},{64,96},{96,128},{128,160},{160,192},{192,224},{224... | collective-permute-start | bytes 1572872 | tf_op jit(solution)/shard_map/ppermute | solution.py:190
  121.0 0.0 collective-permute-done.15.refs_12_
  121.0 4.6 %collective-permute-start.17 = (f32[128,1024]{1,0:T(8,128)}, f32[128,1024]{1,0:T(8,128)S(1)}, u32[]{:S(2)}, u32[]{:S(2)}) collective-permute-start(f32[128,1024]{1,0:T(8,128)} %collective-permute-done.15.refs_12_), channel_id=1, source_target_pairs={{0,480},{32,0},{64,32},{96,64},{128,96},{160,128},{192,160},{224,1... | collective-permute-start | bytes 1572872 | tf_op jit(solution)/shard_map/ppermute | solution.py:190
  125.5 0.8 all-to-all-done.4.a_same.refs_2_
  126.3 7.0 %collective-permute-start.8 = (f32[16,32,256]{2,1,0:T(8,128)S(1)}, f32[16,32,256]{2,1,0:T(8,128)S(1)}, u32[]{:S(2)}, u32[]{:S(2)}) collective-permute-start(f32[16,32,256]{2,1,0:T(8,128)S(1)} %all-to-all-done.4.a_same.refs_2_), channel_id=1, source_target_pairs={{0,1},{1,0},{2,3},{3,2},{4,5},{5,4},{6,7},{7,6},{8,9},{9,8},{10,11... | collective-permute-start | bytes 1572872 | tf_op jit(solution)/shard_map/ppermute | solution.py:185
  133.4 0.0 collective-permute-done.16.refs_13_
  133.4 0.0 copy-start.15
  133.4 1.9 %collective-permute-start.18 = (f32[64,1024]{1,0:T(8,128)S(1)}, f32[64,1024]{1,0:T(8,128)S(1)}, u32[]{:S(2)}, u32[]{:S(2)}) collective-permute-start(f32[64,1024]{1,0:T(8,128)S(1)} %slice.8), channel_id=1, source_target_pairs={{0,32},{32,64},{64,96},{96,128},{128,160},{160,192},{192,224},{224... | collective-permute-start | bytes 786440 | tf_op jit(solution)/shard_map/ppermute | solution.py:190
  135.4 0.0 collective-permute-done.17.refs_14_
  135.4 4.6 %collective-permute-start.19 = (f32[64,1024]{1,0:T(8,128)S(1)}, f32[64,1024]{1,0:T(8,128)S(1)}, u32[]{:S(2)}, u32[]{:S(2)}) collective-permute-start(f32[64,1024]{1,0:T(8,128)S(1)} %slice.9), channel_id=1, source_target_pairs={{0,480},{32,0},{64,32},{96,64},{128,96},{160,128},{192,160},{224,1... | collective-permute-start | bytes 786440 | tf_op jit(solution)/shard_map/ppermute | solution.py:190
  140.0 0.0 collective-permute-done.8.a_other.refs_3_
  140.0 0.8 copy-done.14
  140.8 8.6 %update_near.1.refs_4_ = f32[1024,256]{1,0:T(8,128)} custom-call(s32[1]{0:T(128)} %bitcast.4.plane_ref, s32[1]{0:T(128)} %bitcast.refs_0_.core_ref, f32[16,32,256]{2,1,0:T(8,128)} %copy-done, f32[16,32,256]{2,1,0:T(8,128)} %copy-done.1, f32[16,32,256]{2,1,0:T(8,128)} %copy-done.13, f32[16,32,256]{2,1,0:T(8,128)} %copy-done.14, f32[1024,256]{1,0:T(8,128)} %rhs_ref.1, ...), custom_call_target="tpu_custom_call" | custom-call | tf_op jit(solution)/shard_map/update_near/pallas_call | solution.py:123
  149.4 0.0 collective-permute-done.19.refs_6_
  149.5 0.7 copy-done.21
  150.1 0.7 copy-done.22
  150.8 3.1 %update_far.1 = f32[1024,256]{1,0:T(8,128)} custom-call(s32[1]{0:T(128)} %bitcast.4.plane_ref, s32[1]{0:T(128)} %bitcast.refs_0_.core_ref, f32[16,32,256]{2,1,0:T(8,128)} %copy-done, f32[16,32,256]{2,1,0:T(8,128)} %copy-done.1, f32[16,32,256]{2,1,0:T(8,128)} %copy-done.13, f32[16,32,256]{2,1,0:T(8,128)} %copy-done.14, f32[1024,256]{1,0:T(8,128)} %update_near.1.refs_4_, ...), custom_call_target="tpu_custom_call" | custom-call | tf_op jit(solution)/shard_map/update_far/pallas_call | solution.py:162
  (42 shorter events, 0.2 us)
Async XLA Ops:
  0.6 0.8 copy-start.11
  2.2 7.7 %copy-start.6 = (f32[64,1024]{1,0:T(8,128)S(1)}, f32[64,1024]{1,0:T(8,128)}, u32[]{:S(2)}) copy-start(f32[64,1024]{1,0:T(8,128)} %refs_0_.3) | copy-start | bytes 786436
  2.2 7.7 %copy-start.7 = (f32[64,1024]{1,0:T(8,128)S(1)}, f32[64,1024]{1,0:T(8,128)}, u32[]{:S(2)}) copy-start(f32[64,1024]{1,0:T(8,128)} %refs_1_.2) | copy-start | bytes 786436
  2.2 20.9 %all-to-all-start = ((f32[16,32,256]{2,1,0:T(8,128)}), f32[16,32,256]{2,1,0:T(8,128)S(1)}, u32[]{:S(2)}, u32[]{:S(2)}) async-start(f32[16,32,256]{2,1,0:T(8,128)} %send.1), calls=%async_computation | async-start | bytes 1048576 | tf_op jit(solution)/shard_map/all_to_all | solution.py:180
  10.0 16.3 %copy-start.12 = (f32[64,32]{0,1:T(8,128)S(1)}, f32[64,32]{0,1:T(8,128)}, u32[]{:S(2)}) copy-start(f32[64,32]{0,1:T(8,128)} %param.13) | copy-start | bytes 24580
  10.0 43.9 %copy-start.3 = (f32[128,1024]{1,0:T(8,128)}, f32[128,1024]{1,0:T(8,128)S(1)}, u32[]{:S(2)}) copy-start(f32[128,1024]{1,0:T(8,128)S(1)} %join.1.refs_0_) | copy-start | bytes 1572868
  10.0 30.1 %collective-permute-start.1 = (f32[128,1024]{1,0:T(8,128)S(1)}, f32[128,1024]{1,0:T(8,128)S(1)}, u32[]{:S(2)}, u32[]{:S(2)}) collective-permute-start(f32[128,1024]{1,0:T(8,128)S(1)} %join.1.refs_0_), channel_id=1, source_target_pairs={{0,32},{32,64},{64,96},{96,128},{128,160},{160,192},{192,224},{224... | collective-permute-start | bytes 1572872 | tf_op jit(solution)/shard_map/ppermute | solution.py:190
  13.6 29.9 %collective-permute-start.9 = (f32[128,1024]{1,0:T(8,128)S(1)}, f32[128,1024]{1,0:T(8,128)S(1)}, u32[]{:S(2)}, u32[]{:S(2)}) collective-permute-start(f32[128,1024]{1,0:T(8,128)S(1)} %join.1.refs_0_), channel_id=1, source_target_pairs={{0,480},{32,0},{64,32},{96,64},{128,96},{160,128},{192,160},{224,1... | collective-permute-start | bytes 1572872 | tf_op jit(solution)/shard_map/ppermute | solution.py:190
  23.1 29.5 %collective-permute-start = (f32[16,32,256]{2,1,0:T(8,128)S(1)}, f32[16,32,256]{2,1,0:T(8,128)S(1)}, u32[]{:S(2)}, u32[]{:S(2)}) collective-permute-start(f32[16,32,256]{2,1,0:T(8,128)S(1)} %all-to-all-done.refs_2_), channel_id=1, source_target_pairs={{0,1},{1,0},{2,3},{3,2},{4,5},{5,4},{6,7},{7,6},{8,9},{9,8},{10,11... | collective-permute-start | bytes 1572872 | tf_op jit(solution)/shard_map/ppermute | solution.py:185
  27.0 25.6 %copy-start.9 = (f32[1024,32]{0,1:T(8,128)S(1)}, f32[1024,32]{0,1:T(8,128)}, u32[]{:S(2)}) copy-start(f32[1024,32]{0,1:T(8,128)} %param.15) | copy-start | bytes 393220
  27.0 25.6 %all-to-all-start.1 = ((f32[16,16,128]{2,1,0:T(8,128)}), f32[16,16,128]{2,1,0:T(8,128)S(1)}, u32[]{:S(2)}, u32[]{:S(2)}) async-start(f32[16,16,128]{2,1,0:T(8,128)} %begin.1), calls=%async_computation.1 | async-start | bytes 262144 | tf_op jit(solution)/shard_map/all_to_all | solution.py:180
  40.2 13.7 %copy-start.5 = (f32[128,1024]{1,0:T(8,128)}, f32[128,1024]{1,0:T(8,128)S(1)}, u32[]{:S(2)}) copy-start(f32[128,1024]{1,0:T(8,128)S(1)} %collective-permute-done.1.refs_4_.refs_1_) | copy-start | bytes 1572868
  40.2 20.8 %collective-permute-start.3 = (f32[128,1024]{1,0:T(8,128)S(1)}, f32[128,1024]{1,0:T(8,128)}, u32[]{:S(2)}, u32[]{:S(2)}) collective-permute-start(f32[128,1024]{1,0:T(8,128)S(1)} %collective-permute-done.1.refs_4_.refs_1_), channel_id=1, source_target_pairs={{0,32},{32,64},{64,96},{96,128},{128,160},{160,192},{192,224},{224... | collective-permute-start | bytes 1572872 | tf_op jit(solution)/shard_map/ppermute | solution.py:190
  43.5 10.4 %copy-start.17 = (f32[128,1024]{1,0:T(8,128)}, f32[128,1024]{1,0:T(8,128)S(1)}, u32[]{:S(2)}) copy-start(f32[128,1024]{1,0:T(8,128)S(1)} %collective-permute-done.9.refs_2_) | copy-start | bytes 1572868
  43.5 19.4 %collective-permute-start.10 = (f32[128,1024]{1,0:T(8,128)S(1)}, f32[128,1024]{1,0:T(8,128)}, u32[]{:S(2)}, u32[]{:S(2)}) collective-permute-start(f32[128,1024]{1,0:T(8,128)S(1)} %collective-permute-done.9.refs_2_), channel_id=1, source_target_pairs={{0,480},{32,0},{64,32},{96,64},{128,96},{160,128},{192,160},{224,1... | collective-permute-start | bytes 1572872 | tf_op jit(solution)/shard_map/ppermute | solution.py:190
  53.9 29.6 %copy-start.10 = (f32[32,256]{1,0:T(8,128)S(1)}, f32[32,256]{1,0:T(8,128)}, u32[]{:S(2)}) copy-start(f32[32,256]{1,0:T(8,128)} %refs_1_.3) | copy-start | bytes 98308
  53.9 13.5 %all-to-all-start.2 = ((f32[16,32,256]{2,1,0:T(8,128)}), f32[16,32,256]{2,1,0:T(8,128)S(1)}, u32[]{:S(2)}, u32[]{:S(2)}) async-start(f32[16,32,256]{2,1,0:T(8,128)} %get-tuple-element.8), calls=%async_computation.2 | async-start | bytes 1048576 | tf_op jit(solution)/shard_map/all_to_all | solution.py:180
  60.9 16.0 %collective-permute-start.4 = (f32[128,1024]{1,0:T(8,128)}, f32[128,1024]{1,0:T(8,128)S(1)}, u32[]{:S(2)}, u32[]{:S(2)}) collective-permute-start(f32[128,1024]{1,0:T(8,128)} %collective-permute-done.3.refs_3_), channel_id=1, source_target_pairs={{0,32},{32,64},{64,96},{96,128},{128,160},{160,192},{192,224},{224... | collective-permute-start | bytes 1572872 | tf_op jit(solution)/shard_map/ppermute | solution.py:190
  62.9 16.0 %collective-permute-start.11 = (f32[128,1024]{1,0:T(8,128)}, f32[128,1024]{1,0:T(8,128)S(1)}, u32[]{:S(2)}, u32[]{:S(2)}) collective-permute-start(f32[128,1024]{1,0:T(8,128)} %collective-permute-done.10.refs_4_), channel_id=1, source_target_pairs={{0,480},{32,0},{64,32},{96,64},{128,96},{160,128},{192,160},{224,1... | collective-permute-start | bytes 1572872 | tf_op jit(solution)/shard_map/ppermute | solution.py:190
  67.5 17.4 %copy-start = (f32[16,32,256]{2,1,0:T(8,128)}, f32[16,32,256]{2,1,0:T(8,128)S(1)}, u32[]{:S(2)}) copy-start(f32[16,32,256]{2,1,0:T(8,128)S(1)} %all-to-all-done.2.refs_3_.b_same.refs_0_) | copy-start | bytes 1572868
  67.5 16.0 %collective-permute-start.2 = (f32[16,32,256]{2,1,0:T(8,128)S(1)}, f32[16,32,256]{2,1,0:T(8,128)S(1)}, u32[]{:S(2)}, u32[]{:S(2)}) collective-permute-start(f32[16,32,256]{2,1,0:T(8,128)S(1)} %all-to-all-done.2.refs_3_.b_same.refs_0_), channel_id=1, source_target_pairs={{0,1},{1,0},{2,3},{3,2},{4,5},{5,4},{6,7},{7,6},{8,9},{9,8},{10,11... | collective-permute-start | bytes 1572872 | tf_op jit(solution)/shard_map/ppermute | solution.py:185
  77.0 7.9 %copy-start.2 = (f32[128,1024]{1,0:T(8,128)}, f32[128,1024]{1,0:T(8,128)S(1)}, u32[]{:S(2)}) copy-start(f32[128,1024]{1,0:T(8,128)S(1)} %collective-permute-done.4.refs_5_) | copy-start | bytes 1572868
  77.0 14.9 %collective-permute-start.6 = (f32[128,1024]{1,0:T(8,128)S(1)}, f32[128,1024]{1,0:T(8,128)S(1)}, u32[]{:S(2)}, u32[]{:S(2)}) collective-permute-start(f32[128,1024]{1,0:T(8,128)S(1)} %collective-permute-done.4.refs_5_), channel_id=1, source_target_pairs={{0,32},{32,64},{64,96},{96,128},{128,160},{160,192},{192,224},{224... | collective-permute-start | bytes 1572872 | tf_op jit(solution)/shard_map/ppermute | solution.py:190
  78.9 5.9 %copy-start.18 = (f32[128,1024]{1,0:T(8,128)}, f32[128,1024]{1,0:T(8,128)S(1)}, u32[]{:S(2)}) copy-start(f32[128,1024]{1,0:T(8,128)S(1)} %collective-permute-done.11.refs_6_) | copy-start | bytes 1572868
  78.9 14.9 %collective-permute-start.12 = (f32[128,1024]{1,0:T(8,128)S(1)}, f32[128,1024]{1,0:T(8,128)}, u32[]{:S(2)}, u32[]{:S(2)}) collective-permute-start(f32[128,1024]{1,0:T(8,128)S(1)} %collective-permute-done.11.refs_6_), channel_id=1, source_target_pairs={{0,480},{32,0},{64,32},{96,64},{128,96},{160,128},{192,160},{224,1... | collective-permute-start | bytes 1572872 | tf_op jit(solution)/shard_map/ppermute | solution.py:190
  83.5 1.3 copy-start.1
  84.8 27.6 %copy-start.8 = (f32[1024,32]{0,1:T(8,128)S(1)}, f32[1024,32]{0,1:T(8,128)}, u32[]{:S(2)}) copy-start(f32[1024,32]{0,1:T(8,128)} %param.14) | copy-start | bytes 393220
  84.9 13.5 %all-to-all-start.3 = ((f32[16,32,256]{2,1,0:T(8,128)}), f32[16,32,256]{2,1,0:T(8,128)S(1)}, u32[]{:S(2)}, u32[]{:S(2)}) async-start(f32[16,32,256]{2,1,0:T(8,128)} %couple.1), calls=%async_computation.3 | async-start | bytes 1048576 | tf_op jit(solution)/shard_map/all_to_all | solution.py:180
  91.9 21.8 %copy-start.19 = (f32[128,1024]{1,0:T(8,128)}, f32[128,1024]{1,0:T(8,128)S(1)}, u32[]{:S(2)}) copy-start(f32[128,1024]{1,0:T(8,128)S(1)} %collective-permute-done.6.refs_7_) | copy-start | bytes 1572868
  91.9 14.0 %collective-permute-start.7 = (f32[128,1024]{1,0:T(8,128)S(1)}, f32[128,1024]{1,0:T(8,128)S(1)}, u32[]{:S(2)}, u32[]{:S(2)}) collective-permute-start(f32[128,1024]{1,0:T(8,128)S(1)} %collective-permute-done.6.refs_7_), channel_id=1, source_target_pairs={{0,32},{32,64},{64,96},{96,128},{128,160},{160,192},{192,224},{224... | collective-permute-start | bytes 1572872 | tf_op jit(solution)/shard_map/ppermute | solution.py:190
  93.8 14.0 %collective-permute-start.13 = (f32[128,1024]{1,0:T(8,128)}, f32[128,1024]{1,0:T(8,128)S(1)}, u32[]{:S(2)}, u32[]{:S(2)}) collective-permute-start(f32[128,1024]{1,0:T(8,128)} %collective-permute-done.12.refs_8_), channel_id=1, source_target_pairs={{0,480},{32,0},{64,32},{96,64},{128,96},{160,128},{192,160},{224,1... | collective-permute-start | bytes 1572872 | tf_op jit(solution)/shard_map/ppermute | solution.py:190
  98.4 14.0 %collective-permute-start.5 = (f32[16,32,256]{2,1,0:T(8,128)S(1)}, f32[16,32,256]{2,1,0:T(8,128)S(1)}, u32[]{:S(2)}, u32[]{:S(2)}) collective-permute-start(f32[16,32,256]{2,1,0:T(8,128)S(1)} %all-to-all-done.3.refs_2_), channel_id=1, source_target_pairs={{0,1},{1,0},{2,3},{3,2},{4,5},{5,4},{6,7},{7,6},{8,9},{9,8},{10,11... | collective-permute-start | bytes 1572872 | tf_op jit(solution)/shard_map/ppermute | solution.py:185
  105.9 7.8 %copy-start.4 = (f32[128,1024]{1,0:T(8,128)}, f32[128,1024]{1,0:T(8,128)S(1)}, u32[]{:S(2)}) copy-start(f32[128,1024]{1,0:T(8,128)S(1)} %collective-permute-done.7.refs_4_.refs_9_) | copy-start | bytes 1572868
  105.9 13.2 %collective-permute-start.14 = (f32[128,1024]{1,0:T(8,128)S(1)}, f32[128,1024]{1,0:T(8,128)}, u32[]{:S(2)}, u32[]{:S(2)}) collective-permute-start(f32[128,1024]{1,0:T(8,128)S(1)} %collective-permute-done.7.refs_4_.refs_9_), channel_id=1, source_target_pairs={{0,32},{32,64},{64,96},{96,128},{128,160},{160,192},{192,224},{224... | collective-permute-start | bytes 1572872 | tf_op jit(solution)/shard_map/ppermute | solution.py:190
  107.8 5.9 %copy-start.20 = (f32[128,1024]{1,0:T(8,128)}, f32[128,1024]{1,0:T(8,128)S(1)}, u32[]{:S(2)}) copy-start(f32[128,1024]{1,0:T(8,128)S(1)} %collective-permute-done.13.refs_10_) | copy-start | bytes 1572868
  107.8 13.1 %collective-permute-start.15 = (f32[128,1024]{1,0:T(8,128)S(1)}, f32[128,1024]{1,0:T(8,128)}, u32[]{:S(2)}, u32[]{:S(2)}) collective-permute-start(f32[128,1024]{1,0:T(8,128)S(1)} %collective-permute-done.13.refs_10_), channel_id=1, source_target_pairs={{0,480},{32,0},{64,32},{96,64},{128,96},{160,128},{192,160},{224,1... | collective-permute-start | bytes 1572872 | tf_op jit(solution)/shard_map/ppermute | solution.py:190
  113.7 12.6 %all-to-all-start.4 = ((f32[16,32,256]{2,1,0:T(8,128)}), f32[16,32,256]{2,1,0:T(8,128)S(1)}, u32[]{:S(2)}, u32[]{:S(2)}) async-start(f32[16,32,256]{2,1,0:T(8,128)} %get-tuple-element.10), calls=%async_computation.4 | async-start | bytes 1048576 | tf_op jit(solution)/shard_map/all_to_all | solution.py:180
  119.0 14.4 %collective-permute-start.16 = (f32[128,1024]{1,0:T(8,128)}, f32[128,1024]{1,0:T(8,128)S(1)}, u32[]{:S(2)}, u32[]{:S(2)}) collective-permute-start(f32[128,1024]{1,0:T(8,128)} %collective-permute-done.14.refs_11_), channel_id=1, source_target_pairs={{0,32},{32,64},{64,96},{96,128},{128,160},{160,192},{192,224},{224... | collective-permute-start | bytes 1572872 | tf_op jit(solution)/shard_map/ppermute | solution.py:190
  121.0 14.4 %collective-permute-start.17 = (f32[128,1024]{1,0:T(8,128)}, f32[128,1024]{1,0:T(8,128)S(1)}, u32[]{:S(2)}, u32[]{:S(2)}) collective-permute-start(f32[128,1024]{1,0:T(8,128)} %collective-permute-done.15.refs_12_), channel_id=1, source_target_pairs={{0,480},{32,0},{64,32},{96,64},{128,96},{160,128},{192,160},{224,1... | collective-permute-start | bytes 1572872 | tf_op jit(solution)/shard_map/ppermute | solution.py:190
  126.3 9.1 %copy-start.13 = (f32[16,32,256]{2,1,0:T(8,128)}, f32[16,32,256]{2,1,0:T(8,128)S(1)}, u32[]{:S(2)}) copy-start(f32[16,32,256]{2,1,0:T(8,128)S(1)} %all-to-all-done.4.a_same.refs_2_) | copy-start | bytes 1572868
  126.3 13.7 %collective-permute-start.8 = (f32[16,32,256]{2,1,0:T(8,128)S(1)}, f32[16,32,256]{2,1,0:T(8,128)S(1)}, u32[]{:S(2)}, u32[]{:S(2)}) collective-permute-start(f32[16,32,256]{2,1,0:T(8,128)S(1)} %all-to-all-done.4.a_same.refs_2_), channel_id=1, source_target_pairs={{0,1},{1,0},{2,3},{3,2},{4,5},{5,4},{6,7},{7,6},{8,9},{9,8},{10,11... | collective-permute-start | bytes 1572872 | tf_op jit(solution)/shard_map/ppermute | solution.py:185
  133.4 2.0 %copy-start.15 = (f32[128,1024]{1,0:T(8,128)}, f32[128,1024]{1,0:T(8,128)S(1)}, u32[]{:S(2)}) copy-start(f32[128,1024]{1,0:T(8,128)S(1)} %collective-permute-done.16.refs_13_) | copy-start | bytes 1572868
  133.4 16.0 %collective-permute-start.18 = (f32[64,1024]{1,0:T(8,128)S(1)}, f32[64,1024]{1,0:T(8,128)S(1)}, u32[]{:S(2)}, u32[]{:S(2)}) collective-permute-start(f32[64,1024]{1,0:T(8,128)S(1)} %slice.8), channel_id=1, source_target_pairs={{0,32},{32,64},{64,96},{96,128},{128,160},{160,192},{192,224},{224... | collective-permute-start | bytes 786440 | tf_op jit(solution)/shard_map/ppermute | solution.py:190
  135.4 4.7 %copy-start.16 = (f32[128,1024]{1,0:T(8,128)}, f32[128,1024]{1,0:T(8,128)S(1)}, u32[]{:S(2)}) copy-start(f32[128,1024]{1,0:T(8,128)S(1)} %collective-permute-done.17.refs_14_) | copy-start | bytes 1572868
  135.4 14.0 %collective-permute-start.19 = (f32[64,1024]{1,0:T(8,128)S(1)}, f32[64,1024]{1,0:T(8,128)S(1)}, u32[]{:S(2)}, u32[]{:S(2)}) collective-permute-start(f32[64,1024]{1,0:T(8,128)S(1)} %slice.9), channel_id=1, source_target_pairs={{0,480},{32,0},{64,32},{96,64},{128,96},{160,128},{192,160},{224,1... | collective-permute-start | bytes 786440 | tf_op jit(solution)/shard_map/ppermute | solution.py:190
  140.0 0.8 copy-start.14
  149.4 0.7 copy-start.21
  150.1 0.7 copy-start.22

commit v5 on v4

--- a/solution.py
+++ b/solution.py
@@ -96,9 +96,9 @@
         at += 2 * shard
 
 
-def near_kernel(planes, offsets, plane_ref, core_ref, b_same, b_other, a_same, a_other, rhs_ref, *refs):
+def near_kernel(planes, offsets, plane_ref, core_ref, b_same, b_other, a_same, a_other, *refs):
     count = len(offsets)
-    row_refs, (out_ref, x_ref, rows_ref, total_ref, semaphores) = refs[:count], refs[count:]
+    row_refs, (total_ref, x_ref, rows_ref, semaphores) = refs[:count], refs[count:]
     block = rows_ref.shape[1]
     copies = [pltpu.make_async_copy(r, rows_ref.at[n], semaphores.at[n]) for n, r in enumerate(row_refs)]
     for copy in copies:
@@ -113,67 +113,68 @@
         rows = rows_ref[n:last].reshape((last - n) * block, rows_ref.shape[2])
         part = product(x_ref[n * block : last * block].T, rows)
         total_ref[...] = part if n == 0 else total_ref[...] + part
-    out_ref[...] = rhs_ref[...] - total_ref[...].T
-
-
-def update_near(plane, core, x, rhs, blocks, offsets, planes):
-    height, width = rhs.shape
+
+
+def update_near(plane, core, x, blocks, offsets, planes):
+    height, width = blocks[0].shape[1], x[0].shape[2]
     vmem, smem = pl.BlockSpec(memory_space=pltpu.VMEM), pl.BlockSpec(memory_space=pltpu.SMEM)
     count, block = len(blocks), blocks[0].shape[0]
     return pl.pallas_call(
         functools.partial(near_kernel, planes, offsets),
-        out_shape=jax.ShapeDtypeStruct((height, width), F32),
-        in_specs=[smem] * 2 + [vmem] * (len(x) + 1) + [pl.BlockSpec(memory_space=pl.ANY)] * count,
+        out_shape=jax.ShapeDtypeStruct((width, height), F32),
+        in_specs=[smem] * 2 + [vmem] * len(x) + [pl.BlockSpec(memory_space=pl.ANY)] * count,
         out_specs=vmem,
         scratch_shapes=[
             pltpu.VMEM((count * block, width), F32),
             pltpu.VMEM((count, block, height), F32),
-            pltpu.VMEM((width, height), F32),
             pltpu.SemaphoreType.DMA((count,)),
         ],
         compiler_params=pltpu.CompilerParams(vmem_limit_bytes=UPDATE_LIMIT),
         name="update_near",
-    )(plane, core, *x, rhs, *blocks)
+    )(plane, core, *x, *blocks)
 
 
 def far_kernel(planes, plane_ref, core_ref, *refs):
-    x_refs, rhs_in, row_refs = refs[:4], refs[4], refs[5:-6]
-    out_ref, parts_ref, x_ref, rhs_ref, rows_ref, semaphores = refs[-6:]
+    x_refs, rhs_in, total_in, row_refs = refs[:4], refs[4], refs[5], refs[6:-7]
+    out_ref, parts_ref, x_ref, rhs_ref, total_ref, rows_ref, semaphores = refs[-7:]
     place = lax.rem(plane_ref[0] + planes // 2, planes)
     lines = row_refs[0].shape[0]
     pairs = [(r.at[pl.ds(place, 1)], parts_ref.at[pl.ds(n, 1)]) for n, r in enumerate(x_refs)]
-    pairs += [(r, rows_ref.at[pl.ds(n * lines, lines)]) for n, r in enumerate(row_refs)] + [(rhs_in, rhs_ref)]
+    pairs += [(r, rows_ref.at[pl.ds(n * lines, lines)]) for n, r in enumerate(row_refs)] + [(total_in, total_ref), (rhs_in, rhs_ref)]
     copies = [pltpu.make_async_copy(*pair, semaphores.at[n]) for n, pair in enumerate(pairs)]
     for copy in copies:
         copy.start()
-    for copy in copies[:-1]:
+    for copy in copies[:-2]:
         copy.wait()
     parts = [parts_ref.at[pl.ds(n, 1)] for n in range(4)]
     gather_x((parts[:2], parts[2:]), 0, core_ref[0], x_ref, 0)
-    part = product(x_ref[...].T, rows_ref[...]).T
+    part = product(x_ref[...].T, rows_ref[...])
+    copies[-2].wait()
+    part = (part + total_ref[...]).T
     copies[-1].wait()
     out_ref[...] = rhs_ref[...] - part
 
 
-def update_far(plane, core, x, rhs, blocks, planes):
+def update_far(plane, core, x, rhs, total, blocks, planes):
     vmem, smem, whole = (pl.BlockSpec(memory_space=m) for m in (pltpu.VMEM, pltpu.SMEM, pl.ANY))
     height, width = rhs.shape
     depth = sum(b.shape[0] for b in blocks)
     return pl.pallas_call(
         functools.partial(far_kernel, planes),
         out_shape=jax.ShapeDtypeStruct(rhs.shape, F32),
-        in_specs=[smem] * 2 + [whole] * (len(x) + 1 + len(blocks)),
+        in_specs=[smem] * 2 + [whole] * (len(x) + 2 + len(blocks)),
         out_specs=vmem,
         scratch_shapes=[
             pltpu.VMEM((len(x),) + x[0].shape[1:], F32),
             pltpu.VMEM((depth, width), F32),
             pltpu.VMEM(rhs.shape, F32),
+            pltpu.VMEM(total.shape, F32),
             pltpu.VMEM((depth, height), F32),
-            pltpu.SemaphoreType.DMA((len(x) + len(blocks) + 1,)),
+            pltpu.SemaphoreType.DMA((len(x) + len(blocks) + 2,)),
         ],
         compiler_params=pltpu.CompilerParams(vmem_limit_bytes=UPDATE_LIMIT),
         name="update_far",
-    )(plane, core, *x, rhs, *blocks)
+    )(plane, core, *x, rhs, total, *blocks)
 
 
 def exchange(copies, axis):
@@ -225,8 +226,8 @@
             solve, [local, copies], [core, inverse_a.T, *spread(coupled)], after=blocks[9:10], scratch=[whole]
         )
         x = x_b_all + spread(x_copies)
-        partial = update_near(plane, core, x, rhs_above, blocks[:-2], offsets[:-1], planes)
-        return x_b, x_a, update_far(plane, core, x, partial, blocks[-2:], planes)
+        total = update_near(plane, core, x, blocks[:-2], offsets[:-1], planes)
+        return x_b, x_a, update_far(plane, core, x, rhs_above, total, blocks[-2:], planes)
 
     return shards
 

time: 157 us -> 156 us (level)
  transfers between devices with their start and end apart: 25 -> 25, of which waited for: 7 -> 7; matrix products, arithmetic and copies ran while one was open for 0% -> 0% of each run, Pallas kernels for 9% -> 8%
where the time goes in v5:
time: 156 us; the launch traced here: 154 us
  starting transfers between devices  110 us (71%)
  waiting for transfers between devices  22.6 us (14%)
  Pallas kernels  16.8 us (11%)
  local copies, waits for them, and re-layouts  3.03 us (2%)
    ppermute x16, starting transfers between devices, move(): lax.ppermute(block, 'row', [(i, (i + by) % planes) for i in range(planes)])  58.4 us
    all_to_all x5, starting transfers between devices, exchange(): return lax.all_to_all(copies, axis, 0, 0, tiled=True)  31.7 us
    ppermute x4, starting transfers between devices, spread(): return (same, lax.ppermute(same, 'core', [(0, 1), (1, 0)]))  19.8 us
    ppermute x16, waiting for transfers between devices, move(): lax.ppermute(block, 'row', [(i, (i + by) % planes) for i in range(planes)])  15.9 us
    pallas_call x1, Pallas kernels, update_near(): pl.pallas_call(functools.partial(near_kernel, planes, offsets), out_shape...  8.07 us
    all_to_all x5, waiting for transfers between devices, exchange(): return lax.all_to_all(copies, axis, 0, 0, tiled=True)  6.68 us
    pallas_call x6, Pallas kernels, call(): pl.pallas_call(body, out_shape=[jax.ShapeDtypeStruct(s, F32) for s in sha...  5.48 us
    pallas_call x1, Pallas kernels, update_far(): pl.pallas_call(functools.partial(far_kernel, planes), out_shape=jax.Shape...  3.21 us
  transfers between devices with their start and end apart: 25, of which 7 were waited for; matrix products, arithmetic and copies ran while one was open for 0% of the time, Pallas kernels for 8%

profile of v5, /device:TPU:1, one launch (start us, length us, event | category | flops | bytes accessed | tf_op | source)
XLA Modules:
  0.0 153.5 jit_solution(1296359581871138981)
XLA Ops:
  0.6 0.7 copy-done.11
  1.4 0.8 send.1
  2.2 7.7 %all-to-all-start = ((f32[16,32,256]{2,1,0:T(8,128)}), f32[16,32,256]{2,1,0:T(8,128)S(1)}, u32[]{:S(2)}, u32[]{:S(2)}) async-start(f32[16,32,256]{2,1,0:T(8,128)} %send.1), calls=%async_computation | async-start | bytes 1048576 | tf_op jit(solution)/shard_map/all_to_all | solution.py:181
  10.0 0.0 copy-start.12
  10.0 3.5 %collective-permute-start.1 = (f32[128,1024]{1,0:T(8,128)S(1)}, f32[128,1024]{1,0:T(8,128)S(1)}, u32[]{:S(2)}, u32[]{:S(2)}) collective-permute-start(f32[128,1024]{1,0:T(8,128)S(1)} %join.1.refs_0_), channel_id=1, source_target_pairs={{0,32},{32,64},{64,96},{96,128},{128,160},{160,192},{192,224},{224... | collective-permute-start | bytes 1572872 | tf_op jit(solution)/shard_map/ppermute | solution.py:191
  13.6 9.5 %collective-permute-start.9 = (f32[128,1024]{1,0:T(8,128)S(1)}, f32[128,1024]{1,0:T(8,128)S(1)}, u32[]{:S(2)}, u32[]{:S(2)}) collective-permute-start(f32[128,1024]{1,0:T(8,128)S(1)} %join.1.refs_0_), channel_id=1, source_target_pairs={{0,480},{32,0},{64,32},{96,64},{128,96},{160,128},{192,160},{224,1... | collective-permute-start | bytes 1572872 | tf_op jit(solution)/shard_map/ppermute | solution.py:191
  23.1 0.0 all-to-all-done.refs_2_
  23.1 3.1 %collective-permute-start = (f32[16,32,256]{2,1,0:T(8,128)S(1)}, f32[16,32,256]{2,1,0:T(8,128)S(1)}, u32[]{:S(2)}, u32[]{:S(2)}) collective-permute-start(f32[16,32,256]{2,1,0:T(8,128)S(1)} %all-to-all-done.refs_2_), channel_id=1, source_target_pairs={{0,1},{1,0},{2,3},{3,2},{4,5},{5,4},{6,7},{7,6},{8,9},{9,8},{10,11... | collective-permute-start | bytes 1572872 | tf_op jit(solution)/shard_map/ppermute | solution.py:186
  26.3 0.7 begin.1
  27.0 13.1 %all-to-all-start.1 = ((f32[16,16,128]{2,1,0:T(8,128)}), f32[16,16,128]{2,1,0:T(8,128)S(1)}, u32[]{:S(2)}, u32[]{:S(2)}) async-start(f32[16,16,128]{2,1,0:T(8,128)} %begin.1), calls=%async_computation.1 | async-start | bytes 262144 | tf_op jit(solution)/shard_map/all_to_all | solution.py:181
  40.2 0.0 collective-permute-done.1.refs_4_.refs_1_
  40.2 3.3 %collective-permute-start.3 = (f32[128,1024]{1,0:T(8,128)S(1)}, f32[128,1024]{1,0:T(8,128)}, u32[]{:S(2)}, u32[]{:S(2)}) collective-permute-start(f32[128,1024]{1,0:T(8,128)S(1)} %collective-permute-done.1.refs_4_.refs_1_), channel_id=1, source_target_pairs={{0,32},{32,64},{64,96},{96,128},{128,160},{160,192},{192,224},{224... | collective-permute-start | bytes 1572872 | tf_op jit(solution)/shard_map/ppermute | solution.py:191
  43.5 0.0 collective-permute-done.9.refs_2_
  43.5 3.2 %collective-permute-start.10 = (f32[128,1024]{1,0:T(8,128)S(1)}, f32[128,1024]{1,0:T(8,128)}, u32[]{:S(2)}, u32[]{:S(2)}) collective-permute-start(f32[128,1024]{1,0:T(8,128)S(1)} %collective-permute-done.9.refs_2_), channel_id=1, source_target_pairs={{0,480},{32,0},{64,32},{96,64},{128,96},{160,128},{192,160},{224,1... | collective-permute-start | bytes 1572872 | tf_op jit(solution)/shard_map/ppermute | solution.py:191
  46.7 5.9 %all-to-all-done.1.refs_5_.refs_2_ = f32[16,16,128]{2,1,0:T(8,128)S(1)} async-done(((f32[16,16,128]{2,1,0:T(8,128)}), f32[16,16,128]{2,1,0:T(8,128)S(1)}, u32[]{:S(2)}, u32[]{:S(2)}) %all-to-all-start.1) | async-done | bytes 131104 | tf_op jit(solution)/shard_map/all_to_all | solution.py:181
  52.6 0.0 collective-permute-done.refs_3_
  52.6 1.3 solve.2
  53.9 0.0 copy-start.10
  53.9 3.6 %all-to-all-start.2 = ((f32[16,32,256]{2,1,0:T(8,128)}), f32[16,32,256]{2,1,0:T(8,128)S(1)}, u32[]{:S(2)}, u32[]{:S(2)}) async-start(f32[16,32,256]{2,1,0:T(8,128)} %get-tuple-element.8), calls=%async_computation.2 | async-start | bytes 1048576 | tf_op jit(solution)/shard_map/all_to_all | solution.py:181
  57.5 3.4 %collective-permute-done.3.refs_3_ = f32[128,1024]{1,0:T(8,128)} collective-permute-done((f32[128,1024]{1,0:T(8,128)S(1)}, f32[128,1024]{1,0:T(8,128)}, u32[]{:S(2)}, u32[]{:S(2)}) %collective-permute-start.3) | collective-permute-done | bytes 524320 | tf_op jit(solution)/shard_map/ppermute | solution.py:191
  60.9 1.9 %collective-permute-start.4 = (f32[128,1024]{1,0:T(8,128)}, f32[128,1024]{1,0:T(8,128)S(1)}, u32[]{:S(2)}, u32[]{:S(2)}) collective-permute-start(f32[128,1024]{1,0:T(8,128)} %collective-permute-done.3.refs_3_), channel_id=1, source_target_pairs={{0,32},{32,64},{64,96},{96,128},{128,160},{160,192},{192,224},{224... | collective-permute-start | bytes 1572872 | tf_op jit(solution)/shard_map/ppermute | solution.py:191
  62.9 0.0 collective-permute-done.10.refs_4_
  62.9 4.6 %collective-permute-start.11 = (f32[128,1024]{1,0:T(8,128)}, f32[128,1024]{1,0:T(8,128)S(1)}, u32[]{:S(2)}, u32[]{:S(2)}) collective-permute-start(f32[128,1024]{1,0:T(8,128)} %collective-permute-done.10.refs_4_), channel_id=1, source_target_pairs={{0,480},{32,0},{64,32},{96,64},{128,96},{160,128},{192,160},{224,1... | collective-permute-start | bytes 1572872 | tf_op jit(solution)/shard_map/ppermute | solution.py:191
  67.5 0.0 all-to-all-done.2.refs_3_.b_same.refs_0_
  67.5 4.6 %collective-permute-start.2 = (f32[16,32,256]{2,1,0:T(8,128)S(1)}, f32[16,32,256]{2,1,0:T(8,128)S(1)}, u32[]{:S(2)}, u32[]{:S(2)}) collective-permute-start(f32[16,32,256]{2,1,0:T(8,128)S(1)} %all-to-all-done.2.refs_3_.b_same.refs_0_), channel_id=1, source_target_pairs={{0,1},{1,0},{2,3},{3,2},{4,5},{5,4},{6,7},{7,6},{8,9},{9,8},{10,11... | collective-permute-start | bytes 1572872 | tf_op jit(solution)/shard_map/ppermute | solution.py:186
  72.0 4.9 %collective-permute-done.4.refs_5_ = f32[128,1024]{1,0:T(8,128)S(1)} collective-permute-done((f32[128,1024]{1,0:T(8,128)}, f32[128,1024]{1,0:T(8,128)S(1)}, u32[]{:S(2)}, u32[]{:S(2)}) %collective-permute-start.4) | collective-permute-done | bytes 524320 | tf_op jit(solution)/shard_map/ppermute | solution.py:191
  77.0 1.9 %collective-permute-start.6 = (f32[128,1024]{1,0:T(8,128)S(1)}, f32[128,1024]{1,0:T(8,128)S(1)}, u32[]{:S(2)}, u32[]{:S(2)}) collective-permute-start(f32[128,1024]{1,0:T(8,128)S(1)} %collective-permute-done.4.refs_5_), channel_id=1, source_target_pairs={{0,32},{32,64},{64,96},{96,128},{128,160},{160,192},{192,224},{224... | collective-permute-start | bytes 1572872 | tf_op jit(solution)/shard_map/ppermute | solution.py:191
  78.9 0.0 collective-permute-done.11.refs_6_
  78.9 4.6 %collective-permute-start.12 = (f32[128,1024]{1,0:T(8,128)S(1)}, f32[128,1024]{1,0:T(8,128)}, u32[]{:S(2)}, u32[]{:S(2)}) collective-permute-start(f32[128,1024]{1,0:T(8,128)S(1)} %collective-permute-done.11.refs_6_), channel_id=1, source_target_pairs={{0,480},{32,0},{64,32},{96,64},{128,96},{160,128},{192,160},{224,1... | collective-permute-start | bytes 1572872 | tf_op jit(solution)/shard_map/ppermute | solution.py:191
  83.5 0.0 collective-permute-done.2.refs_4_.b_other.refs_1_
  83.5 1.3 couple.1
  84.8 0.0 copy-start.8
  84.9 3.7 %all-to-all-start.3 = ((f32[16,32,256]{2,1,0:T(8,128)}), f32[16,32,256]{2,1,0:T(8,128)S(1)}, u32[]{:S(2)}, u32[]{:S(2)}) async-start(f32[16,32,256]{2,1,0:T(8,128)} %couple.1), calls=%async_computation.3 | async-start | bytes 1048576 | tf_op jit(solution)/shard_map/all_to_all | solution.py:181
  88.6 3.3 %collective-permute-done.6.refs_7_ = f32[128,1024]{1,0:T(8,128)S(1)} collective-permute-done((f32[128,1024]{1,0:T(8,128)S(1)}, f32[128,1024]{1,0:T(8,128)S(1)}, u32[]{:S(2)}, u32[]{:S(2)}) %collective-permute-start.6) | collective-permute-done | bytes 524320 | tf_op jit(solution)/shard_map/ppermute | solution.py:191
  91.9 1.9 %collective-permute-start.7 = (f32[128,1024]{1,0:T(8,128)S(1)}, f32[128,1024]{1,0:T(8,128)S(1)}, u32[]{:S(2)}, u32[]{:S(2)}) collective-permute-start(f32[128,1024]{1,0:T(8,128)S(1)} %collective-permute-done.6.refs_7_), channel_id=1, source_target_pairs={{0,32},{32,64},{64,96},{96,128},{128,160},{160,192},{192,224},{224... | collective-permute-start | bytes 1572872 | tf_op jit(solution)/shard_map/ppermute | solution.py:191
  93.8 0.0 collective-permute-done.12.refs_8_
  93.8 4.6 %collective-permute-start.13 = (f32[128,1024]{1,0:T(8,128)}, f32[128,1024]{1,0:T(8,128)S(1)}, u32[]{:S(2)}, u32[]{:S(2)}) collective-permute-start(f32[128,1024]{1,0:T(8,128)} %collective-permute-done.12.refs_8_), channel_id=1, source_target_pairs={{0,480},{32,0},{64,32},{96,64},{128,96},{160,128},{192,160},{224,1... | collective-permute-start | bytes 1572872 | tf_op jit(solution)/shard_map/ppermute | solution.py:191
  98.4 0.0 all-to-all-done.3.refs_2_
  98.4 5.0 %collective-permute-start.5 = (f32[16,32,256]{2,1,0:T(8,128)S(1)}, f32[16,32,256]{2,1,0:T(8,128)S(1)}, u32[]{:S(2)}, u32[]{:S(2)}) collective-permute-start(f32[16,32,256]{2,1,0:T(8,128)S(1)} %all-to-all-done.3.refs_2_), channel_id=1, source_target_pairs={{0,1},{1,0},{2,3},{3,2},{4,5},{5,4},{6,7},{7,6},{8,9},{9,8},{10,11... | collective-permute-start | bytes 1572872 | tf_op jit(solution)/shard_map/ppermute | solution.py:186
  103.4 2.5 %collective-permute-done.7.refs_4_.refs_9_ = f32[128,1024]{1,0:T(8,128)S(1)} collective-permute-done((f32[128,1024]{1,0:T(8,128)S(1)}, f32[128,1024]{1,0:T(8,128)S(1)}, u32[]{:S(2)}, u32[]{:S(2)}) %collective-permute-start.7) | collective-permute-done | bytes 524320 | tf_op jit(solution)/shard_map/ppermute | solution.py:191
  105.9 1.9 %collective-permute-start.14 = (f32[128,1024]{1,0:T(8,128)S(1)}, f32[128,1024]{1,0:T(8,128)}, u32[]{:S(2)}, u32[]{:S(2)}) collective-permute-start(f32[128,1024]{1,0:T(8,128)S(1)} %collective-permute-done.7.refs_4_.refs_9_), channel_id=1, source_target_pairs={{0,32},{32,64},{64,96},{96,128},{128,160},{160,192},{192,224},{224... | collective-permute-start | bytes 1572872 | tf_op jit(solution)/shard_map/ppermute | solution.py:191
  107.8 0.0 collective-permute-done.13.refs_10_
  107.8 4.6 %collective-permute-start.15 = (f32[128,1024]{1,0:T(8,128)S(1)}, f32[128,1024]{1,0:T(8,128)}, u32[]{:S(2)}, u32[]{:S(2)}) collective-permute-start(f32[128,1024]{1,0:T(8,128)S(1)} %collective-permute-done.13.refs_10_), channel_id=1, source_target_pairs={{0,480},{32,0},{64,32},{96,64},{128,96},{160,128},{192,160},{224,1... | collective-permute-start | bytes 1572872 | tf_op jit(solution)/shard_map/ppermute | solution.py:191
  112.4 0.0 collective-permute-done.5.refs_3_
  112.4 1.3 solve.3
  113.7 3.6 %all-to-all-start.4 = ((f32[16,32,256]{2,1,0:T(8,128)}), f32[16,32,256]{2,1,0:T(8,128)S(1)}, u32[]{:S(2)}, u32[]{:S(2)}) async-start(f32[16,32,256]{2,1,0:T(8,128)} %get-tuple-element.10), calls=%async_computation.4 | async-start | bytes 1048576 | tf_op jit(solution)/shard_map/all_to_all | solution.py:181
  117.3 1.7 %collective-permute-done.14.refs_11_ = f32[128,1024]{1,0:T(8,128)} collective-permute-done((f32[128,1024]{1,0:T(8,128)S(1)}, f32[128,1024]{1,0:T(8,128)}, u32[]{:S(2)}, u32[]{:S(2)}) %collective-permute-start.14) | collective-permute-done | bytes 524320 | tf_op jit(solution)/shard_map/ppermute | solution.py:191
  119.0 1.9 %collective-permute-start.16 = (f32[128,1024]{1,0:T(8,128)}, f32[128,1024]{1,0:T(8,128)S(1)}, u32[]{:S(2)}, u32[]{:S(2)}) collective-permute-start(f32[128,1024]{1,0:T(8,128)} %collective-permute-done.14.refs_11_), channel_id=1, source_target_pairs={{0,32},{32,64},{64,96},{96,128},{128,160},{160,192},{192,224},{224... | collective-permute-start | bytes 1572872 | tf_op jit(solution)/shard_map/ppermute | solution.py:191
  121.0 0.0 collective-permute-done.15.refs_12_
  121.0 4.6 %collective-permute-start.17 = (f32[128,1024]{1,0:T(8,128)}, f32[128,1024]{1,0:T(8,128)S(1)}, u32[]{:S(2)}, u32[]{:S(2)}) collective-permute-start(f32[128,1024]{1,0:T(8,128)} %collective-permute-done.15.refs_12_), channel_id=1, source_target_pairs={{0,480},{32,0},{64,32},{96,64},{128,96},{160,128},{192,160},{224,1... | collective-permute-start | bytes 1572872 | tf_op jit(solution)/shard_map/ppermute | solution.py:191
  125.5 0.8 all-to-all-done.4.a_same.refs_2_
  126.3 7.0 %collective-permute-start.8 = (f32[16,32,256]{2,1,0:T(8,128)S(1)}, f32[16,32,256]{2,1,0:T(8,128)S(1)}, u32[]{:S(2)}, u32[]{:S(2)}) collective-permute-start(f32[16,32,256]{2,1,0:T(8,128)S(1)} %all-to-all-done.4.a_same.refs_2_), channel_id=1, source_target_pairs={{0,1},{1,0},{2,3},{3,2},{4,5},{5,4},{6,7},{7,6},{8,9},{9,8},{10,11... | collective-permute-start | bytes 1572872 | tf_op jit(solution)/shard_map/ppermute | solution.py:186
  133.4 0.0 collective-permute-done.16.refs_13_
  133.4 0.0 copy-start.15
  133.4 1.9 %collective-permute-start.18 = (f32[64,1024]{1,0:T(8,128)S(1)}, f32[64,1024]{1,0:T(8,128)S(1)}, u32[]{:S(2)}, u32[]{:S(2)}) collective-permute-start(f32[64,1024]{1,0:T(8,128)S(1)} %slice.8), channel_id=1, source_target_pairs={{0,32},{32,64},{64,96},{96,128},{128,160},{160,192},{192,224},{224... | collective-permute-start | bytes 786440 | tf_op jit(solution)/shard_map/ppermute | solution.py:191
  135.4 0.0 collective-permute-done.17.refs_14_
  135.4 4.6 %collective-permute-start.19 = (f32[64,1024]{1,0:T(8,128)S(1)}, f32[64,1024]{1,0:T(8,128)S(1)}, u32[]{:S(2)}, u32[]{:S(2)}) collective-permute-start(f32[64,1024]{1,0:T(8,128)S(1)} %slice.9), channel_id=1, source_target_pairs={{0,480},{32,0},{64,32},{96,64},{128,96},{160,128},{192,160},{224,1... | collective-permute-start | bytes 786440 | tf_op jit(solution)/shard_map/ppermute | solution.py:191
  140.0 0.0 collective-permute-done.8.a_other.refs_3_
  140.0 0.8 copy-done.14
  140.8 8.1 %update_near.1.refs_5_ = f32[256,1024]{1,0:T(8,128)} custom-call(s32[1]{0:T(128)} %bitcast.4.plane_ref, s32[1]{0:T(128)} %bitcast.refs_0_.core_ref, f32[16,32,256]{2,1,0:T(8,128)} %copy-done, f32[16,32,256]{2,1,0:T(8,128)} %copy-done.1, f32[16,32,256]{2,1,0:T(8,128)} %copy-done.13, f32[16,32,256]{2,1,0:T(8,128)} %copy-done.14, f32[128,1024]{1,0:T(8,128)} %copy-done.3, ...), custom_call_target="tpu_custom_call" | custom-call | tf_op jit(solution)/shard_map/update_near/pallas_call | solution.py:122
  148.9 0.0 collective-permute-done.18.refs_6_
  148.9 0.7 copy-done.21
  149.6 0.7 copy-done.22
  150.3 3.2 %update_far.1 = f32[1024,256]{1,0:T(8,128)} custom-call(s32[1]{0:T(128)} %bitcast.4.plane_ref, s32[1]{0:T(128)} %bitcast.refs_0_.core_ref, f32[16,32,256]{2,1,0:T(8,128)} %copy-done, f32[16,32,256]{2,1,0:T(8,128)} %copy-done.1, f32[16,32,256]{2,1,0:T(8,128)} %copy-done.13, f32[16,32,256]{2,1,0:T(8,128)} %copy-done.14, f32[1024,256]{1,0:T(8,128)} %refs_4_.1, ...), custom_call_target="tpu_custom_call" | custom-call | tf_op jit(solution)/shard_map/update_far/pallas_call | solution.py:162
  (42 shorter events, 0.2 us)
Async XLA Ops:
  0.6 0.8 copy-start.11
  2.2 7.7 %copy-start.6 = (f32[64,1024]{1,0:T(8,128)S(1)}, f32[64,1024]{1,0:T(8,128)}, u32[]{:S(2)}) copy-start(f32[64,1024]{1,0:T(8,128)} %refs_0_.3) | copy-start | bytes 786436
  2.2 7.7 %copy-start.7 = (f32[64,1024]{1,0:T(8,128)S(1)}, f32[64,1024]{1,0:T(8,128)}, u32[]{:S(2)}) copy-start(f32[64,1024]{1,0:T(8,128)} %refs_1_.2) | copy-start | bytes 786436
  2.2 20.9 %all-to-all-start = ((f32[16,32,256]{2,1,0:T(8,128)}), f32[16,32,256]{2,1,0:T(8,128)S(1)}, u32[]{:S(2)}, u32[]{:S(2)}) async-start(f32[16,32,256]{2,1,0:T(8,128)} %send.1), calls=%async_computation | async-start | bytes 1048576 | tf_op jit(solution)/shard_map/all_to_all | solution.py:181
  10.0 16.3 %copy-start.12 = (f32[64,32]{0,1:T(8,128)S(1)}, f32[64,32]{0,1:T(8,128)}, u32[]{:S(2)}) copy-start(f32[64,32]{0,1:T(8,128)} %param.13) | copy-start | bytes 24580
  10.0 43.9 %copy-start.3 = (f32[128,1024]{1,0:T(8,128)}, f32[128,1024]{1,0:T(8,128)S(1)}, u32[]{:S(2)}) copy-start(f32[128,1024]{1,0:T(8,128)S(1)} %join.1.refs_0_) | copy-start | bytes 1572868
  10.0 30.1 %collective-permute-start.1 = (f32[128,1024]{1,0:T(8,128)S(1)}, f32[128,1024]{1,0:T(8,128)S(1)}, u32[]{:S(2)}, u32[]{:S(2)}) collective-permute-start(f32[128,1024]{1,0:T(8,128)S(1)} %join.1.refs_0_), channel_id=1, source_target_pairs={{0,32},{32,64},{64,96},{96,128},{128,160},{160,192},{192,224},{224... | collective-permute-start | bytes 1572872 | tf_op jit(solution)/shard_map/ppermute | solution.py:191
  13.6 29.9 %collective-permute-start.9 = (f32[128,1024]{1,0:T(8,128)S(1)}, f32[128,1024]{1,0:T(8,128)S(1)}, u32[]{:S(2)}, u32[]{:S(2)}) collective-permute-start(f32[128,1024]{1,0:T(8,128)S(1)} %join.1.refs_0_), channel_id=1, source_target_pairs={{0,480},{32,0},{64,32},{96,64},{128,96},{160,128},{192,160},{224,1... | collective-permute-start | bytes 1572872 | tf_op jit(solution)/shard_map/ppermute | solution.py:191
  23.1 29.5 %collective-permute-start = (f32[16,32,256]{2,1,0:T(8,128)S(1)}, f32[16,32,256]{2,1,0:T(8,128)S(1)}, u32[]{:S(2)}, u32[]{:S(2)}) collective-permute-start(f32[16,32,256]{2,1,0:T(8,128)S(1)} %all-to-all-done.refs_2_), channel_id=1, source_target_pairs={{0,1},{1,0},{2,3},{3,2},{4,5},{5,4},{6,7},{7,6},{8,9},{9,8},{10,11... | collective-permute-start | bytes 1572872 | tf_op jit(solution)/shard_map/ppermute | solution.py:186
  27.0 25.6 %copy-start.9 = (f32[1024,32]{0,1:T(8,128)S(1)}, f32[1024,32]{0,1:T(8,128)}, u32[]{:S(2)}) copy-start(f32[1024,32]{0,1:T(8,128)} %param.15) | copy-start | bytes 393220
  27.0 25.6 %all-to-all-start.1 = ((f32[16,16,128]{2,1,0:T(8,128)}), f32[16,16,128]{2,1,0:T(8,128)S(1)}, u32[]{:S(2)}, u32[]{:S(2)}) async-start(f32[16,16,128]{2,1,0:T(8,128)} %begin.1), calls=%async_computation.1 | async-start | bytes 262144 | tf_op jit(solution)/shard_map/all_to_all | solution.py:181
  40.2 13.7 %copy-start.5 = (f32[128,1024]{1,0:T(8,128)}, f32[128,1024]{1,0:T(8,128)S(1)}, u32[]{:S(2)}) copy-start(f32[128,1024]{1,0:T(8,128)S(1)} %collective-permute-done.1.refs_4_.refs_1_) | copy-start | bytes 1572868
  40.2 20.8 %collective-permute-start.3 = (f32[128,1024]{1,0:T(8,128)S(1)}, f32[128,1024]{1,0:T(8,128)}, u32[]{:S(2)}, u32[]{:S(2)}) collective-permute-start(f32[128,1024]{1,0:T(8,128)S(1)} %collective-permute-done.1.refs_4_.refs_1_), channel_id=1, source_target_pairs={{0,32},{32,64},{64,96},{96,128},{128,160},{160,192},{192,224},{224... | collective-permute-start | bytes 1572872 | tf_op jit(solution)/shard_map/ppermute | solution.py:191
  43.5 10.4 %copy-start.17 = (f32[128,1024]{1,0:T(8,128)}, f32[128,1024]{1,0:T(8,128)S(1)}, u32[]{:S(2)}) copy-start(f32[128,1024]{1,0:T(8,128)S(1)} %collective-permute-done.9.refs_2_) | copy-start | bytes 1572868
  43.5 19.4 %collective-permute-start.10 = (f32[128,1024]{1,0:T(8,128)S(1)}, f32[128,1024]{1,0:T(8,128)}, u32[]{:S(2)}, u32[]{:S(2)}) collective-permute-start(f32[128,1024]{1,0:T(8,128)S(1)} %collective-permute-done.9.refs_2_), channel_id=1, source_target_pairs={{0,480},{32,0},{64,32},{96,64},{128,96},{160,128},{192,160},{224,1... | collective-permute-start | bytes 1572872 | tf_op jit(solution)/shard_map/ppermute | solution.py:191
  53.9 29.6 %copy-start.10 = (f32[32,256]{1,0:T(8,128)S(1)}, f32[32,256]{1,0:T(8,128)}, u32[]{:S(2)}) copy-start(f32[32,256]{1,0:T(8,128)} %refs_1_.3) | copy-start | bytes 98308
  53.9 13.5 %all-to-all-start.2 = ((f32[16,32,256]{2,1,0:T(8,128)}), f32[16,32,256]{2,1,0:T(8,128)S(1)}, u32[]{:S(2)}, u32[]{:S(2)}) async-start(f32[16,32,256]{2,1,0:T(8,128)} %get-tuple-element.8), calls=%async_computation.2 | async-start | bytes 1048576 | tf_op jit(solution)/shard_map/all_to_all | solution.py:181
  60.9 16.0 %collective-permute-start.4 = (f32[128,1024]{1,0:T(8,128)}, f32[128,1024]{1,0:T(8,128)S(1)}, u32[]{:S(2)}, u32[]{:S(2)}) collective-permute-start(f32[128,1024]{1,0:T(8,128)} %collective-permute-done.3.refs_3_), channel_id=1, source_target_pairs={{0,32},{32,64},{64,96},{96,128},{128,160},{160,192},{192,224},{224... | collective-permute-start | bytes 1572872 | tf_op jit(solution)/shard_map/ppermute | solution.py:191
  62.9 16.0 %collective-permute-start.11 = (f32[128,1024]{1,0:T(8,128)}, f32[128,1024]{1,0:T(8,128)S(1)}, u32[]{:S(2)}, u32[]{:S(2)}) collective-permute-start(f32[128,1024]{1,0:T(8,128)} %collective-permute-done.10.refs_4_), channel_id=1, source_target_pairs={{0,480},{32,0},{64,32},{96,64},{128,96},{160,128},{192,160},{224,1... | collective-permute-start | bytes 1572872 | tf_op jit(solution)/shard_map/ppermute | solution.py:191
  67.5 17.4 %copy-start = (f32[16,32,256]{2,1,0:T(8,128)}, f32[16,32,256]{2,1,0:T(8,128)S(1)}, u32[]{:S(2)}) copy-start(f32[16,32,256]{2,1,0:T(8,128)S(1)} %all-to-all-done.2.refs_3_.b_same.refs_0_) | copy-start | bytes 1572868
  67.5 16.0 %collective-permute-start.2 = (f32[16,32,256]{2,1,0:T(8,128)S(1)}, f32[16,32,256]{2,1,0:T(8,128)S(1)}, u32[]{:S(2)}, u32[]{:S(2)}) collective-permute-start(f32[16,32,256]{2,1,0:T(8,128)S(1)} %all-to-all-done.2.refs_3_.b_same.refs_0_), channel_id=1, source_target_pairs={{0,1},{1,0},{2,3},{3,2},{4,5},{5,4},{6,7},{7,6},{8,9},{9,8},{10,11... | collective-permute-start | bytes 1572872 | tf_op jit(solution)/shard_map/ppermute | solution.py:186
  77.0 7.9 %copy-start.2 = (f32[128,1024]{1,0:T(8,128)}, f32[128,1024]{1,0:T(8,128)S(1)}, u32[]{:S(2)}) copy-start(f32[128,1024]{1,0:T(8,128)S(1)} %collective-permute-done.4.refs_5_) | copy-start | bytes 1572868
  77.0 14.9 %collective-permute-start.6 = (f32[128,1024]{1,0:T(8,128)S(1)}, f32[128,1024]{1,0:T(8,128)S(1)}, u32[]{:S(2)}, u32[]{:S(2)}) collective-permute-start(f32[128,1024]{1,0:T(8,128)S(1)} %collective-permute-done.4.refs_5_), channel_id=1, source_target_pairs={{0,32},{32,64},{64,96},{96,128},{128,160},{160,192},{192,224},{224... | collective-permute-start | bytes 1572872 | tf_op jit(solution)/shard_map/ppermute | solution.py:191
  78.9 5.9 %copy-start.18 = (f32[128,1024]{1,0:T(8,128)}, f32[128,1024]{1,0:T(8,128)S(1)}, u32[]{:S(2)}) copy-start(f32[128,1024]{1,0:T(8,128)S(1)} %collective-permute-done.11.refs_6_) | copy-start | bytes 1572868
  78.9 14.9 %collective-permute-start.12 = (f32[128,1024]{1,0:T(8,128)S(1)}, f32[128,1024]{1,0:T(8,128)}, u32[]{:S(2)}, u32[]{:S(2)}) collective-permute-start(f32[128,1024]{1,0:T(8,128)S(1)} %collective-permute-done.11.refs_6_), channel_id=1, source_target_pairs={{0,480},{32,0},{64,32},{96,64},{128,96},{160,128},{192,160},{224,1... | collective-permute-start | bytes 1572872 | tf_op jit(solution)/shard_map/ppermute | solution.py:191
  83.5 1.3 copy-start.1
  84.8 27.6 %copy-start.8 = (f32[1024,32]{0,1:T(8,128)S(1)}, f32[1024,32]{0,1:T(8,128)}, u32[]{:S(2)}) copy-start(f32[1024,32]{0,1:T(8,128)} %param.14) | copy-start | bytes 393220
  84.9 13.5 %all-to-all-start.3 = ((f32[16,32,256]{2,1,0:T(8,128)}), f32[16,32,256]{2,1,0:T(8,128)S(1)}, u32[]{:S(2)}, u32[]{:S(2)}) async-start(f32[16,32,256]{2,1,0:T(8,128)} %couple.1), calls=%async_computation.3 | async-start | bytes 1048576 | tf_op jit(solution)/shard_map/all_to_all | solution.py:181
  91.9 21.8 %copy-start.19 = (f32[128,1024]{1,0:T(8,128)}, f32[128,1024]{1,0:T(8,128)S(1)}, u32[]{:S(2)}) copy-start(f32[128,1024]{1,0:T(8,128)S(1)} %collective-permute-done.6.refs_7_) | copy-start | bytes 1572868
  91.9 14.0 %collective-permute-start.7 = (f32[128,1024]{1,0:T(8,128)S(1)}, f32[128,1024]{1,0:T(8,128)S(1)}, u32[]{:S(2)}, u32[]{:S(2)}) collective-permute-start(f32[128,1024]{1,0:T(8,128)S(1)} %collective-permute-done.6.refs_7_), channel_id=1, source_target_pairs={{0,32},{32,64},{64,96},{96,128},{128,160},{160,192},{192,224},{224... | collective-permute-start | bytes 1572872 | tf_op jit(solution)/shard_map/ppermute | solution.py:191
  93.8 14.0 %collective-permute-start.13 = (f32[128,1024]{1,0:T(8,128)}, f32[128,1024]{1,0:T(8,128)S(1)}, u32[]{:S(2)}, u32[]{:S(2)}) collective-permute-start(f32[128,1024]{1,0:T(8,128)} %collective-permute-done.12.refs_8_), channel_id=1, source_target_pairs={{0,480},{32,0},{64,32},{96,64},{128,96},{160,128},{192,160},{224,1... | collective-permute-start | bytes 1572872 | tf_op jit(solution)/shard_map/ppermute | solution.py:191
  98.4 14.0 %collective-permute-start.5 = (f32[16,32,256]{2,1,0:T(8,128)S(1)}, f32[16,32,256]{2,1,0:T(8,128)S(1)}, u32[]{:S(2)}, u32[]{:S(2)}) collective-permute-start(f32[16,32,256]{2,1,0:T(8,128)S(1)} %all-to-all-done.3.refs_2_), channel_id=1, source_target_pairs={{0,1},{1,0},{2,3},{3,2},{4,5},{5,4},{6,7},{7,6},{8,9},{9,8},{10,11... | collective-permute-start | bytes 1572872 | tf_op jit(solution)/shard_map/ppermute | solution.py:186
  105.9 7.8 %copy-start.4 = (f32[128,1024]{1,0:T(8,128)}, f32[128,1024]{1,0:T(8,128)S(1)}, u32[]{:S(2)}) copy-start(f32[128,1024]{1,0:T(8,128)S(1)} %collective-permute-done.7.refs_4_.refs_9_) | copy-start | bytes 1572868
  105.9 13.2 %collective-permute-start.14 = (f32[128,1024]{1,0:T(8,128)S(1)}, f32[128,1024]{1,0:T(8,128)}, u32[]{:S(2)}, u32[]{:S(2)}) collective-permute-start(f32[128,1024]{1,0:T(8,128)S(1)} %collective-permute-done.7.refs_4_.refs_9_), channel_id=1, source_target_pairs={{0,32},{32,64},{64,96},{96,128},{128,160},{160,192},{192,224},{224... | collective-permute-start | bytes 1572872 | tf_op jit(solution)/shard_map/ppermute | solution.py:191
  107.8 5.9 %copy-start.20 = (f32[128,1024]{1,0:T(8,128)}, f32[128,1024]{1,0:T(8,128)S(1)}, u32[]{:S(2)}) copy-start(f32[128,1024]{1,0:T(8,128)S(1)} %collective-permute-done.13.refs_10_) | copy-start | bytes 1572868
  107.8 13.1 %collective-permute-start.15 = (f32[128,1024]{1,0:T(8,128)S(1)}, f32[128,1024]{1,0:T(8,128)}, u32[]{:S(2)}, u32[]{:S(2)}) collective-permute-start(f32[128,1024]{1,0:T(8,128)S(1)} %collective-permute-done.13.refs_10_), channel_id=1, source_target_pairs={{0,480},{32,0},{64,32},{96,64},{128,96},{160,128},{192,160},{224,1... | collective-permute-start | bytes 1572872 | tf_op jit(solution)/shard_map/ppermute | solution.py:191
  113.7 12.6 %all-to-all-start.4 = ((f32[16,32,256]{2,1,0:T(8,128)}), f32[16,32,256]{2,1,0:T(8,128)S(1)}, u32[]{:S(2)}, u32[]{:S(2)}) async-start(f32[16,32,256]{2,1,0:T(8,128)} %get-tuple-element.10), calls=%async_computation.4 | async-start | bytes 1048576 | tf_op jit(solution)/shard_map/all_to_all | solution.py:181
  119.0 14.4 %collective-permute-start.16 = (f32[128,1024]{1,0:T(8,128)}, f32[128,1024]{1,0:T(8,128)S(1)}, u32[]{:S(2)}, u32[]{:S(2)}) collective-permute-start(f32[128,1024]{1,0:T(8,128)} %collective-permute-done.14.refs_11_), channel_id=1, source_target_pairs={{0,32},{32,64},{64,96},{96,128},{128,160},{160,192},{192,224},{224... | collective-permute-start | bytes 1572872 | tf_op jit(solution)/shard_map/ppermute | solution.py:191
  121.0 14.4 %collective-permute-start.17 = (f32[128,1024]{1,0:T(8,128)}, f32[128,1024]{1,0:T(8,128)S(1)}, u32[]{:S(2)}, u32[]{:S(2)}) collective-permute-start(f32[128,1024]{1,0:T(8,128)} %collective-permute-done.15.refs_12_), channel_id=1, source_target_pairs={{0,480},{32,0},{64,32},{96,64},{128,96},{160,128},{192,160},{224,1... | collective-permute-start | bytes 1572872 | tf_op jit(solution)/shard_map/ppermute | solution.py:191
  126.3 9.1 %copy-start.13 = (f32[16,32,256]{2,1,0:T(8,128)}, f32[16,32,256]{2,1,0:T(8,128)S(1)}, u32[]{:S(2)}) copy-start(f32[16,32,256]{2,1,0:T(8,128)S(1)} %all-to-all-done.4.a_same.refs_2_) | copy-start | bytes 1572868
  126.3 13.7 %collective-permute-start.8 = (f32[16,32,256]{2,1,0:T(8,128)S(1)}, f32[16,32,256]{2,1,0:T(8,128)S(1)}, u32[]{:S(2)}, u32[]{:S(2)}) collective-permute-start(f32[16,32,256]{2,1,0:T(8,128)S(1)} %all-to-all-done.4.a_same.refs_2_), channel_id=1, source_target_pairs={{0,1},{1,0},{2,3},{3,2},{4,5},{5,4},{6,7},{7,6},{8,9},{9,8},{10,11... | collective-permute-start | bytes 1572872 | tf_op jit(solution)/shard_map/ppermute | solution.py:186
  133.4 2.0 %copy-start.15 = (f32[128,1024]{1,0:T(8,128)}, f32[128,1024]{1,0:T(8,128)S(1)}, u32[]{:S(2)}) copy-start(f32[128,1024]{1,0:T(8,128)S(1)} %collective-permute-done.16.refs_13_) | copy-start | bytes 1572868
  133.4 15.5 %collective-permute-start.18 = (f32[64,1024]{1,0:T(8,128)S(1)}, f32[64,1024]{1,0:T(8,128)S(1)}, u32[]{:S(2)}, u32[]{:S(2)}) collective-permute-start(f32[64,1024]{1,0:T(8,128)S(1)} %slice.8), channel_id=1, source_target_pairs={{0,32},{32,64},{64,96},{96,128},{128,160},{160,192},{192,224},{224... | collective-permute-start | bytes 786440 | tf_op jit(solution)/shard_map/ppermute | solution.py:191
  135.4 4.7 %copy-start.16 = (f32[128,1024]{1,0:T(8,128)}, f32[128,1024]{1,0:T(8,128)S(1)}, u32[]{:S(2)}) copy-start(f32[128,1024]{1,0:T(8,128)S(1)} %collective-permute-done.17.refs_14_) | copy-start | bytes 1572868
  135.4 13.5 %collective-permute-start.19 = (f32[64,1024]{1,0:T(8,128)S(1)}, f32[64,1024]{1,0:T(8,128)S(1)}, u32[]{:S(2)}, u32[]{:S(2)}) collective-permute-start(f32[64,1024]{1,0:T(8,128)S(1)} %slice.9), channel_id=1, source_target_pairs={{0,480},{32,0},{64,32},{96,64},{128,96},{160,128},{192,160},{224,1... | collective-permute-start | bytes 786440 | tf_op jit(solution)/shard_map/ppermute | solution.py:191
  140.0 0.8 copy-start.14
  148.9 0.7 copy-start.21
  149.6 0.7 copy-start.22
